TPU v7x, 32 devices: a whole 2x2x4 slice. The times are simulated.
32 devices in a mesh: fib: 2 (over y), len: 4 (over x, core), emg: 4 (over z).
Axes of the slice: x: 2, y: 2, z: 4, core: 2. Of those that a mesh axis runs over, the one named last changes fastest.
Arguments:
- states: float32 [57, 256, 1024], P(None, 'len', ('fib', 'emg')), may hold values from -6 to 6
- voltage: float32 [256, 1024], P('len', ('fib', 'emg')), may hold values from -6 to 6
- coupling: float32 [57, 57], replicated, may hold values from -0.75 to 0.75
- decay_rates: float32 [57], replicated, may hold values from 0.05 to 1.9
- volt_gain: float32 [57], replicated, may hold values from -4 to 4
- current_weights: float32 [57], replicated, may hold values from -0.75 to 0.75
- fibre_home: int32 [1024, 1], P(('fib', 'emg')), may hold values from 0 to 7; in each aligned block of 128 rows (0 to 127, 128 to 255, ...) at most 48 rows name the same one
- cross_cell: int32 [1024], P(('fib', 'emg')), may hold values from 0 to 1023
- motor_unit: int32 [1024], P(('fib', 'emg')), may hold values from 0 to 99
- stim_step: int32 [100], replicated, may hold values from 0 to 2
- tissue: float32 [128, 16, 512], P('len', 'fib', 'emg'), may hold values from 0.5 to 2
Outputs:
- states_out: float32 [57, 256, 1024], P(None, 'len', ('fib', 'emg'))
- voltage_out: float32 [256, 1024], P('len', ('fib', 'emg'))
- potential: float32 [2, 128, 16, 512], P(None, 'len', 'fib', 'emg')
Inputs may be any that keep to these rules, and one draw needn't show every extreme that they name: `fibre_home`: the fibres of one fib and emg index name any one brick column at most 48 times, and some brick column is named exactly 48 times by the fibres of some index. `stim_step`: A value of 2 means the motor unit does not fire in this window.
All inputs are finite; a program needn't handle non-finite values.
Results may differ from a plain program's by a relative error of at most 0.0003.
Values sent between devices are 32-bit elements; how exact they have to be, the bound alone decides.
No kernel may reach another device: no remote copies, remote signals or barrier semaphores. Data moves between devices by JAX's collectives and lax.ppermute only.
A program may use at most 64 MiB of HBM per device.

v0:
```python
import functools

import jax
import jax.numpy as jnp
import numpy as np
from jax import lax
from jax.experimental import pallas as pl
from jax.experimental.pallas import tpu as pltpu
from jax.sharding import PartitionSpec as P

STEPS = 2
SWEEPS = 4
NPC = 2

time_step = 0.5
conductance = 2000.0
amplitude = 200.0
band_half = 4
low_bound = 0.5
high_bound = 14.0
middle = 0.5 * (high_bound + low_bound)

SUB = 8
LANES = 128
EDGE = SUB // NPC
REACH = SWEEPS - 1
HIGHEST = lax.Precision.HIGHEST
VMEM = pl.BlockSpec(memory_space=pltpu.VMEM)


def kernel_call(body, outs, *args, limit=16 << 20, scratch=(), hbm_outs=()):
    shapes = [jax.ShapeDtypeStruct(shape, dtype) for shape, dtype in outs]
    specs = [
        pl.BlockSpec(memory_space=pl.ANY) if i in hbm_outs else VMEM for i in range(len(outs))
    ]
    return pl.pallas_call(
        body,
        out_shape=shapes,
        in_specs=[VMEM] * len(args),
        out_specs=specs,
        scratch_shapes=list(scratch),
        compiler_params=pltpu.CompilerParams(vmem_limit_bytes=limit),
    )(*args)


def iota(shape, dim):
    return lax.broadcasted_iota(jnp.int32, shape, dim)


def dot_nt(a, b, precision=None):
    return lax.dot_general(
        a, b, (((1,), (1,)), ((), ())), preferred_element_type=jnp.float32, precision=precision
    )


def split(x):
    high = x.astype(jnp.bfloat16)
    return high, (x - high.astype(jnp.float32)).astype(jnp.bfloat16)


def polynomial():
    spread = 0.5 * (high_bound - low_bound)
    ratio = middle / spread
    weight = 1.0 / ratio
    mul, add, sub = (
        np.polynomial.polynomial.polymul,
        np.polynomial.polynomial.polyadd,
        np.polynomial.polynomial.polysub,
    )
    total, rest, step = np.zeros(1), np.ones(1), np.ones(1) / middle
    for sweep in range(SWEEPS):
        total = add(total, step)
        if sweep + 1 < SWEEPS:
            rest = sub(rest, mul(np.array([middle, 1.0]), step))
            later = 1.0 / (2.0 * ratio - weight)
            step = add(later * weight * step, 2.0 * later / spread * rest)
            weight = later
    return [float(c) for c in total]


def cable_tables(nodes, shards):
    matrix = np.zeros((nodes, nodes))
    index = np.arange(nodes)
    matrix[index, index] = 1.0 + 2.0 * conductance
    matrix[0, 0] = matrix[-1, -1] = 1.0 + conductance
    matrix[index[1:], index[:-1]] = matrix[index[:-1], index[1:]] = -conductance
    inverse = np.linalg.inv(matrix)
    fall = inverse[0]
    rise = inverse[:, -1] / inverse[0, -1]
    local = nodes // shards
    blocks = []
    for k in range(shards):
        mine = slice(k * local, (k + 1) * local)
        tail = np.zeros((SUB, local))
        tail[0], tail[1] = rise[mine], fall[mine]
        blocks.append(np.concatenate([inverse[mine, mine], tail]))
    wide = lambda v: np.repeat(np.pad(v, SUB)[:, None], LANES, axis=1).astype(np.float32)
    return np.concatenate(blocks).astype(np.float32), wide(rise), wide(fall)


def prepare(states, coupling, decay, gain, weight, unit, fire, home, cell, emg, rows, depth):
    count = states + states % 2
    size = count * SUB
    span = -(-size // 256) * 256
    mu = fire.shape[1]
    fibres = unit.shape[1]

    def body(coupling_ref, decay_ref, gain_ref, weight_ref, unit_ref, fire_ref, home_ref, cell_ref,
             big_ref, param_ref, misc_ref):
        expand = (iota((size, states), 0) // SUB == iota((size, states), 1))
        spread_f = expand.astype(jnp.float32)
        spread_b = expand.astype(jnp.bfloat16)
        same = iota((size, size), 0) % SUB == iota((size, size), 1) % SUB
        parts = []
        for part in split(coupling_ref[...]):
            tall = jnp.dot(spread_b, part, preferred_element_type=jnp.float32)
            full = dot_nt(tall.astype(jnp.bfloat16), spread_b)
            parts.append(jnp.where(same, full, 0.0).astype(jnp.bfloat16))
        big_ref[...] = jnp.zeros_like(big_ref)
        big_ref[:, 0:size] = parts[0]
        big_ref[:, span:span + size] = parts[1]
        big_ref[:, 2 * span:2 * span + size] = parts[0]
        for i, row in enumerate((1.0 - time_step * decay_ref[...], gain_ref[...], weight_ref[...])):
            wide = jnp.broadcast_to(row, (LANES, states))
            param_ref[i] = dot_nt(spread_f, wide, HIGHEST)[:states * SUB].reshape(states, SUB, LANES)
        match = (iota((mu, fibres), 0) == unit_ref[...]).astype(jnp.float32)
        fires = jnp.broadcast_to(fire_ref[...].astype(jnp.float32), (SUB, mu))
        fires = jnp.dot(fires, match, preferred_element_type=jnp.float32, precision=HIGHEST)
        brick, spot = home_ref[...], cell_ref[...]
        row = (brick // emg) * rows + spot // depth
        column = (brick % emg) * depth + spot % depth
        line = iota((SUB, fibres), 0)
        out = jnp.where(line == 0, row.astype(jnp.float32), column.astype(jnp.float32))
        misc_ref[...] = jnp.where(line == 2, fires, out)

    return kernel_call(
        body,
        [((size, 3 * span), jnp.bfloat16), ((3, states, SUB, LANES), jnp.float32),
         ((SUB, fibres), jnp.float32)],
        coupling, decay, gain, weight, unit, fire, home, cell,
    )


def coupled(big, first, second):
    states = first.shape[0]
    pad = big.shape[0] - states * SUB
    span = big.shape[1] // 3
    both = jnp.concatenate(
        [first.reshape(states * SUB, LANES), second.reshape(states * SUB, LANES)], axis=1
    )
    if pad:
        both = jnp.concatenate([both, jnp.zeros((pad, 2 * LANES), jnp.float32)], axis=0)
    high, low = split(both)
    blank = [jnp.zeros((span - both.shape[0], 2 * LANES), jnp.bfloat16)]
    if span == both.shape[0]:
        blank = []
    stacked = jnp.concatenate([high, *blank, high, *blank, low, *blank], axis=0)
    out = jnp.dot(big, stacked, preferred_element_type=jnp.float32)[:states * SUB]
    return (out[:, :LANES].reshape(states, SUB, LANES), out[:, LANES:].reshape(states, SUB, LANES))


def advanced(values, drive, param_ref, voltage):
    drive = drive + param_ref[1] * voltage[None]
    values = param_ref[0] * values + time_step * jnp.tanh(drive)
    return values, jnp.sum(param_ref[2] * values, axis=0)


def cable(voltage, current, fires, step, table_ref, shard, shards):
    nodes = voltage.shape[0]
    place = shard * nodes + iota((nodes, 1), 0)
    centre = nodes * shards // 2
    band = ((place >= centre - band_half) & (place < centre + band_half)).astype(jnp.float32)
    active = (fires == float(step)).astype(jnp.float32)
    right = voltage + time_step * (amplitude * band * active - current)
    size = nodes + SUB
    table = table_ref[pl.ds(pl.multiple_of(shard * size, SUB), size), :]
    return jnp.dot(table, right, preferred_element_type=jnp.float32, precision=HIGHEST)


def far_sums(rows, owners, target):
    below = sum(jnp.where(owner < target, row[0:1], 0.0) for row, owner in zip(rows, owners))
    above = sum(jnp.where(owner > target, row[1:2], 0.0) for row, owner in zip(rows, owners))
    return below, above


def from_far(rise_ref, fall_ref, start, count, below, above):
    here = pl.ds(pl.multiple_of(start, SUB), count)
    return rise_ref[here, :] * above + fall_ref[here, :] * below


def first_step(shards, states, voltage, big, param, misc, table, tissue):
    count, nodes, fibres = states.shape
    cells = tissue.shape[0]
    face = 2 * tissue.shape[0] * NPC // nodes * 0 + 2 * (tissue.shape[0] // (nodes // NPC))
    edge = count * SUB + face + 3 * SUB

    def body(states_ref, voltage_ref, big_ref, param_ref, misc_ref, table_ref, tissue_ref,
             states_out, solved_ref, current_ref, one_ref, two_ref, sums_ref):
        shard = lax.axis_index("len")
        big = big_ref[...]
        for start in range(0, nodes, 2 * SUB):
            one, two = pl.ds(start, SUB), pl.ds(start + SUB, SUB)
            first, second = states_ref[:, one, :], states_ref[:, two, :]
            for here, values, drive in zip((one, two), (first, second), coupled(big, first, second)):
                values, current = advanced(values, drive, param_ref, voltage_ref[here, :])
                states_out[:, here, :] = values
                current_ref[here, :] = current
        solved = cable(
            voltage_ref[...], current_ref[...], misc_ref[2:3, :], 0, table_ref, shard, shards
        )
        solved_ref[...] = solved[:nodes]
        sums_ref[...] = solved[nodes:]
        even = lax.rem(shard, 2) == 0
        for out, upper in ((one_ref, even), (two_ref, jnp.logical_not(even))):
            start = pl.multiple_of(jnp.where(upper, nodes - SUB, 0), SUB)
            begin = pl.multiple_of(jnp.where(upper, cells - face, 0), SUB)
            at = count * SUB
            out[0:at, :] = states_out[:, pl.ds(start, SUB), :].reshape(at, fibres)
            out[at:at + face, :] = tissue_ref[pl.ds(begin, face), :]
            at = at + face
            out[at:at + SUB, :] = solved_ref[pl.ds(start, SUB), :]
            out[at + SUB:at + 2 * SUB, :] = current_ref[pl.ds(start, SUB), :]
            out[at + 2 * SUB:at + 3 * SUB, :] = solved[nodes:]

    f32 = jnp.float32
    return kernel_call(
        body,
        [((count, nodes, fibres), f32), ((nodes, fibres), f32), ((nodes, fibres), f32),
         ((edge, fibres), f32), ((edge, fibres), f32), ((SUB, fibres), f32)],
        states, voltage, big, param, misc, table, tissue,
    )


def coupled_all(states, big):
    def body(states_ref, big_ref, out_ref):
        big = big_ref[...]
        for start in range(0, states.shape[1], 2 * SUB):
            one, two = pl.ds(start, SUB), pl.ds(start + SUB, SUB)
            drives = coupled(big, states_ref[:, one, :], states_ref[:, two, :])
            out_ref[:, one, :], out_ref[:, two, :] = drives

    return kernel_call(body, [(states.shape, jnp.float32)], states, big)[0]


def tissue_faces(tissue, got_one, got_two, at, rows):
    cells = tissue.shape[0] // rows
    long = cells + 2 * EDGE
    depth = tissue.shape[1]

    def body(tissue_ref, one_ref, two_ref, wide_ref, up_ref, down_ref, ends_ref):
        even = lax.rem(lax.axis_index("len"), 2) == 0
        wide_ref[...] = jnp.zeros_like(wide_ref)
        lane = iota((long, depth), 1)
        ends = jnp.zeros((long, depth), jnp.float32)
        for y in range(rows):
            one = one_ref[pl.ds(at + y, 2, stride=rows), :]
            two = two_ref[pl.ds(at + y, 2, stride=rows), :]
            base = y * long
            wide_ref[base + EDGE - 2:base + EDGE, :] = jnp.where(even, two, one)
            wide_ref[base + EDGE:base + EDGE + cells, :] = tissue_ref[pl.ds(y, cells, stride=rows), :]
            wide_ref[base + EDGE + cells:base + EDGE + cells + 2, :] = jnp.where(even, one, two)
            slab = wide_ref[base:base + long, :]
            spot = lane - 8 * y
            near = pltpu.roll(slab, 8 * y, 1)
            far = pltpu.roll(slab, (8 * y + 4) % depth, 1)
            ends = jnp.where((spot >= 0) & (spot < 2), near, ends)
            ends = jnp.where((spot >= 2) & (spot < 4), far, ends)
        ends_ref[...] = ends
        up_ref[...] = wide_ref[(rows - 2) * long:, :]
        down_ref[...] = wide_ref[0:2 * long, :]

    f32 = jnp.float32
    return kernel_call(
        body,
        [((rows * long, depth), f32), ((2 * long, depth), f32), ((2 * long, depth), f32),
         ((long, depth), f32)],
        tissue, got_one, got_two,
    )


def second_step(shards, groups, states, drive, solved, current, big, param, misc, table, rise, fall,
                got_one, got_two, sums, ends):
    count, nodes, fibres = states.shape
    at = got_one.shape[0] - 3 * SUB
    cells = (nodes + 2 * SUB) // NPC
    long = ends.shape[0]
    height = STEPS * cells + SUB + long
    parts = len(sums)

    def body(states_ref, drive_ref, solved_ref, current_ref, big_ref, param_ref, misc_ref, table_ref,
             rise_ref, fall_ref, one_ref, two_ref, ends_ref, *rest):
        sums_refs, rest = rest[:parts], rest[parts:]
        states_out, solved_out, sums_out, send_ref, volt_ref, line_ref, stage_ref, sems = rest
        shard = lax.axis_index("len")
        even = lax.rem(shard, 2) == 0
        rows = [ref[...] for ref in sums_refs]
        owners = [jnp.bitwise_xor(shard, k) for k in range(parts)]

        below, above = far_sums(rows, owners, shard)
        volt_ref[...] = solved_ref[...] + from_far(
            rise_ref, fall_ref, SUB + shard * nodes, nodes, below, above
        )
        copies = []
        for start in range(0, nodes, 2 * SUB):
            for part in (start, start + SUB):
                here = pl.ds(part, SUB)
                values, now = advanced(
                    states_ref[:, here, :], drive_ref[:, here, :], param_ref, volt_ref[here, :]
                )
                stage_ref[:, here, :] = values
                line_ref[SUB + part:2 * SUB + part, :] = now
            here = pl.ds(start, 2 * SUB)
            copies.append(
                pltpu.make_async_copy(
                    stage_ref.at[:, here, :], states_out.at[:, here, :], sems.at[len(copies)]
                )
            )
            copies[-1].start()

        solved_next = cable(
            volt_ref[...], line_ref[SUB:SUB + nodes, :], misc_ref[2:3, :], 1, table_ref, shard, shards
        )
        solved_out[...] = solved_next[:nodes]
        sums_out[...] = solved_next[nodes:]

        sides = []
        for mine, other in ((two_ref, one_ref), (one_ref, two_ref)):
            sides.append(jnp.where(even, mine[...], other[...]))
        edges = [side[:count * SUB].reshape(count, SUB, fibres) for side in sides]
        drives = coupled(big_ref[...], *edges)
        inside = (shard > 0, shard < shards - 1)
        for i, (side, edge, push) in enumerate(zip(sides, edges, drives)):
            neighbour = shard + (1 if i else -1)
            below, above = far_sums(rows, owners, neighbour)
            start = shard * nodes + (SUB + nodes if i else 0)
            value = side[at:at + SUB] + from_far(rise_ref, fall_ref, start, SUB, below, above)
            _, now = advanced(edge, push, param_ref, value)
            to = SUB + nodes if i else 0
            keep = inside[i].astype(jnp.float32)
            line_ref[to:to + SUB, :] = keep * now
            far = nodes + 2 * SUB + to
            line_ref[far:far + SUB, :] = keep * side[at + SUB:at + 2 * SUB]
        line_ref[nodes + 3 * SUB:2 * nodes + 3 * SUB, :] = current_ref[...]

        total = nodes + 2 * SUB
        for step in range(STEPS):
            begin = (STEPS - 1 - step) * total
            binned = line_ref[pl.ds(begin, cells, stride=NPC), :]
            for k in range(1, NPC):
                binned = binned + line_ref[pl.ds(begin + k, cells, stride=NPC), :]
            for g in range(groups):
                send_ref[g, step * cells:(step + 1) * cells, :] = binned
        low = STEPS * cells
        for g in range(groups):
            send_ref[g, low:low + SUB, :] = misc_ref[...]
            send_ref[g, low + SUB:, :] = ends_ref[...]
        for copy in copies:
            copy.wait()

    f32 = jnp.float32
    return kernel_call(
        body,
        [((count, nodes, fibres), f32), ((nodes, fibres), f32), ((SUB, fibres), f32),
         ((groups, height, fibres), f32)],
        states, drive, solved, current, big, param, misc, table, rise, fall, got_one, got_two, ends,
        *sums,
        hbm_outs=(0,),
        scratch=[
            pltpu.VMEM((nodes, fibres), f32),
            pltpu.VMEM((STEPS * (nodes + 2 * SUB), fibres), f32),
            pltpu.VMEM((count, nodes, fibres), f32),
            pltpu.SemaphoreType.DMA((nodes // (2 * SUB),)),
        ],
    )


def last_voltage(solved, rise, fall, sums):
    nodes, fibres = solved.shape

    def body(solved_ref, rise_ref, fall_ref, *rest):
        out_ref = rest[-1]
        shard = lax.axis_index("len")
        rows = [ref[...] for ref in rest[:-1]]
        owners = [jnp.bitwise_xor(shard, k) for k in range(len(rows))]
        below, above = far_sums(rows, owners, shard)
        out_ref[...] = solved_ref[...] + from_far(
            rise_ref, fall_ref, SUB + shard * nodes, nodes, below, above
        )

    return kernel_call(body, [((nodes, fibres), jnp.float32)], solved, rise, fall, *sums)[0]


def potentials(sizes, got, wide, lower, upper, rows):
    shards, fib, emg = sizes
    groups, height, fibres = got.shape
    long = wide.shape[0] // rows
    depth = wide.shape[1]
    cells = long - 2 * EDGE
    tall = STEPS * long
    slabs = rows + 2 * REACH
    lanes = 2 * depth
    low = STEPS * long
    coefs = polynomial()
    scale = [c / coefs[-1] for c in coefs]

    def body(got_ref, wide_ref, lower_ref, upper_ref, out_ref, mask_ref, hot_ref, left_ref, src_ref,
             diag_ref, one_ref, two_ref):
        shard, mine, place = (lax.axis_index(a) for a in ("len", "fib", "emg"))
        lane = iota((lanes, fibres), 0)
        lane = jnp.where(lane < lanes - depth // 2, lane, lane - lanes)
        for g in range(groups):
            column = got_ref[g, low + 1:low + 2, :].astype(jnp.int32) - place * depth
            hot_ref[:, g * fibres:(g + 1) * fibres] = (
                (lane == column) & (lane >= -REACH) & (lane < depth + REACH)
            ).astype(jnp.bfloat16)
            high, rest = split(got_ref[g, 0:low, :])
            both = jnp.concatenate([high, rest], axis=0)
            row = got_ref[g, low:low + 1, :].astype(jnp.int32) - mine * rows + REACH
            for y in range(slabs):
                pick = (row == y).astype(jnp.float32).astype(jnp.bfloat16)
                left_ref[y * 2 * tall:(y + 1) * 2 * tall, g * fibres:(g + 1) * fibres] = both * pick
        product = dot_nt(left_ref[...], hot_ref[...])
        for y in range(slabs):
            base = y * 2 * tall
            src_ref[y * tall:(y + 1) * tall, :] = (
                product[base:base + tall] + product[base + tall:base + 2 * tall]
            )
        spot = iota((long, depth), 1)
        for y in range(-2, rows + 2):
            if y < 0:
                main = lower_ref[(y + 2) * long:(y + 3) * long, :]
            elif y >= rows:
                main = upper_ref[(y - rows) * long:(y - rows + 1) * long, :]
            else:
                main = wide_ref[y * long:(y + 1) * long, :]
            f = mine + (-1 if y < 0 else 1 if y >= rows else 0)
            yy = y % rows
            f = jnp.clip(f, 0, fib - 1)
            after = f * emg + jnp.minimum(place + 1, emg - 1)
            before = f * emg + jnp.maximum(place - 1, 0)
            after = got_ref[after, low + SUB:, :]
            before = got_ref[before, low + SUB:, :]
            after = pltpu.roll(after, (depth - 8 * yy) % depth, 1)
            before = pltpu.roll(before, (depth - 4 - 8 * yy) % depth, 1)
            side = jnp.where(spot < 2, after, jnp.where(spot >= depth - 2, before, 0.0))
            whole = jnp.concatenate([main, side], axis=1) + (6.0 - middle)
            base = (y + 2) * tall
            for step in range(STEPS):
                diag_ref[base + step * long:base + (step + 1) * long, :] = whole
        x = lax.rem(iota((tall, lanes), 0), long) - EDGE + shard * cells
        z = iota((tall, lanes), 1)
        z = jnp.where(z < lanes - depth // 2, z, z - lanes) + place * depth
        mask_ref[...] = (
            (x >= 0) & (x < shards * cells) & (z >= 0) & (z < emg * depth)
        ).astype(jnp.float32)

        def sweep(ref, y, constant):
            here = lambda k: ref[(k + REACH) * tall:(k + REACH + 1) * tall, :]
            centre = here(y)
            beside = here(y - 1) + here(y + 1)
            beside = beside + pltpu.roll(centre, 1, 0) + pltpu.roll(centre, tall - 1, 0)
            beside = beside + pltpu.roll(centre, 1, 1) + pltpu.roll(centre, lanes - 1, 1)
            diag = diag_ref[(y + 2) * tall:(y + 3) * tall, :]
            source = src_ref[(y + REACH) * tall:(y + REACH + 1) * tall, :]
            return diag * centre - beside + constant * source

        for k, (source, target) in enumerate(((src_ref, one_ref), (one_ref, two_ref))):
            reach = REACH - 1 - k
            for y in range(-reach, rows + reach):
                value = sweep(source, y, scale[2 - k]) * mask_ref[...]
                if y < 0:
                    value = value * (mine > 0).astype(jnp.float32)
                if y >= rows:
                    value = value * (mine < fib - 1).astype(jnp.float32)
                target[(y + REACH) * tall:(y + REACH + 1) * tall, :] = value
        for y in range(rows):
            value = sweep(two_ref, y, scale[0])[:, :depth] * coefs[-1]
            for step in range(STEPS):
                begin = step * long + EDGE
                out_ref[pl.ds(step * cells * rows + y, cells, stride=rows), :] = value[
                    begin:begin + cells
                ]

    f32, b16 = jnp.float32, jnp.bfloat16
    wide_k = groups * fibres
    limit = (24 << 20) + slabs * 2 * tall * wide_k * 2 + 2 * groups * height * fibres * 4
    return kernel_call(
        body,
        [((STEPS * cells * rows, depth), f32)],
        got, wide, lower, upper,
        limit=limit,
        scratch=[
            pltpu.VMEM((tall, lanes), f32),
            pltpu.VMEM((lanes, wide_k), b16),
            pltpu.VMEM((slabs * 2 * tall, wide_k), b16),
            pltpu.VMEM((slabs * tall, lanes), f32),
            pltpu.VMEM(((rows + 4) * tall, lanes), f32),
            pltpu.VMEM((slabs * tall, lanes), f32),
            pltpu.VMEM((slabs * tall, lanes), f32),
        ],
    )[0]


def pairs(count, first):
    out = []
    for i in range(first, count - 1, 2):
        out += [(i, i + 1), (i + 1, i)]
    return out


def xor_swap(value, axis, k):
    return lax.ppermute(value, axis, [(i, i ^ k) for i in range(lax.axis_size(axis))])


def on_device(
    states,
    voltage,
    coupling,
    decay_rates,
    volt_gain,
    current_weights,
    fibre_home,
    cross_cell,
    motor_unit,
    stim_step,
    tissue,
):
    count, nodes, fibres = states.shape
    cells, rows, depth = tissue.shape
    shards, fib, emg = (lax.axis_size(a) for a in ("len", "fib", "emg"))
    groups = fib * emg
    line = lambda v: v.reshape(1, v.size)
    table, rise, fall = (jnp.asarray(t) for t in cable_tables(nodes * shards, shards))
    flat = tissue.reshape(cells * rows, depth)
    big, param, misc = prepare(
        count, coupling, line(decay_rates), line(volt_gain), line(current_weights),
        line(motor_unit), line(stim_step), line(fibre_home), line(cross_cell), emg, rows, depth,
    )
    states, solved, current, one, two, sums = first_step(
        shards, states, voltage, big, param, misc, table, flat
    )
    got_two = lax.ppermute(two, "len", pairs(shards, 1))
    got_one = lax.ppermute(one, "len", pairs(shards, 0))
    others = [xor_swap(sums, "len", k) for k in range(2, shards)]
    drive = coupled_all(states, big)
    at = got_one.shape[0] - 3 * SUB
    all_sums = [sums, got_one[at + 2 * SUB:], *others]
    wide, up, down, ends = tissue_faces(flat, got_one, got_two, at - 2 * rows, rows)
    states, solved, sums, send = second_step(
        shards, groups, states, drive, solved, current, big, param, misc, table, rise, fall,
        got_one, got_two, all_sums, ends,
    )
    got = lax.all_to_all(send, ("fib", "emg"), split_axis=0, concat_axis=0, tiled=True)
    if fib == 2:
        from_other = lax.ppermute(
            jnp.where(lax.axis_index("fib") == 0, up, down), "fib", [(0, 1), (1, 0)]
        )
        lower = upper = from_other
    else:
        lower = lax.ppermute(up, "fib", [(i, i + 1) for i in range(fib - 1)])
        upper = lax.ppermute(down, "fib", [(i + 1, i) for i in range(fib - 1)])
    others = [xor_swap(sums, "len", k) for k in range(1, shards)]
    voltage = last_voltage(solved, rise, fall, [sums, *others])
    potential = potentials((shards, fib, emg), got, wide, lower, upper, rows)
    return states, voltage, potential.reshape(STEPS, cells, rows, depth)


def solution(mesh):
    return jax.shard_map(
        on_device,
        mesh=mesh,
        in_specs=(
            P(None, "len", ("fib", "emg")),
            P("len", ("fib", "emg")),
            P(),
            P(),
            P(),
            P(),
            P(("fib", "emg"), None),
            P(("fib", "emg")),
            P(("fib", "emg")),
            P(),
            P("len", "fib", "emg"),
        ),
        out_specs=(
            P(None, "len", ("fib", "emg")),
            P("len", ("fib", "emg")),
            P(None, "len", "fib", "emg"),
        ),
        check_vma=False,
    )
```

profile of v0, /device:TPU:0, one launch (start us, length us, event | category | flops | bytes accessed | tf_op | source)
XLA Modules:
  0.0 51.8 jit_solution(13807263885843969093)
XLA Ops:
  0.6 0.0 copy-start.7
  0.6 0.7 %copy-done.7 = f32[57,57]{1,0:T(8,128)S(1)} copy-done((f32[57,57]{1,0:T(8,128)S(1)}, f32[57,57]{1,0:T(8,128)}, u32[]{:S(2)}) %copy-start.7) | copy-done | bytes 13020
  1.4 0.0 copy-start.8
  1.4 0.7 %copy-done.8 = f32[57]{0:T(128)S(1)} copy-done((f32[57]{0:T(128)S(1)}, f32[57]{0:T(128)}, u32[]{:S(2)}) %copy-start.8) | copy-done | bytes 252
  2.0 0.0 copy-start.9
  2.1 0.7 %copy-done.9 = f32[57]{0:T(128)S(1)} copy-done((f32[57]{0:T(128)S(1)}, f32[57]{0:T(128)}, u32[]{:S(2)}) %copy-start.9) | copy-done | bytes 252
  2.7 0.0 copy-start.10
  2.7 0.7 %copy-done.10 = f32[57]{0:T(128)S(1)} copy-done((f32[57]{0:T(128)S(1)}, f32[57]{0:T(128)}, u32[]{:S(2)}) %copy-start.10) | copy-done | bytes 252
  3.4 0.0 copy-start.11
  3.4 0.7 %copy-done.11 = s32[128]{0:T(128)S(1)} copy-done((s32[128]{0:T(128)S(1)}, s32[128]{0:T(128)}, u32[]{:S(2)}) %copy-start.11) | copy-done | bytes 536
  4.0 0.0 copy-start.12
  4.0 0.7 %copy-done.12 = s32[100]{0:T(128)S(1)} copy-done((s32[100]{0:T(128)S(1)}, s32[100]{0:T(128)}, u32[]{:S(2)}) %copy-start.12) | copy-done | bytes 424
  4.7 0.0 copy-start.13
  4.7 0.7 %copy-done.13 = s32[128,1]{0,1:T(1,128)S(1)} copy-done((s32[128,1]{0,1:T(1,128)S(1)}, s32[128,1]{0,1:T(1,128)}, u32[]{:S(2)}) %copy-start.13) | copy-done | bytes 536
  5.3 0.7 %copy-done.14 = s32[128]{0:T(128)S(1)} copy-done((s32[128]{0:T(128)S(1)}, s32[128]{0:T(128)}, u32[]{:S(2)}) %copy-start.14) | copy-done | bytes 536
  6.0 1.5 %shard_map.157 = (bf16[464,1536]{1,0:T(8,128)(2,1)S(1)}, f32[3,57,8,128]{3,2,1,0:T(8,128)S(1)}, f32[8,128]{1,0:T(8,128)S(1)}) custom-call(f32[57,57]{1,0:T(8,128)S(1)} %copy-done.7, f32[1,57]{1,0:T(1,128)S(1)} %bitcast.11, f32[1,57]{1,0:T(1,128)S(1)} %bitcast.12, f32[1,57]{1,0:T(1,128)S(1)} %bitcast.13, s32[1,128]{1,0:T(1,128)S(1)} %bitcast.14, ...), custom_call_target="tpu_custom_call" | custom-call | tf_op jit(solution)/shard_map/pallas_call | solution.py:36
  7.5 0.0 copy-start
  7.5 1.5 %copy-done = f32[57,64,128]{2,1,0:T(8,128)S(1)} copy-done((f32[57,64,128]{2,1,0:T(8,128)S(1)}, f32[57,64,128]{2,1,0:T(8,128)}, u32[]{:S(2)}) %copy-start) | copy-done | bytes 1867800
  9.0 0.9 %copy-done.1 = f32[288,64]{1,0:T(8,128)S(1)} copy-done((f32[288,64]{1,0:T(8,128)S(1)}, f32[288,64]{1,0:T(8,128)}, u32[]{:S(2)}) %copy-start.1) | copy-done | bytes 73752
  9.9 0.9 %copy-done.5 = f32[32,8,128]{2,1,0:T(8,128)S(1)} copy-done((f32[32,8,128]{2,1,0:T(8,128)S(1)}, f32[32,8,128]{2,1,0:T(8,128)}, u32[]{:S(2)}) %copy-start.5) | copy-done | bytes 131096
  10.8 0.8 %copy-done.6 = f32[64,128]{1,0:T(8,128)S(1)} copy-done((f32[64,128]{1,0:T(8,128)S(1)}, f32[64,128]{1,0:T(8,128)}, u32[]{:S(2)}) %copy-start.6) | copy-done | bytes 32792
  11.5 2.0 %shard_map.158 = (f32[57,64,128]{2,1,0:T(8,128)S(1)}, f32[64,128]{1,0:T(8,128)S(1)}, f32[64,128]{1,0:T(8,128)S(1)}, f32[496,128]{1,0:T(8,128)S(1)}, f32[496,128]{1,0:T(8,128)S(1)}, /*index=5*/f32[8,128]{1,0:T(8,128)S(1)}) custom-call(f32[57,64,128]{2,1,0:T(8,128)S(1)} %copy-done, f32[64,128]{1,0:T(8,128)S(1)} %copy-done.6, ...), custom_call_target="tpu_custom_call" | custom-call | tf_op jit(solution)/shard_map/pallas_call | solution.py:36
  13.6 0.5 %collective-permute-start = (f32[496,128]{1,0:T(8,128)S(1)}, f32[496,128]{1,0:T(8,128)S(1)}, u32[]{:S(2)}, u32[]{:S(2)}) collective-permute-start(f32[496,128]{1,0:T(8,128)S(1)} %get-tuple-element.26), channel_id=1, source_target_pairs={{0,4},{4,0},{8,12},{12,8},{1,5},{5,1},{9,13},{13,9},{2,6},{6,2},{1... | collective-permute-start | bytes 761864 | tf_op jit(solution)/shard_map/ppermute | solution.py:543
  14.1 0.7 %collective-permute-start.1 = (f32[496,128]{1,0:T(8,128)S(1)}, f32[496,128]{1,0:T(8,128)S(1)}, u32[]{:S(2)}, u32[]{:S(2)}) collective-permute-start(f32[496,128]{1,0:T(8,128)S(1)} %get-tuple-element.27), channel_id=1, source_target_pairs={{4,8},{8,4},{5,9},{9,5},{6,10},{10,6},{7,11},{11,7},{20,24},{24,20... | collective-permute-start | bytes 761864 | tf_op jit(solution)/shard_map/ppermute | solution.py:542
  14.8 2.7 %collective-permute-start.3 = (f32[8,128]{1,0:T(8,128)S(1)}, f32[8,128]{1,0:T(8,128)S(1)}, u32[]{:S(2)}, u32[]{:S(2)}) collective-permute-start(f32[8,128]{1,0:T(8,128)S(1)} %get-tuple-element.29.rest_0_), channel_id=1, source_target_pairs={{0,12},{4,8},{8,4},{12,0},{1,13},{5,9},{9,5},{13,1},{2,14},{6,10},... | collective-permute-start | bytes 12296 | tf_op jit(solution)/shard_map/ppermute | solution.py:512
  17.5 2.9 %collective-permute-start.2 = (f32[8,128]{1,0:T(8,128)S(1)}, f32[8,128]{1,0:T(8,128)S(1)}, u32[]{:S(2)}, u32[]{:S(2)}) collective-permute-start(f32[8,128]{1,0:T(8,128)S(1)} %get-tuple-element.29.rest_0_), channel_id=1, source_target_pairs={{0,8},{4,12},{8,0},{12,4},{1,9},{5,13},{9,1},{13,5},{2,10},{6,14},... | collective-permute-start | bytes 12296 | tf_op jit(solution)/shard_map/ppermute | solution.py:512
  20.4 1.7 %shard_map.159.drive_ref = f32[57,64,128]{2,1,0:T(8,128)S(1)} custom-call(f32[57,64,128]{2,1,0:T(8,128)S(1)} %get-tuple-element.23.states_ref, bf16[464,1536]{1,0:T(8,128)(2,1)S(1)} %get-tuple-element.20.big_ref), custom_call_target="tpu_custom_call" | custom-call | tf_op jit(solution)/shard_map/pallas_call | solution.py:36
  22.0 0.0 collective-permute-done.one_ref
  22.0 0.0 collective-permute-done.1.two_ref
  22.0 0.2 shard_map.160
  22.2 0.0 collective-permute-done.3.rest_3_
  22.2 0.7 %collective-permute-done.2.rest_2_ = f32[8,128]{1,0:T(8,128)S(1)} collective-permute-done((f32[8,128]{1,0:T(8,128)S(1)}, f32[8,128]{1,0:T(8,128)S(1)}, u32[]{:S(2)}, u32[]{:S(2)}) %collective-permute-start.2) | collective-permute-done | bytes 4128 | tf_op jit(solution)/shard_map/ppermute | solution.py:512
  22.9 0.0 copy-done.2
  22.9 0.0 copy-done.3
  22.9 0.0 copy-done.4
  22.9 3.5 %shard_map.161 = (f32[57,64,128]{2,1,0:T(8,128)}, f32[64,128]{1,0:T(8,128)S(1)}, f32[8,128]{1,0:T(8,128)S(1)}, f32[8,128,128]{2,1,0:T(8,128)}) custom-call(f32[57,64,128]{2,1,0:T(8,128)S(1)} %get-tuple-element.23.states_ref, f32[57,64,128]{2,1,0:T(8,128)S(1)} %shard_map.159.drive_ref, f32[64,128]{1,0:T(8,128)S(1)} %get-tuple-element.24.solved_ref, ...), custom_call_target="tpu_custom_call" | custom-call | tf_op jit(solution)/shard_map/pallas_call | solution.py:36
  26.4 6.5 %all-to-all-start = ((f32[8,128,128]{2,1,0:T(8,128)}), f32[8,128,128]{2,1,0:T(8,128)S(1)}, u32[]{:S(2)}, u32[]{:S(2)}) async-start(f32[8,128,128]{2,1,0:T(8,128)} %get-tuple-element.33), calls=%async_computation | async-start | bytes 1048576 | tf_op jit(solution)/shard_map/all_to_all | solution.py:553
  32.9 2.1 %collective-permute-start.7 = (f32[80,128]{1,0:T(8,128)S(1)}, f32[80,128]{1,0:T(8,128)S(1)}, u32[]{:S(2)}, u32[]{:S(2)}) collective-permute-start(f32[80,128]{1,0:T(8,128)S(1)} %broadcast_select_fusion), channel_id=1, source_target_pairs={{0,16},{16,0},{1,17},{17,1},{2,18},{18,2},{3,19},{19,3},{4,20},{20... | collective-permute-start | bytes 122888 | tf_op jit(solution)/shard_map/ppermute | solution.py:555
  35.0 0.0 collective-permute-start.6
  35.0 1.0 %collective-permute-start.5 = (f32[8,128]{1,0:T(8,128)S(1)}, f32[8,128]{1,0:T(8,128)S(1)}, u32[]{:S(2)}, u32[]{:S(2)}) collective-permute-start(f32[8,128]{1,0:T(8,128)S(1)} %get-tuple-element.32.rest_0_), channel_id=1, source_target_pairs={{0,8},{4,12},{8,0},{12,4},{1,9},{5,13},{9,1},{13,5},{2,10},{6,14},... | collective-permute-start | bytes 12296 | tf_op jit(solution)/shard_map/ppermute | solution.py:512
  36.0 0.9 %collective-permute-start.4 = (f32[8,128]{1,0:T(8,128)S(1)}, f32[8,128]{1,0:T(8,128)S(1)}, u32[]{:S(2)}, u32[]{:S(2)}) collective-permute-start(f32[8,128]{1,0:T(8,128)S(1)} %get-tuple-element.32.rest_0_), channel_id=1, source_target_pairs={{0,4},{4,0},{8,12},{12,8},{1,5},{5,1},{9,13},{13,9},{2,6},{6,2},{1... | collective-permute-start | bytes 12296 | tf_op jit(solution)/shard_map/ppermute | solution.py:512
  36.8 1.2 %collective-permute-done.6.rest_3_ = f32[8,128]{1,0:T(8,128)S(1)} collective-permute-done((f32[8,128]{1,0:T(8,128)S(1)}, f32[8,128]{1,0:T(8,128)S(1)}, u32[]{:S(2)}, u32[]{:S(2)}) %collective-permute-start.6) | collective-permute-done | bytes 4128 | tf_op jit(solution)/shard_map/ppermute | solution.py:512
  38.0 0.6 %collective-permute-done.5.rest_2_ = f32[8,128]{1,0:T(8,128)S(1)} collective-permute-done((f32[8,128]{1,0:T(8,128)S(1)}, f32[8,128]{1,0:T(8,128)S(1)}, u32[]{:S(2)}, u32[]{:S(2)}) %collective-permute-start.5) | collective-permute-done | bytes 4128 | tf_op jit(solution)/shard_map/ppermute | solution.py:512
  38.6 0.0 collective-permute-done.4.rest_1_
  38.6 0.6 %shard_map.162 = f32[64,128]{1,0:T(8,128)} custom-call(f32[64,128]{1,0:T(8,128)S(1)} %get-tuple-element.31.solved_ref, f32[272,128]{1,0:T(8,128)S(1)} %copy-done.4, f32[272,128]{1,0:T(8,128)S(1)} %copy-done.3, f32[8,128]{1,0:T(8,128)S(1)} %get-tuple-element.32.rest_0_, f32[8,128]{1,0:T(8,128)S(1)} %collective-permute-done.4.rest_1_, ...), custom_call_target="tpu_custom_call" | custom-call | tf_op jit(solution)/shard_map/pallas_call | solution.py:36
  39.2 0.0 collective-permute-done.7.lower_ref.upper_ref
  39.2 9.1 %all-to-all-done.got_ref = f32[8,128,128]{2,1,0:T(8,128)S(1)} async-done(((f32[8,128,128]{2,1,0:T(8,128)}), f32[8,128,128]{2,1,0:T(8,128)S(1)}, u32[]{:S(2)}, u32[]{:S(2)}) %all-to-all-start) | async-done | bytes 524320 | tf_op jit(solution)/shard_map/all_to_all | solution.py:553
  48.4 3.5 %shard_map.163 = f32[512,128]{1,0:T(8,128)} custom-call(f32[8,128,128]{2,1,0:T(8,128)S(1)} %all-to-all-done.got_ref, f32[320,128]{1,0:T(8,128)S(1)} %get-tuple-element.34.wide_ref, f32[80,128]{1,0:T(8,128)S(1)} %collective-permute-done.7.lower_ref.upper_ref, f32[80,128]{1,0:T(8,128)S(1)} %collective-permute-done.7.lower_ref.upper_ref), custom_call_target="tpu_custom_call" | custom-call | tf_op jit(solution)/shard_map/pallas_call | solution.py:36
  (9 shorter events, 0.0 us)
Async XLA Ops:
  0.6 0.8 %copy-start.7 = (f32[57,57]{1,0:T(8,128)S(1)}, f32[57,57]{1,0:T(8,128)}, u32[]{:S(2)}) copy-start(f32[57,57]{1,0:T(8,128)} %coupling_ref.1) | copy-start | bytes 38992
  1.4 0.7 %copy-start.8 = (f32[57]{0:T(128)S(1)}, f32[57]{0:T(128)}, u32[]{:S(2)}) copy-start(f32[57]{0:T(128)} %param.17) | copy-start | bytes 688
  2.0 0.7 %copy-start.9 = (f32[57]{0:T(128)S(1)}, f32[57]{0:T(128)}, u32[]{:S(2)}) copy-start(f32[57]{0:T(128)} %param.18) | copy-start | bytes 688
  2.7 0.7 %copy-start.10 = (f32[57]{0:T(128)S(1)}, f32[57]{0:T(128)}, u32[]{:S(2)}) copy-start(f32[57]{0:T(128)} %param.19) | copy-start | bytes 688
  3.4 0.7 %copy-start.11 = (s32[128]{0:T(128)S(1)}, s32[128]{0:T(128)}, u32[]{:S(2)}) copy-start(s32[128]{0:T(128)} %param.22) | copy-start | bytes 1540
  4.0 0.7 %copy-start.12 = (s32[100]{0:T(128)S(1)}, s32[100]{0:T(128)}, u32[]{:S(2)}) copy-start(s32[100]{0:T(128)} %param.23) | copy-start | bytes 1204
  4.7 0.7 %copy-start.13 = (s32[128,1]{0,1:T(1,128)S(1)}, s32[128,1]{0,1:T(1,128)}, u32[]{:S(2)}) copy-start(s32[128,1]{0,1:T(1,128)} %param.20) | copy-start | bytes 1540
  5.3 0.7 %copy-start.14 = (s32[128]{0:T(128)S(1)}, s32[128]{0:T(128)}, u32[]{:S(2)}) copy-start(s32[128]{0:T(128)} %param.21) | copy-start | bytes 1540
  7.5 1.5 %copy-start = (f32[57,64,128]{2,1,0:T(8,128)S(1)}, f32[57,64,128]{2,1,0:T(8,128)}, u32[]{:S(2)}) copy-start(f32[57,64,128]{2,1,0:T(8,128)} %states_ref.1) | copy-start | bytes 5603332
  9.0 0.9 %copy-start.1 = (f32[288,64]{1,0:T(8,128)S(1)}, f32[288,64]{1,0:T(8,128)}, u32[]{:S(2)}) copy-start(f32[288,64]{1,0:T(8,128)} %constant.14.clone.table_ref) | copy-start | bytes 221188
  9.9 0.9 %copy-start.5 = (f32[32,8,128]{2,1,0:T(8,128)S(1)}, f32[32,8,128]{2,1,0:T(8,128)}, u32[]{:S(2)}) copy-start(f32[32,8,128]{2,1,0:T(8,128)} %param.24) | copy-start | bytes 393220
  10.8 0.8 %copy-start.6 = (f32[64,128]{1,0:T(8,128)S(1)}, f32[64,128]{1,0:T(8,128)}, u32[]{:S(2)}) copy-start(f32[64,128]{1,0:T(8,128)} %voltage_ref.1) | copy-start | bytes 98308
  13.6 8.4 %collective-permute-start = (f32[496,128]{1,0:T(8,128)S(1)}, f32[496,128]{1,0:T(8,128)S(1)}, u32[]{:S(2)}, u32[]{:S(2)}) collective-permute-start(f32[496,128]{1,0:T(8,128)S(1)} %get-tuple-element.26), channel_id=1, source_target_pairs={{0,4},{4,0},{8,12},{12,8},{1,5},{5,1},{9,13},{13,9},{2,6},{6,2},{1... | collective-permute-start | bytes 761864 | tf_op jit(solution)/shard_map/ppermute | solution.py:543
  14.1 7.9 %collective-permute-start.1 = (f32[496,128]{1,0:T(8,128)S(1)}, f32[496,128]{1,0:T(8,128)S(1)}, u32[]{:S(2)}, u32[]{:S(2)}) collective-permute-start(f32[496,128]{1,0:T(8,128)S(1)} %get-tuple-element.27), channel_id=1, source_target_pairs={{4,8},{8,4},{5,9},{9,5},{6,10},{10,6},{7,11},{11,7},{20,24},{24,20... | collective-permute-start | bytes 761864 | tf_op jit(solution)/shard_map/ppermute | solution.py:542
  14.8 7.4 %collective-permute-start.3 = (f32[8,128]{1,0:T(8,128)S(1)}, f32[8,128]{1,0:T(8,128)S(1)}, u32[]{:S(2)}, u32[]{:S(2)}) collective-permute-start(f32[8,128]{1,0:T(8,128)S(1)} %get-tuple-element.29.rest_0_), channel_id=1, source_target_pairs={{0,12},{4,8},{8,4},{12,0},{1,13},{5,9},{9,5},{13,1},{2,14},{6,10},... | collective-permute-start | bytes 12296 | tf_op jit(solution)/shard_map/ppermute | solution.py:512
  17.5 5.5 %collective-permute-start.2 = (f32[8,128]{1,0:T(8,128)S(1)}, f32[8,128]{1,0:T(8,128)S(1)}, u32[]{:S(2)}, u32[]{:S(2)}) collective-permute-start(f32[8,128]{1,0:T(8,128)S(1)} %get-tuple-element.29.rest_0_), channel_id=1, source_target_pairs={{0,8},{4,12},{8,0},{12,4},{1,9},{5,13},{9,1},{13,5},{2,10},{6,14},... | collective-permute-start | bytes 12296 | tf_op jit(solution)/shard_map/ppermute | solution.py:512
  20.4 2.6 %copy-start.2 = (f32[288,64]{1,0:T(8,128)S(1)}, f32[288,64]{1,0:T(8,128)}, u32[]{:S(2)}) copy-start(f32[288,64]{1,0:T(8,128)} %constant.14.clone.table_ref) | copy-start | bytes 221188
  20.4 2.6 %copy-start.3 = (f32[272,128]{1,0:T(8,128)S(1)}, f32[272,128]{1,0:T(8,128)}, u32[]{:S(2)}) copy-start(f32[272,128]{1,0:T(8,128)} %constant.16.clone.fall_ref) | copy-start | bytes 417796
  20.4 2.6 %copy-start.4 = (f32[272,128]{1,0:T(8,128)S(1)}, f32[272,128]{1,0:T(8,128)}, u32[]{:S(2)}) copy-start(f32[272,128]{1,0:T(8,128)} %constant.15.clone.rise_ref) | copy-start | bytes 417796
  26.4 22.0 %all-to-all-start = ((f32[8,128,128]{2,1,0:T(8,128)}), f32[8,128,128]{2,1,0:T(8,128)S(1)}, u32[]{:S(2)}, u32[]{:S(2)}) async-start(f32[8,128,128]{2,1,0:T(8,128)} %get-tuple-element.33), calls=%async_computation | async-start | bytes 1048576 | tf_op jit(solution)/shard_map/all_to_all | solution.py:553
  32.9 6.4 %collective-permute-start.7 = (f32[80,128]{1,0:T(8,128)S(1)}, f32[80,128]{1,0:T(8,128)S(1)}, u32[]{:S(2)}, u32[]{:S(2)}) collective-permute-start(f32[80,128]{1,0:T(8,128)S(1)} %broadcast_select_fusion), channel_id=1, source_target_pairs={{0,16},{16,0},{1,17},{17,1},{2,18},{18,2},{3,19},{19,3},{4,20},{20... | collective-permute-start | bytes 122888 | tf_op jit(solution)/shard_map/ppermute | solution.py:555
  35.0 3.0 %collective-permute-start.6 = (f32[8,128]{1,0:T(8,128)S(1)}, f32[8,128]{1,0:T(8,128)S(1)}, u32[]{:S(2)}, u32[]{:S(2)}) collective-permute-start(f32[8,128]{1,0:T(8,128)S(1)} %get-tuple-element.32.rest_0_), channel_id=1, source_target_pairs={{0,12},{4,8},{8,4},{12,0},{1,13},{5,9},{9,5},{13,1},{2,14},{6,10},... | collective-permute-start | bytes 12296 | tf_op jit(solution)/shard_map/ppermute | solution.py:512
  35.0 3.6 %collective-permute-start.5 = (f32[8,128]{1,0:T(8,128)S(1)}, f32[8,128]{1,0:T(8,128)S(1)}, u32[]{:S(2)}, u32[]{:S(2)}) collective-permute-start(f32[8,128]{1,0:T(8,128)S(1)} %get-tuple-element.32.rest_0_), channel_id=1, source_target_pairs={{0,8},{4,12},{8,0},{12,4},{1,9},{5,13},{9,1},{13,5},{2,10},{6,14},... | collective-permute-start | bytes 12296 | tf_op jit(solution)/shard_map/ppermute | solution.py:512
  36.0 2.7 %collective-permute-start.4 = (f32[8,128]{1,0:T(8,128)S(1)}, f32[8,128]{1,0:T(8,128)S(1)}, u32[]{:S(2)}, u32[]{:S(2)}) collective-permute-start(f32[8,128]{1,0:T(8,128)S(1)} %get-tuple-element.32.rest_0_), channel_id=1, source_target_pairs={{0,4},{4,0},{8,12},{12,8},{1,5},{5,1},{9,13},{13,9},{2,6},{6,2},{1... | collective-permute-start | bytes 12296 | tf_op jit(solution)/shard_map/ppermute | solution.py:512
where the time goes:
time: 52.3 us; the launch traced here: 51.8 us
  starting transfers between devices  17.1 us (33%)
  Pallas kernels  12.9 us (25%)
  waiting for transfers between devices  11.6 us (22%)
  local copies, waits for them, and re-layouts  9.42 us (18%)
  between operations  0.75 us (1%)
    pallas_call x7, Pallas kernels, kernel_call(): pl.pallas_call(body, out_shape=shapes, in_specs=[VMEM] * len(args), out_s...  12.9 us
    unnamed x30, local copies, waits for them, and re-layouts  9.42 us
    all_to_all x1, waiting for transfers between devices, on_device(): lax.all_to_all(send, ('fib', 'emg'), split_axis=0, concat_axis=0, tiled=T...  9.12 us
    ppermute x5, starting transfers between devices, xor_swap(): lax.ppermute(value, axis, [(i, i ^ k) for i in range(lax.axis_size(axis))])  7.41 us
    all_to_all x1, starting transfers between devices, on_device(): lax.all_to_all(send, ('fib', 'emg'), split_axis=0, concat_axis=0, tiled=T...  6.46 us
    ppermute x5, waiting for transfers between devices, xor_swap(): lax.ppermute(value, axis, [(i, i ^ k) for i in range(lax.axis_size(axis))])  2.46 us
    ppermute x1, starting transfers between devices, on_device(): lax.ppermute(jnp.where(lax.axis_index('fib') == 0, up, down), 'fib', [(0,...  2.09 us
  transfers between devices with their start and end apart: 9, of which 4 were waited for; matrix products, arithmetic and copies ran while one was open for 0% of the time, Pallas kernels for 5%

commit v1 on v0

v1 whole, which is shorter than its diff:
```python
import jax
import jax.numpy as jnp
import numpy as np
from jax import lax
from jax.experimental import pallas as pl
from jax.experimental.pallas import tpu as pltpu
from jax.sharding import PartitionSpec as P

STEPS = 2
SWEEPS = 4
NPC = 2

time_step = 0.5
conductance = 2000.0
amplitude = 200.0
band_half = 4
low_bound = 0.5
high_bound = 14.0
middle = 0.5 * (high_bound + low_bound)

SUB = 8
LANES = 128
EDGE = SUB // NPC
REACH = SWEEPS - 1
HIGHEST = lax.Precision.HIGHEST
VMEM = pl.BlockSpec(memory_space=pltpu.VMEM)
HBM = pl.BlockSpec(memory_space=pl.ANY)


def kernel_call(body, outs, *args, limit=16 << 20, scratch=(), hbm_ins=(), hbm_outs=()):
    f32 = jnp.float32
    shapes = []
    for i, out in enumerate(outs):
        shape, dtype = out if isinstance(out[0], tuple) else (out, f32)
        shapes.append(
            jax.ShapeDtypeStruct(shape, dtype) if i in hbm_outs else pltpu.VMEM(shape, dtype)
        )
    args = [
        pltpu.with_memory_space_constraint(arg, pltpu.HBM if i in hbm_ins else pltpu.VMEM)
        for i, arg in enumerate(args)
    ]
    return pl.pallas_call(
        body,
        out_shape=shapes,
        in_specs=[HBM if i in hbm_ins else VMEM for i in range(len(args))],
        out_specs=[HBM if i in hbm_outs else VMEM for i in range(len(outs))],
        scratch_shapes=list(scratch),
        compiler_params=pltpu.CompilerParams(vmem_limit_bytes=limit),
    )(*args)


def iota(shape, dim):
    return lax.broadcasted_iota(jnp.int32, shape, dim)


def dot_nt(a, b, precision=None):
    return lax.dot_general(
        a, b, (((1,), (1,)), ((), ())), preferred_element_type=jnp.float32, precision=precision
    )


def split(x):
    high = x.astype(jnp.bfloat16)
    return high, (x - high.astype(jnp.float32)).astype(jnp.bfloat16)


def polynomial():
    spread = 0.5 * (high_bound - low_bound)
    ratio = middle / spread
    weight = 1.0 / ratio
    mul, add, sub = (
        np.polynomial.polynomial.polymul,
        np.polynomial.polynomial.polyadd,
        np.polynomial.polynomial.polysub,
    )
    total, rest, step = np.zeros(1), np.ones(1), np.ones(1) / middle
    for sweep in range(SWEEPS):
        total = add(total, step)
        if sweep + 1 < SWEEPS:
            rest = sub(rest, mul(np.array([middle, 1.0]), step))
            later = 1.0 / (2.0 * ratio - weight)
            step = add(later * weight * step, 2.0 * later / spread * rest)
            weight = later
    return [float(c) for c in total]


def cable_tables(nodes, shards):
    matrix = np.zeros((nodes, nodes))
    index = np.arange(nodes)
    matrix[index, index] = 1.0 + 2.0 * conductance
    matrix[0, 0] = matrix[-1, -1] = 1.0 + conductance
    matrix[index[1:], index[:-1]] = matrix[index[:-1], index[1:]] = -conductance
    inverse = np.linalg.inv(matrix)
    fall = inverse[0]
    rise = inverse[:, -1] / inverse[0, -1]
    local = nodes // shards
    blocks = []
    for k in range(shards):
        mine = slice(k * local, (k + 1) * local)
        tail = np.zeros((SUB, local))
        tail[0], tail[1] = rise[mine], fall[mine]
        blocks.append(np.concatenate([inverse[mine, mine], tail]))
    wide = lambda v: np.repeat(np.pad(v, SUB)[:, None], LANES, axis=1).astype(np.float32)
    return np.concatenate(blocks).astype(np.float32), wide(rise), wide(fall)


def prepare(states, voltage, tissue, tables, coupling, decay, gain, weight, unit, fire, home, cell, emg,
            rows, depth):
    number, nodes, fibres = states.shape
    count = number + number % 2
    size = count * SUB
    span = -(-size // 256) * 256
    mu = fire.shape[1]
    at = number * SUB
    small = [coupling, decay, gain, weight, unit, fire, home, cell]
    large = [states, voltage, tissue, *tables]
    kept = len(large)

    def body(*refs):
        sources, refs = refs[:len(small) + kept], refs[len(small) + kept:]
        big_ref, param_ref, misc_ref = refs[:3]
        homes, refs = refs[3:3 + kept], refs[3 + kept:]
        stages, sems = refs[:-1], refs[-1]
        copies = [
            pltpu.make_async_copy(source, target, sems.at[i])
            for i, (source, target) in enumerate(zip(sources, (*stages, *homes)))
        ]
        for copy in copies:
            copy.start()
        for copy in copies[:len(small)]:
            copy.wait()
        coupling_ref, decay_ref, gain_ref, weight_ref, unit_ref, fire_ref, home_ref, cell_ref = stages
        expand = (iota((size, number), 0) // SUB == iota((size, number), 1))
        spread_f = expand.astype(jnp.float32)
        spread_b = expand.astype(jnp.bfloat16)
        same = iota((size, size), 0) % SUB == iota((size, size), 1) % SUB
        parts = []
        for part in split(coupling_ref[...]):
            tall = jnp.dot(spread_b, part, preferred_element_type=jnp.float32)
            full = dot_nt(tall.astype(jnp.bfloat16), spread_b)
            parts.append(jnp.where(same, full, 0.0).astype(jnp.bfloat16))
        big_ref[...] = jnp.zeros_like(big_ref)
        big_ref[:, 0:size] = parts[0]
        big_ref[:, span:span + size] = parts[1]
        big_ref[:, 2 * span:2 * span + size] = parts[0]
        for i, row in enumerate((1.0 - time_step * decay_ref[...], gain_ref[...], weight_ref[...])):
            wide = jnp.broadcast_to(row, (LANES, number))
            param_ref[i] = dot_nt(spread_f, wide, HIGHEST)[:at].reshape(number, SUB, LANES)
        match = (iota((mu, fibres), 0) == unit_ref[...]).astype(jnp.float32)
        fires = jnp.broadcast_to(fire_ref[...].astype(jnp.float32), (SUB, mu))
        fires = jnp.dot(fires, match, preferred_element_type=jnp.float32, precision=HIGHEST)
        brick, spot = home_ref[...], cell_ref[...]
        row = (brick // emg) * rows + spot // depth
        column = (brick % emg) * depth + spot % depth
        line = iota((SUB, fibres), 0)
        out = jnp.where(line == 0, row.astype(jnp.float32), column.astype(jnp.float32))
        misc_ref[...] = jnp.where(line == 2, fires, out)
        for copy in copies[len(small):]:
            copy.wait()

    out = kernel_call(
        body,
        [((size, 3 * span), jnp.bfloat16), (3, number, SUB, LANES), (SUB, fibres),
         *(array.shape for array in large)],
        *small, *large,
        hbm_ins=range(len(small) + kept),
        scratch=[
            *(pltpu.VMEM(array.shape, array.dtype) for array in small),
            pltpu.SemaphoreType.DMA((len(small) + kept,)),
        ],
    )
    return out[:3], out[3:]


def coupled(big, first, second):
    states = first.shape[0]
    pad = big.shape[0] - states * SUB
    span = big.shape[1] // 3
    both = jnp.concatenate(
        [first.reshape(states * SUB, LANES), second.reshape(states * SUB, LANES)], axis=1
    )
    if pad:
        both = jnp.concatenate([both, jnp.zeros((pad, 2 * LANES), jnp.float32)], axis=0)
    high, low = split(both)
    blank = [jnp.zeros((span - both.shape[0], 2 * LANES), jnp.bfloat16)]
    if span == both.shape[0]:
        blank = []
    stacked = jnp.concatenate([high, *blank, high, *blank, low, *blank], axis=0)
    out = jnp.dot(big, stacked, preferred_element_type=jnp.float32)[:states * SUB]
    return (out[:, :LANES].reshape(states, SUB, LANES), out[:, LANES:].reshape(states, SUB, LANES))


def advanced(values, drive, param_ref, voltage):
    drive = drive + param_ref[1] * voltage[None]
    values = param_ref[0] * values + time_step * jnp.tanh(drive)
    return values, jnp.sum(param_ref[2] * values, axis=0)


def cable(voltage, current, fires, step, table_ref, shard, shards):
    nodes = voltage.shape[0]
    place = shard * nodes + iota((nodes, 1), 0)
    centre = nodes * shards // 2
    band = ((place >= centre - band_half) & (place < centre + band_half)).astype(jnp.float32)
    active = (fires == float(step)).astype(jnp.float32)
    right = voltage + time_step * (amplitude * band * active - current)
    size = nodes + SUB
    table = table_ref[pl.ds(pl.multiple_of(shard * size, SUB), size), :]
    return jnp.dot(table, right, preferred_element_type=jnp.float32, precision=HIGHEST)


def far_sums(rows, owners, target):
    below = sum(jnp.where(owner < target, row[0:1], 0.0) for row, owner in zip(rows, owners))
    above = sum(jnp.where(owner > target, row[1:2], 0.0) for row, owner in zip(rows, owners))
    return below, above


def from_far(rise_ref, fall_ref, start, count, below, above):
    here = pl.ds(pl.multiple_of(start, SUB), count)
    return rise_ref[here, :] * above + fall_ref[here, :] * below


def first_step(shards, states, voltage, big, param, misc, table):
    count, nodes, fibres = states.shape

    def body(states_ref, voltage_ref, big_ref, param_ref, misc_ref, table_ref,
             states_out, solved_ref, current_ref, sums_ref):
        shard = lax.axis_index("len")
        big = big_ref[...]
        for start in range(0, nodes, 2 * SUB):
            one, two = pl.ds(start, SUB), pl.ds(start + SUB, SUB)
            first, second = states_ref[:, one, :], states_ref[:, two, :]
            for here, values, drive in zip((one, two), (first, second), coupled(big, first, second)):
                values, current = advanced(values, drive, param_ref, voltage_ref[here, :])
                states_out[:, here, :] = values
                current_ref[here, :] = current
        solved = cable(
            voltage_ref[...], current_ref[...], misc_ref[2:3, :], 0, table_ref, shard, shards
        )
        solved_ref[...] = solved[:nodes]
        sums_ref[...] = solved[nodes:]

    return kernel_call(
        body,
        [(count, nodes, fibres), (nodes, fibres), (nodes, fibres), (SUB, fibres)],
        states, voltage, big, param, misc, table,
    )


def coupled_all(states, big):
    def body(states_ref, big_ref, out_ref):
        big = big_ref[...]
        for start in range(0, states.shape[1], 2 * SUB):
            one, two = pl.ds(start, SUB), pl.ds(start + SUB, SUB)
            out_ref[:, one, :], out_ref[:, two, :] = coupled(
                big, states_ref[:, one, :], states_ref[:, two, :]
            )

    return kernel_call(body, [states.shape], states, big)[0]


def second_step(states, drive, solved, current, param, misc, table, rise, fall, near):
    count, nodes, fibres = states.shape
    cells = nodes // NPC
    shards = len(near)

    def body(states_ref, drive_ref, solved_ref, current_ref, param_ref, misc_ref, table_ref, rise_ref,
             fall_ref, *rest):
        near_refs, rest = rest[:shards], rest[shards:]
        states_out, next_ref, flows_ref, sums_ref, *face_refs, volt_ref, line_ref = rest
        shard = lax.axis_index("len")
        rows = [ref[0:SUB, :] for ref in near_refs]
        owners = [jnp.bitwise_xor(shard, k) for k in range(shards)]
        below, above = far_sums(rows, owners, shard)
        volt_ref[...] = solved_ref[...] + from_far(
            rise_ref, fall_ref, SUB + shard * nodes, nodes, below, above
        )
        line_ref[0:nodes, :] = current_ref[...]
        for start in range(0, nodes, SUB):
            here = pl.ds(start, SUB)
            values, flow = advanced(
                states_ref[:, here, :], drive_ref[:, here, :], param_ref, volt_ref[here, :]
            )
            states_out[:, here, :] = values
            line_ref[nodes + start:nodes + start + SUB, :] = flow
        binned = line_ref[pl.ds(0, STEPS * cells, stride=NPC), :]
        for k in range(1, NPC):
            binned = binned + line_ref[pl.ds(k, STEPS * cells, stride=NPC), :]
        flows_ref[...] = binned
        solved = cable(
            volt_ref[...], line_ref[nodes:2 * nodes, :], misc_ref[2:3, :], 1, table_ref, shard, shards
        )
        next_ref[...] = solved[:nodes]
        sums = solved[nodes:]
        sums_ref[...] = sums
        first = jnp.concatenate([binned[t * cells:t * cells + EDGE] for t in range(STEPS)], axis=0)
        last = jnp.concatenate(
            [binned[(t + 1) * cells - EDGE:(t + 1) * cells] for t in range(STEPS)], axis=0
        )
        for ref, k in zip(face_refs, facing(shards)):
            ref[0:SUB, :] = sums
            ref[SUB:, :] = for_partner(shard, k, first, last)

    edge = (SUB + STEPS * EDGE, fibres)
    return kernel_call(
        body,
        [(count, nodes, fibres), (nodes, fibres), (STEPS * cells, fibres), (SUB, fibres)]
        + [edge] * len(facing(shards)),
        states, drive, solved, current, param, misc, table, rise, fall, *near,
        scratch=[
            pltpu.VMEM((nodes, fibres), jnp.float32),
            pltpu.VMEM((STEPS * nodes, fibres), jnp.float32),
        ],
    )


def packed(fib, flows, misc, near, wide, ends, rows):
    shards = len(near)
    cells = flows.shape[0] // STEPS
    fibres = flows.shape[1]
    long = cells + 2 * EDGE
    tall = STEPS * long
    layers = 2 * long

    def body(flows_ref, misc_ref, wide_ref, lanes_ref, *rest):
        near_refs, (send_ref, ends_ref, *face_refs) = rest[:shards], rest[shards:]
        before, after = beside("len", near_refs, slice(SUB, None))
        for t in range(STEPS):
            base = t * long
            part = slice(t * EDGE, (t + 1) * EDGE)
            send_ref[base:base + EDGE, :] = before[part]
            send_ref[base + EDGE:base + EDGE + cells, :] = flows_ref[t * cells:(t + 1) * cells, :]
            send_ref[base + EDGE + cells:base + long, :] = after[part]
        send_ref[0:1, :] = misc_ref[0:1, :]
        send_ref[long - 1:long, :] = misc_ref[1:2, :]
        ends_ref[0:tall, :] = send_ref[...]
        ends_ref[tall:, :] = lanes_ref[...]
        first, last = wide_ref[0:layers, :], wide_ref[rows * long - layers:, :]
        for ref, k in zip(face_refs, facing(fib)):
            ref[0:tall, :] = send_ref[...]
            ref[tall:, :] = for_partner(lax.axis_index("fib"), k, first, last)

    return kernel_call(
        body,
        [(tall, fibres), (tall + long, fibres)] + [(tall + layers, fibres)] * len(facing(fib)),
        flows, misc, wide, ends, *near,
    )


def finished(states, solved, rise, fall, near):
    nodes, fibres = solved.shape
    shards = len(near)

    def body(states_ref, solved_ref, rise_ref, fall_ref, *rest):
        near_refs, (states_out, voltage_out, volt_ref, sems) = rest[:shards], rest[shards:]
        move = pltpu.make_async_copy(states_ref, states_out, sems.at[0])
        move.start()
        shard = lax.axis_index("len")
        rows = [ref[0:SUB, :] for ref in near_refs]
        owners = [jnp.bitwise_xor(shard, k) for k in range(shards)]
        below, above = far_sums(rows, owners, shard)
        volt_ref[...] = solved_ref[...] + from_far(
            rise_ref, fall_ref, SUB + shard * nodes, nodes, below, above
        )
        place = pltpu.make_async_copy(volt_ref, voltage_out, sems.at[1])
        place.start()
        move.wait()
        place.wait()

    return kernel_call(
        body,
        [states.shape, (nodes, fibres)],
        states, solved, rise, fall, *near,
        hbm_outs=(0, 1),
        scratch=[pltpu.VMEM((nodes, fibres), jnp.float32), pltpu.SemaphoreType.DMA((2,))],
    )


def facing(count):
    return [k for k in range(1, count) if k & (k + 1) == 0]


def for_partner(place, k, first, last):
    return jnp.where(jnp.bitwise_xor(place, k) == place + 1, last, first)


def beside(axis, refs, part):
    place = lax.axis_index(axis)
    return tuple(
        sum(
            jnp.where(jnp.bitwise_xor(place, k) == place + side, refs[k][part], 0.0)
            for k in facing(len(refs))
        )
        for side in (-1, 1)
    )


def with_faces(shards, sums, tissue, rows):
    face = 2 * rows

    def body(sums_ref, tissue_ref, *refs):
        first, last = tissue_ref[0:face, :], tissue_ref[tissue.shape[0] - face:, :]
        for ref, k in zip(refs, facing(shards)):
            ref[0:SUB, :] = sums_ref[...]
            ref[SUB:, :] = for_partner(lax.axis_index("len"), k, first, last)

    edge = (SUB + face, tissue.shape[1])
    return kernel_call(body, [edge] * len(facing(shards)), sums, tissue)


def widened(tissue, near, rows):
    shards = len(near)
    cells = tissue.shape[0] // rows
    long = cells + 2 * EDGE
    depth = tissue.shape[1]

    def body(tissue_ref, *rest):
        near_refs, (wide_ref, lanes_ref) = rest[:shards], rest[shards:]
        wide_ref[...] = jnp.zeros_like(wide_ref)
        before, after = beside("len", near_refs, slice(SUB, None))
        lane = iota((long, depth), 1)
        out = jnp.zeros((long, depth), jnp.float32)
        for y in range(rows):
            base = y * long + EDGE
            wide_ref[base:base + cells, :] = tissue_ref[pl.ds(y, cells, stride=rows), :]
            for k in range(2):
                row = k * rows + y
                wide_ref[base - 2 + k:base - 1 + k, :] = before[row:row + 1]
                wide_ref[base + cells + k:base + cells + k + 1, :] = after[row:row + 1]
            slab = wide_ref[y * long:(y + 1) * long, :]
            spot = lane - 8 * y
            out = jnp.where((spot >= 0) & (spot < 2), pltpu.roll(slab, 8 * y, 1) if y else slab, out)
            out = jnp.where((spot >= 2) & (spot < 4), pltpu.roll(slab, 8 * y + 4, 1), out)
        lanes_ref[...] = out

    return kernel_call(body, [(rows * long, depth), (long, depth)], tissue, *near)


def operator_terms(sizes, wide, blocks, rows):
    shards, fib, emg = sizes
    long = wide.shape[0] // rows
    depth = wide.shape[1]
    cells = long - 2 * EDGE
    tall, lanes = STEPS * long, 2 * depth
    needed = sorted(
        (k, m) for k in (0, *facing(fib)) for m in (0, *facing(emg)) if k or m
    )

    def body(wide_ref, *refs):
        block, (diag_ref, mask_ref) = dict(zip(needed, refs)), refs[len(needed):]
        shard, mine, place = (lax.axis_index(a) for a in ("len", "fib", "emg"))
        below, above = beside(
            "fib", [block.get((k, 0)) for k in range(fib)], slice(tall, tall + 2 * long)
        )

        def end_lanes(k):
            line = [block.get((k, m)) for m in range(emg)]
            return beside("emg", line, slice(tall, tall + long))

        def of(side):
            parts = [
                [jnp.where(jnp.bitwise_xor(mine, k) == mine + side, v, 0.0) for v in end_lanes(k)]
                for k in facing(fib)
            ]
            return [sum(part) for part in zip(*parts)]

        own, under, over = end_lanes(0), of(-1), of(1)
        spot = iota((long, depth), 1)
        for y in range(-2, rows + 2):
            if y < 0:
                main = below[(y + 2) * long:(y + 3) * long]
            elif y >= rows:
                main = above[(y - rows) * long:(y - rows + 1) * long]
            else:
                main = wide_ref[y * long:(y + 1) * long, :]
            side = jnp.zeros((long, depth), jnp.float32)
            if -2 < y < rows + 1:
                before, after = under if y < 0 else over if y >= rows else own
                k = y % rows
                after = pltpu.roll(after, depth - 8 * k, 1) if k else after
                before = pltpu.roll(before, depth - 4 - 8 * k, 1)
                side = jnp.where(spot < 2, after, jnp.where(spot >= depth - 2, before, side))
            whole = jnp.concatenate([main, side], axis=1) + (6.0 - middle)
            base = (y + 2) * tall
            for step in range(STEPS):
                diag_ref[base + step * long:base + (step + 1) * long, :] = whole
        x = lax.rem(iota((tall, lanes), 0), long) - EDGE + shard * cells
        z = iota((tall, lanes), 1)
        z = jnp.where(z < lanes - depth // 2, z, z - lanes) + place * depth
        mask_ref[...] = (
            (x >= 0) & (x < shards * cells) & (z >= 0) & (z < emg * depth)
        ).astype(jnp.float32)

    return kernel_call(
        body,
        [((rows + 4) * tall, lanes), (tall, lanes)],
        wide, *(blocks[key] for key in needed),
    )


def potentials(fib, got, diag, mask, rows):
    tall, lanes = mask.shape
    fibres = got[0].shape[1]
    groups = len(got)
    long = tall // STEPS
    depth = lanes // 2
    cells = long - 2 * EDGE
    slabs = rows + 2 * REACH
    coefs = polynomial()
    scale = [c / coefs[-1] for c in coefs]

    def body(*refs):
        got_refs = refs[:groups]
        diag_ref, mask_ref, out_ref, hot_ref, left_ref, src_ref, one_ref, two_ref = refs[groups:]
        mine, place = lax.axis_index("fib"), lax.axis_index("emg")
        lane = iota((lanes, fibres), 0)
        lane = jnp.where(lane < lanes - depth // 2, lane, lane - lanes)
        lane = jnp.where((lane >= -REACH) & (lane < depth + REACH), lane, -lanes)
        for g, got_ref in enumerate(got_refs):
            column = got_ref[long - 1:long, :].astype(jnp.int32) - place * depth
            hot_ref[:, g * fibres:(g + 1) * fibres] = (lane == column).astype(jnp.bfloat16)
            both = jnp.concatenate(split(got_ref[0:tall, :]), axis=0)
            row = got_ref[0:1, :].astype(jnp.int32) - mine * rows + REACH
            for y in range(slabs):
                pick = (row == y).astype(jnp.float32).astype(jnp.bfloat16)
                left_ref[y * 2 * tall:(y + 1) * 2 * tall, g * fibres:(g + 1) * fibres] = both * pick
        product = dot_nt(left_ref[...], hot_ref[...])
        for y in range(slabs):
            base = y * 2 * tall
            src_ref[y * tall:(y + 1) * tall, :] = (
                product[base:base + tall] + product[base + tall:base + 2 * tall]
            )

        def sweep(ref, y, constant):
            here = lambda k: ref[(k + REACH) * tall:(k + REACH + 1) * tall, :]
            centre = here(y)
            beside = here(y - 1) + here(y + 1)
            beside = beside + pltpu.roll(centre, 1, 0) + pltpu.roll(centre, tall - 1, 0)
            beside = beside + pltpu.roll(centre, 1, 1) + pltpu.roll(centre, lanes - 1, 1)
            diag = diag_ref[(y + 2) * tall:(y + 3) * tall, :]
            source = src_ref[(y + REACH) * tall:(y + REACH + 1) * tall, :]
            return diag * centre - beside + constant * source

        for k, (source, target) in enumerate(((src_ref, one_ref), (one_ref, two_ref))):
            reach = REACH - 1 - k
            for y in range(-reach, rows + reach):
                value = sweep(source, y, scale[2 - k]) * mask_ref[...]
                if y < 0:
                    value = value * (mine > 0).astype(jnp.float32)
                if y >= rows:
                    value = value * (mine < fib - 1).astype(jnp.float32)
                target[(y + REACH) * tall:(y + REACH + 1) * tall, :] = value
        for y in range(rows):
            value = sweep(two_ref, y, scale[0])[:, :depth] * coefs[-1]
            for step in range(STEPS):
                begin = step * long + EDGE
                out_ref[pl.ds(step * cells * rows + y, cells, stride=rows), :] = value[
                    begin:begin + cells
                ]

    f32, b16 = jnp.float32, jnp.bfloat16
    wide_k = groups * fibres
    return pl.pallas_call(
        body,
        out_shape=jax.ShapeDtypeStruct((STEPS * cells * rows, depth), f32),
        in_specs=[VMEM] * (groups + 2),
        out_specs=VMEM,
        scratch_shapes=[
            pltpu.VMEM((lanes, wide_k), b16),
            pltpu.VMEM((slabs * 2 * tall, wide_k), b16),
            pltpu.VMEM((slabs * tall, lanes), f32),
            pltpu.VMEM((slabs * tall, lanes), f32),
            pltpu.VMEM((slabs * tall, lanes), f32),
        ],
        compiler_params=pltpu.CompilerParams(
            vmem_limit_bytes=(20 << 20) + slabs * 2 * tall * wide_k * 2
        ),
    )(*(pltpu.with_memory_space_constraint(a, pltpu.VMEM) for a in (*got, diag, mask)))


def xor_swap(value, axis, k):
    return lax.ppermute(value, axis, [(i, i ^ k) for i in range(lax.axis_size(axis))])


def swaps(axis, plain, faces):
    count = lax.axis_size(axis)
    faces = dict(zip(facing(count), faces))
    return [plain, *(xor_swap(faces.get(k, plain), axis, k) for k in range(1, count))]


def on_device(
    states,
    voltage,
    coupling,
    decay_rates,
    volt_gain,
    current_weights,
    fibre_home,
    cross_cell,
    motor_unit,
    stim_step,
    tissue,
):
    count, nodes, fibres = states.shape
    cells, rows, depth = tissue.shape
    shards, fib, emg = (lax.axis_size(a) for a in ("len", "fib", "emg"))
    groups = fib * emg
    line = lambda v: v.reshape(1, v.size)
    tables = [jnp.asarray(t) for t in cable_tables(nodes * shards, shards)]
    (big, param, misc), kept = prepare(
        states, voltage, tissue.reshape(cells * rows, depth), tables,
        coupling, line(decay_rates), line(volt_gain), line(current_weights),
        line(motor_unit), line(stim_step), line(fibre_home), line(cross_cell), emg, rows, depth,
    )
    states, voltage, flat, table, rise, fall = kept
    states, solved, current, sums = first_step(shards, states, voltage, big, param, misc, table)
    near = swaps("len", sums, with_faces(shards, sums, flat, rows))
    drive = coupled_all(states, big)
    states, solved, flows, sums, *faces = second_step(
        states, drive, solved, current, param, misc, table, rise, fall, near
    )
    wide, ends = widened(flat, near, rows)
    near = swaps("len", sums, faces)
    send, with_ends, *with_layers = packed(fib, flows, misc, near, wide, ends, rows)
    blocks = {(k, 0): block for k, block in enumerate(swaps("fib", send, with_layers))}
    across = swaps("emg", send, [with_ends] * len(facing(emg)))
    for m in range(1, emg):
        for k, block in enumerate(swaps("fib", across[m], [across[m]] * len(facing(fib)))):
            blocks[k, m] = block
    states, voltage = finished(states, solved, rise, fall, near)
    diag, mask = operator_terms((shards, fib, emg), wide, blocks, rows)
    potential = potentials(fib, [blocks[key] for key in sorted(blocks)], diag, mask, rows)
    return states, voltage, potential.reshape(STEPS, cells, rows, depth)


def solution(mesh):
    return jax.shard_map(
        on_device,
        mesh=mesh,
        in_specs=(
            P(None, "len", ("fib", "emg")),
            P("len", ("fib", "emg")),
            P(),
            P(),
            P(),
            P(),
            P(("fib", "emg"), None),
            P(("fib", "emg")),
            P(("fib", "emg")),
            P(),
            P("len", "fib", "emg"),
        ),
        out_specs=(
            P(None, "len", ("fib", "emg")),
            P("len", ("fib", "emg")),
            P(None, "len", "fib", "emg"),
        ),
        check_vma=False,
    )
```

time: 52.3 us -> 36.3 us (0.69)
  local copies, waits for them, and re-layouts: 9.42 us -> 0 us
  waiting for transfers between devices: 11.6 us -> 8.39 us
  starting transfers between devices: 17.1 us -> 14.3 us
    unnamed x30 -> x0, local copies, waits for them, and re-layouts: 9.42 us -> none
    all_to_all x1 -> x0, waiting for transfers between devices: 9.12 us -> none  [on_device(): lax.all_to_all(send, ('fib', 'emg'), split_axis=0, concat_axis=0, tiled=T...]
    ppermute x5 -> x13, starting transfers between devices: 7.41 us -> 14.3 us  [xor_swap(): lax.ppermute(value, axis, [(i, i ^ k) for i in range(lax.axis_size(axis))])]
    all_to_all x1 -> x0, starting transfers between devices: 6.46 us -> none  [on_device(): lax.all_to_all(send, ('fib', 'emg'), split_axis=0, concat_axis=0, tiled=T...]
    ppermute x5 -> x13, waiting for transfers between devices: 2.46 us -> 8.39 us  [xor_swap(): lax.ppermute(value, axis, [(i, i ^ k) for i in range(lax.axis_size(axis))])]
    ppermute x3 -> x0, starting transfers between devices: 3.28 us -> none  [the longest x1 2.09 us: on_device(): lax.ppermute(jnp.where(lax.axis_index('fib') == 0, up, down), 'fib', [(0,...]
    pallas_call x7 -> x10, Pallas kernels: 12.9 us -> 12.6 us  [the longest x9 9.11 us: kernel_call(): pl.pallas_call(body, out_shape=shapes, in_specs=[HBM if i in hbm_ins else...]
  transfers between devices with their start and end apart: 9 -> 13, of which waited for: 4 -> 5; matrix products, arithmetic and copies ran while one was open for 0% -> 0% of each run, Pallas kernels for 5% -> 9%
where the time goes in v1:
time: 36.3 us; the launch traced here: 36.1 us
  starting transfers between devices  14.3 us (39%)
  Pallas kernels  12.6 us (35%)
  waiting for transfers between devices  8.39 us (23%)
  between operations  0.74 us (2%)
    ppermute x13, starting transfers between devices, xor_swap(): lax.ppermute(value, axis, [(i, i ^ k) for i in range(lax.axis_size(axis))])  14.3 us
    pallas_call x9, Pallas kernels, kernel_call(): pl.pallas_call(body, out_shape=shapes, in_specs=[HBM if i in hbm_ins else...  9.11 us
    ppermute x13, waiting for transfers between devices, xor_swap(): lax.ppermute(value, axis, [(i, i ^ k) for i in range(lax.axis_size(axis))])  8.39 us
    pallas_call x1, Pallas kernels, potentials(): pl.pallas_call(body, out_shape=jax.ShapeDtypeStruct((STEPS * cells * rows...  3.53 us
  transfers between devices with their start and end apart: 13, of which 5 were waited for; matrix products, arithmetic and copies ran while one was open for 0% of the time, Pallas kernels for 9%

profile of v1, /device:TPU:0, one launch (start us, length us, event | category | flops | bytes accessed | tf_op | source)
XLA Modules:
  0.0 36.1 jit_solution(5703151573715894762)
XLA Ops:
  0.6 2.4 %shard_map.157 = (bf16[464,1536]{1,0:T(8,128)(2,1)S(1)}, f32[3,57,8,128]{3,2,1,0:T(8,128)S(1)}, f32[8,128]{1,0:T(8,128)S(1)}, f32[57,64,128]{2,1,0:T(8,128)S(1)}...) custom-call(f32[57,57]{1,0:T(8,128)} %refs_0_.1, ...), custom_call_target="tpu_custom_call" | custom-call | tf_op jit(solution)/shard_map/pallas_call | solution.py:42
  3.0 2.1 %shard_map.158 = (f32[57,64,128]{2,1,0:T(8,128)S(1)}, f32[64,128]{1,0:T(8,128)S(1)}, f32[64,128]{1,0:T(8,128)S(1)}, f32[8,128]{1,0:T(8,128)S(1)}) custom-call(f32[57,64,128]{2,1,0:T(8,128)S(1)} %get-tuple-element.33.states_ref, f32[64,128]{1,0:T(8,128)S(1)} %get-tuple-element.34.voltage_ref, bf16[464,1536]{1,0:T(8,128)(2,1)S(1)} %get-tuple-element.35.big_ref, ...), custom_call_target="tpu_custom_call" | custom-call | tf_op jit(solution)/shard_map/pallas_call | solution.py:42
  5.2 0.5 %collective-permute-start = (f32[24,128]{1,0:T(8,128)S(1)}, f32[24,128]{1,0:T(8,128)S(1)}, u32[]{:S(2)}, u32[]{:S(2)}) collective-permute-start(f32[24,128]{1,0:T(8,128)S(1)} %get-tuple-element.46), channel_id=1, source_target_pairs={{0,4},{4,0},{8,12},{12,8},{1,5},{5,1},{9,13},{13,9},{2,6},{6,2},{1... | collective-permute-start | bytes 36872 | tf_op jit(solution)/shard_map/ppermute | solution.py:581
  5.7 2.6 %collective-permute-start.2 = (f32[24,128]{1,0:T(8,128)S(1)}, f32[24,128]{1,0:T(8,128)S(1)}, u32[]{:S(2)}, u32[]{:S(2)}) collective-permute-start(f32[24,128]{1,0:T(8,128)S(1)} %get-tuple-element.47), channel_id=1, source_target_pairs={{0,12},{4,8},{8,4},{12,0},{1,13},{5,9},{9,5},{13,1},{2,14},{6,10},... | collective-permute-start | bytes 36872 | tf_op jit(solution)/shard_map/ppermute | solution.py:581
  8.3 0.0 collective-permute-start.1
  8.4 1.7 %shard_map.159.drive_ref = f32[57,64,128]{2,1,0:T(8,128)S(1)} custom-call(f32[57,64,128]{2,1,0:T(8,128)S(1)} %get-tuple-element.39.states_ref, bf16[464,1536]{1,0:T(8,128)(2,1)S(1)} %get-tuple-element.35.big_ref), custom_call_target="tpu_custom_call" | custom-call | tf_op jit(solution)/shard_map/pallas_call | solution.py:42
  10.1 1.9 %collective-permute-done.1.rest_2_ = f32[8,128]{1,0:T(8,128)S(1)} collective-permute-done((f32[8,128]{1,0:T(8,128)S(1)}, f32[8,128]{1,0:T(8,128)S(1)}, u32[]{:S(2)}, u32[]{:S(2)}) %collective-permute-start.1) | collective-permute-done | bytes 4128 | tf_op jit(solution)/shard_map/ppermute | solution.py:581
  11.9 0.0 collective-permute-done.rest_1_
  12.0 0.0 collective-permute-done.2.rest_3_
  12.0 1.2 %shard_map.161 = (f32[57,64,128]{2,1,0:T(8,128)S(1)}, f32[64,128]{1,0:T(8,128)S(1)}, f32[64,128]{1,0:T(8,128)S(1)}, f32[8,128]{1,0:T(8,128)S(1)}, f32[16,128]{1,0:T(8,128)S(1)}, /*index=5*/f32[16,128]{1,0:T(8,128)S(1)}) custom-call(f32[57,64,128]{2,1,0:T(8,128)S(1)} %get-tuple-element.39.states_ref, f32[57,64,128]{2,1,0:T(8,128)S(1)} %shard_map.159.drive_ref, ...), custom_call_target="tpu_custom_call" | custom-call | tf_op jit(solution)/shard_map/pallas_call | solution.py:42
  13.2 0.1 collective-permute-start.3
  13.3 0.2 collective-permute-start.5
  13.5 1.9 %collective-permute-start.4 = (f32[8,128]{1,0:T(8,128)S(1)}, f32[8,128]{1,0:T(8,128)S(1)}, u32[]{:S(2)}, u32[]{:S(2)}) collective-permute-start(f32[8,128]{1,0:T(8,128)S(1)} %get-tuple-element.50.rest_0_), channel_id=1, source_target_pairs={{0,8},{4,12},{8,0},{12,4},{1,9},{5,13},{9,1},{13,5},{2,10},{6,14},... | collective-permute-start | bytes 12296 | tf_op jit(solution)/shard_map/ppermute | solution.py:581
  15.4 0.2 shard_map.163
  15.6 1.5 %collective-permute-done.4.rest_2_ = f32[8,128]{1,0:T(8,128)S(1)} collective-permute-done((f32[8,128]{1,0:T(8,128)S(1)}, f32[8,128]{1,0:T(8,128)S(1)}, u32[]{:S(2)}, u32[]{:S(2)}) %collective-permute-start.4) | collective-permute-done | bytes 4128 | tf_op jit(solution)/shard_map/ppermute | solution.py:581
  17.1 0.0 collective-permute-done.3.rest_1_
  17.1 0.0 collective-permute-done.5.rest_3_
  17.2 2.0 %collective-permute-start.6 = (f32[120,128]{1,0:T(8,128)S(1)}, f32[120,128]{1,0:T(8,128)S(1)}, u32[]{:S(2)}, u32[]{:S(2)}) collective-permute-start(f32[120,128]{1,0:T(8,128)S(1)} %get-tuple-element.59), channel_id=1, source_target_pairs={{0,1},{1,0},{2,3},{3,2},{4,5},{5,4},{6,7},{7,6},{8,9},{9,8},{10,11... | collective-permute-start | bytes 184328 | tf_op jit(solution)/shard_map/ppermute | solution.py:581
  19.2 2.5 %collective-permute-start.8 = (f32[120,128]{1,0:T(8,128)S(1)}, f32[120,128]{1,0:T(8,128)S(1)}, u32[]{:S(2)}, u32[]{:S(2)}) collective-permute-start(f32[120,128]{1,0:T(8,128)S(1)} %get-tuple-element.59), channel_id=1, source_target_pairs={{0,3},{1,2},{2,1},{3,0},{4,7},{5,6},{6,5},{7,4},{8,11},{9,10},{10,... | collective-permute-start | bytes 184328 | tf_op jit(solution)/shard_map/ppermute | solution.py:581
  21.7 1.5 %collective-permute-start.9 = (f32[160,128]{1,0:T(8,128)S(1)}, f32[160,128]{1,0:T(8,128)S(1)}, u32[]{:S(2)}, u32[]{:S(2)}) collective-permute-start(f32[160,128]{1,0:T(8,128)S(1)} %get-tuple-element.60), channel_id=1, source_target_pairs={{0,16},{16,0},{1,17},{17,1},{2,18},{18,2},{3,19},{19,3},{4,20},{20... | collective-permute-start | bytes 245768 | tf_op jit(solution)/shard_map/ppermute | solution.py:581
  23.2 0.1 collective-permute-start.7
  23.3 0.0 collective-permute-done.6.refs_0_.refs_1_
  23.3 0.5 %collective-permute-start.10 = (f32[120,128]{1,0:T(8,128)S(1)}, f32[120,128]{1,0:T(8,128)S(1)}, u32[]{:S(2)}, u32[]{:S(2)}) collective-permute-start(f32[120,128]{1,0:T(8,128)S(1)} %collective-permute-done.6.refs_0_.refs_1_), channel_id=1, source_target_pairs={{0,16},{16,0},{1,17},{17,1},{2,18},{18,2},{3,19},{19,3},{4,20},{20... | collective-permute-start | bytes 184328 | tf_op jit(solution)/shard_map/ppermute | solution.py:581
  23.9 1.4 %collective-permute-done.8.refs_1_.refs_3_ = f32[120,128]{1,0:T(8,128)S(1)} collective-permute-done((f32[120,128]{1,0:T(8,128)S(1)}, f32[120,128]{1,0:T(8,128)S(1)}, u32[]{:S(2)}, u32[]{:S(2)}) %collective-permute-start.8) | collective-permute-done | bytes 61472 | tf_op jit(solution)/shard_map/ppermute | solution.py:581
  25.2 1.8 %collective-permute-start.12 = (f32[120,128]{1,0:T(8,128)S(1)}, f32[120,128]{1,0:T(8,128)S(1)}, u32[]{:S(2)}, u32[]{:S(2)}) collective-permute-start(f32[120,128]{1,0:T(8,128)S(1)} %collective-permute-done.8.refs_1_.refs_3_), channel_id=1, source_target_pairs={{0,16},{16,0},{1,17},{17,1},{2,18},{18,2},{3,19},{19,3},{4,20},{20... | collective-permute-start | bytes 184328 | tf_op jit(solution)/shard_map/ppermute | solution.py:581
  27.0 1.5 %collective-permute-done.7.refs_2_ = f32[80,128]{1,0:T(8,128)S(1)} collective-permute-done((f32[80,128]{1,0:T(8,128)S(1)}, f32[80,128]{1,0:T(8,128)S(1)}, u32[]{:S(2)}, u32[]{:S(2)}) %collective-permute-start.7) | collective-permute-done | bytes 40992 | tf_op jit(solution)/shard_map/ppermute | solution.py:581
  28.6 0.5 %collective-permute-start.11 = (f32[80,128]{1,0:T(8,128)S(1)}, f32[80,128]{1,0:T(8,128)S(1)}, u32[]{:S(2)}, u32[]{:S(2)}) collective-permute-start(f32[80,128]{1,0:T(8,128)S(1)} %collective-permute-done.7.refs_2_), channel_id=1, source_target_pairs={{0,16},{16,0},{1,17},{17,1},{2,18},{18,2},{3,19},{19,3},{4,20},{20... | collective-permute-start | bytes 122888 | tf_op jit(solution)/shard_map/ppermute | solution.py:581
  29.1 1.3 %shard_map.162 = (f32[57,64,128]{2,1,0:T(8,128)}, f32[64,128]{1,0:T(8,128)}) custom-call(f32[57,64,128]{2,1,0:T(8,128)S(1)} %get-tuple-element.48.states_ref, f32[64,128]{1,0:T(8,128)S(1)} %get-tuple-element.49.solved_ref, f32[272,128]{1,0:T(8,128)S(1)} %get-tuple-element.42.rise_ref, f32[272,128]{1,0:T(8,128)S(1)} %get-tuple-element.43.fall_ref, ...), custom_call_target="tpu_custom_call" | custom-call | tf_op jit(solution)/shard_map/pallas_call | solution.py:42
  30.3 0.0 collective-permute-done.9.refs_2_.refs_4_
  30.3 0.0 collective-permute-done.10.refs_3_.refs_5_
  30.4 0.0 collective-permute-done.12.refs_4_.refs_7_
  30.4 0.2 shard_map.165
  30.6 2.0 %collective-permute-done.11.refs_6_ = f32[80,128]{1,0:T(8,128)S(1)} collective-permute-done((f32[80,128]{1,0:T(8,128)S(1)}, f32[80,128]{1,0:T(8,128)S(1)}, u32[]{:S(2)}, u32[]{:S(2)}) %collective-permute-start.11) | collective-permute-done | bytes 40992 | tf_op jit(solution)/shard_map/ppermute | solution.py:581
  32.6 3.5 %shard_map.166 = f32[512,128]{1,0:T(8,128)} custom-call(f32[80,128]{1,0:T(8,128)S(1)} %get-tuple-element.58.refs_0_, f32[120,128]{1,0:T(8,128)S(1)} %collective-permute-done.6.refs_0_.refs_1_, f32[80,128]{1,0:T(8,128)S(1)} %collective-permute-done.7.refs_2_, f32[120,128]{1,0:T(8,128)S(1)} %collective-permute-done.8.refs_1_.refs_3_, ...), custom_call_target="tpu_custom_call" | custom-call | tf_op jit(solution)/shard_map/pallas_call | solution.py:562
  (2 shorter events, 0.0 us)
Async XLA Ops:
  5.2 6.7 %collective-permute-start = (f32[24,128]{1,0:T(8,128)S(1)}, f32[24,128]{1,0:T(8,128)S(1)}, u32[]{:S(2)}, u32[]{:S(2)}) collective-permute-start(f32[24,128]{1,0:T(8,128)S(1)} %get-tuple-element.46), channel_id=1, source_target_pairs={{0,4},{4,0},{8,12},{12,8},{1,5},{5,1},{9,13},{13,9},{2,6},{6,2},{1... | collective-permute-start | bytes 36872 | tf_op jit(solution)/shard_map/ppermute | solution.py:581
  5.7 6.2 %collective-permute-start.2 = (f32[24,128]{1,0:T(8,128)S(1)}, f32[24,128]{1,0:T(8,128)S(1)}, u32[]{:S(2)}, u32[]{:S(2)}) collective-permute-start(f32[24,128]{1,0:T(8,128)S(1)} %get-tuple-element.47), channel_id=1, source_target_pairs={{0,12},{4,8},{8,4},{12,0},{1,13},{5,9},{9,5},{13,1},{2,14},{6,10},... | collective-permute-start | bytes 36872 | tf_op jit(solution)/shard_map/ppermute | solution.py:581
  8.3 3.6 %collective-permute-start.1 = (f32[8,128]{1,0:T(8,128)S(1)}, f32[8,128]{1,0:T(8,128)S(1)}, u32[]{:S(2)}, u32[]{:S(2)}) collective-permute-start(f32[8,128]{1,0:T(8,128)S(1)} %get-tuple-element.44.sums_ref.rest_0_), channel_id=1, source_target_pairs={{0,8},{4,12},{8,0},{12,4},{1,9},{5,13},{9,1},{13,5},{2,10},{6,14},... | collective-permute-start | bytes 12296 | tf_op jit(solution)/shard_map/ppermute | solution.py:581
  13.2 3.9 %collective-permute-start.3 = (f32[16,128]{1,0:T(8,128)S(1)}, f32[16,128]{1,0:T(8,128)S(1)}, u32[]{:S(2)}, u32[]{:S(2)}) collective-permute-start(f32[16,128]{1,0:T(8,128)S(1)} %get-tuple-element.51), channel_id=1, source_target_pairs={{0,4},{4,0},{8,12},{12,8},{1,5},{5,1},{9,13},{13,9},{2,6},{6,2},{1... | collective-permute-start | bytes 24584 | tf_op jit(solution)/shard_map/ppermute | solution.py:581
  13.3 3.9 %collective-permute-start.5 = (f32[16,128]{1,0:T(8,128)S(1)}, f32[16,128]{1,0:T(8,128)S(1)}, u32[]{:S(2)}, u32[]{:S(2)}) collective-permute-start(f32[16,128]{1,0:T(8,128)S(1)} %get-tuple-element.52), channel_id=1, source_target_pairs={{0,12},{4,8},{8,4},{12,0},{1,13},{5,9},{9,5},{13,1},{2,14},{6,10},... | collective-permute-start | bytes 24584 | tf_op jit(solution)/shard_map/ppermute | solution.py:581
  13.5 3.6 %collective-permute-start.4 = (f32[8,128]{1,0:T(8,128)S(1)}, f32[8,128]{1,0:T(8,128)S(1)}, u32[]{:S(2)}, u32[]{:S(2)}) collective-permute-start(f32[8,128]{1,0:T(8,128)S(1)} %get-tuple-element.50.rest_0_), channel_id=1, source_target_pairs={{0,8},{4,12},{8,0},{12,4},{1,9},{5,13},{9,1},{13,5},{2,10},{6,14},... | collective-permute-start | bytes 12296 | tf_op jit(solution)/shard_map/ppermute | solution.py:581
  17.2 6.2 %collective-permute-start.6 = (f32[120,128]{1,0:T(8,128)S(1)}, f32[120,128]{1,0:T(8,128)S(1)}, u32[]{:S(2)}, u32[]{:S(2)}) collective-permute-start(f32[120,128]{1,0:T(8,128)S(1)} %get-tuple-element.59), channel_id=1, source_target_pairs={{0,1},{1,0},{2,3},{3,2},{4,5},{5,4},{6,7},{7,6},{8,9},{9,8},{10,11... | collective-permute-start | bytes 184328 | tf_op jit(solution)/shard_map/ppermute | solution.py:581
  19.2 6.0 %collective-permute-start.8 = (f32[120,128]{1,0:T(8,128)S(1)}, f32[120,128]{1,0:T(8,128)S(1)}, u32[]{:S(2)}, u32[]{:S(2)}) collective-permute-start(f32[120,128]{1,0:T(8,128)S(1)} %get-tuple-element.59), channel_id=1, source_target_pairs={{0,3},{1,2},{2,1},{3,0},{4,7},{5,6},{6,5},{7,4},{8,11},{9,10},{10,... | collective-permute-start | bytes 184328 | tf_op jit(solution)/shard_map/ppermute | solution.py:581
  21.7 8.6 %collective-permute-start.9 = (f32[160,128]{1,0:T(8,128)S(1)}, f32[160,128]{1,0:T(8,128)S(1)}, u32[]{:S(2)}, u32[]{:S(2)}) collective-permute-start(f32[160,128]{1,0:T(8,128)S(1)} %get-tuple-element.60), channel_id=1, source_target_pairs={{0,16},{16,0},{1,17},{17,1},{2,18},{18,2},{3,19},{19,3},{4,20},{20... | collective-permute-start | bytes 245768 | tf_op jit(solution)/shard_map/ppermute | solution.py:581
  23.2 5.3 %collective-permute-start.7 = (f32[80,128]{1,0:T(8,128)S(1)}, f32[80,128]{1,0:T(8,128)S(1)}, u32[]{:S(2)}, u32[]{:S(2)}) collective-permute-start(f32[80,128]{1,0:T(8,128)S(1)} %get-tuple-element.58.refs_0_), channel_id=1, source_target_pairs={{0,2},{1,3},{2,0},{3,1},{4,6},{5,7},{6,4},{7,5},{8,10},{9,11},{10,... | collective-permute-start | bytes 122888 | tf_op jit(solution)/shard_map/ppermute | solution.py:581
  23.3 7.0 %collective-permute-start.10 = (f32[120,128]{1,0:T(8,128)S(1)}, f32[120,128]{1,0:T(8,128)S(1)}, u32[]{:S(2)}, u32[]{:S(2)}) collective-permute-start(f32[120,128]{1,0:T(8,128)S(1)} %collective-permute-done.6.refs_0_.refs_1_), channel_id=1, source_target_pairs={{0,16},{16,0},{1,17},{17,1},{2,18},{18,2},{3,19},{19,3},{4,20},{20... | collective-permute-start | bytes 184328 | tf_op jit(solution)/shard_map/ppermute | solution.py:581
  25.2 5.1 %collective-permute-start.12 = (f32[120,128]{1,0:T(8,128)S(1)}, f32[120,128]{1,0:T(8,128)S(1)}, u32[]{:S(2)}, u32[]{:S(2)}) collective-permute-start(f32[120,128]{1,0:T(8,128)S(1)} %collective-permute-done.8.refs_1_.refs_3_), channel_id=1, source_target_pairs={{0,16},{16,0},{1,17},{17,1},{2,18},{18,2},{3,19},{19,3},{4,20},{20... | collective-permute-start | bytes 184328 | tf_op jit(solution)/shard_map/ppermute | solution.py:581
  28.6 4.0 %collective-permute-start.11 = (f32[80,128]{1,0:T(8,128)S(1)}, f32[80,128]{1,0:T(8,128)S(1)}, u32[]{:S(2)}, u32[]{:S(2)}) collective-permute-start(f32[80,128]{1,0:T(8,128)S(1)} %collective-permute-done.7.refs_2_), channel_id=1, source_target_pairs={{0,16},{16,0},{1,17},{17,1},{2,18},{18,2},{3,19},{19,3},{4,20},{20... | collective-permute-start | bytes 122888 | tf_op jit(solution)/shard_map/ppermute | solution.py:581

commit v2 on v1

--- a/solution.py
+++ b/solution.py
@@ -23,6 +23,7 @@
 EDGE = SUB // NPC
 REACH = SWEEPS - 1
 HIGHEST = lax.Precision.HIGHEST
+PART = 32
 VMEM = pl.BlockSpec(memory_space=pltpu.VMEM)
 HBM = pl.BlockSpec(memory_space=pl.ANY)
 
@@ -104,96 +105,19 @@
     return np.concatenate(blocks).astype(np.float32), wide(rise), wide(fall)
 
 
-def prepare(states, voltage, tissue, tables, coupling, decay, gain, weight, unit, fire, home, cell, emg,
-            rows, depth):
-    number, nodes, fibres = states.shape
-    count = number + number % 2
-    size = count * SUB
-    span = -(-size // 256) * 256
-    mu = fire.shape[1]
-    at = number * SUB
-    small = [coupling, decay, gain, weight, unit, fire, home, cell]
-    large = [states, voltage, tissue, *tables]
-    kept = len(large)
-
-    def body(*refs):
-        sources, refs = refs[:len(small) + kept], refs[len(small) + kept:]
-        big_ref, param_ref, misc_ref = refs[:3]
-        homes, refs = refs[3:3 + kept], refs[3 + kept:]
-        stages, sems = refs[:-1], refs[-1]
-        copies = [
-            pltpu.make_async_copy(source, target, sems.at[i])
-            for i, (source, target) in enumerate(zip(sources, (*stages, *homes)))
-        ]
-        for copy in copies:
-            copy.start()
-        for copy in copies[:len(small)]:
-            copy.wait()
-        coupling_ref, decay_ref, gain_ref, weight_ref, unit_ref, fire_ref, home_ref, cell_ref = stages
-        expand = (iota((size, number), 0) // SUB == iota((size, number), 1))
-        spread_f = expand.astype(jnp.float32)
-        spread_b = expand.astype(jnp.bfloat16)
-        same = iota((size, size), 0) % SUB == iota((size, size), 1) % SUB
-        parts = []
-        for part in split(coupling_ref[...]):
-            tall = jnp.dot(spread_b, part, preferred_element_type=jnp.float32)
-            full = dot_nt(tall.astype(jnp.bfloat16), spread_b)
-            parts.append(jnp.where(same, full, 0.0).astype(jnp.bfloat16))
-        big_ref[...] = jnp.zeros_like(big_ref)
-        big_ref[:, 0:size] = parts[0]
-        big_ref[:, span:span + size] = parts[1]
-        big_ref[:, 2 * span:2 * span + size] = parts[0]
-        for i, row in enumerate((1.0 - time_step * decay_ref[...], gain_ref[...], weight_ref[...])):
-            wide = jnp.broadcast_to(row, (LANES, number))
-            param_ref[i] = dot_nt(spread_f, wide, HIGHEST)[:at].reshape(number, SUB, LANES)
-        match = (iota((mu, fibres), 0) == unit_ref[...]).astype(jnp.float32)
-        fires = jnp.broadcast_to(fire_ref[...].astype(jnp.float32), (SUB, mu))
-        fires = jnp.dot(fires, match, preferred_element_type=jnp.float32, precision=HIGHEST)
-        brick, spot = home_ref[...], cell_ref[...]
-        row = (brick // emg) * rows + spot // depth
-        column = (brick % emg) * depth + spot % depth
-        line = iota((SUB, fibres), 0)
-        out = jnp.where(line == 0, row.astype(jnp.float32), column.astype(jnp.float32))
-        misc_ref[...] = jnp.where(line == 2, fires, out)
-        for copy in copies[len(small):]:
-            copy.wait()
-
-    out = kernel_call(
-        body,
-        [((size, 3 * span), jnp.bfloat16), (3, number, SUB, LANES), (SUB, fibres),
-         *(array.shape for array in large)],
-        *small, *large,
-        hbm_ins=range(len(small) + kept),
-        scratch=[
-            *(pltpu.VMEM(array.shape, array.dtype) for array in small),
-            pltpu.SemaphoreType.DMA((len(small) + kept,)),
-        ],
-    )
-    return out[:3], out[3:]
-
-
-def coupled(big, first, second):
-    states = first.shape[0]
-    pad = big.shape[0] - states * SUB
-    span = big.shape[1] // 3
-    both = jnp.concatenate(
-        [first.reshape(states * SUB, LANES), second.reshape(states * SUB, LANES)], axis=1
-    )
-    if pad:
-        both = jnp.concatenate([both, jnp.zeros((pad, 2 * LANES), jnp.float32)], axis=0)
-    high, low = split(both)
-    blank = [jnp.zeros((span - both.shape[0], 2 * LANES), jnp.bfloat16)]
-    if span == both.shape[0]:
-        blank = []
-    stacked = jnp.concatenate([high, *blank, high, *blank, low, *blank], axis=0)
-    out = jnp.dot(big, stacked, preferred_element_type=jnp.float32)[:states * SUB]
-    return (out[:, :LANES].reshape(states, SUB, LANES), out[:, LANES:].reshape(states, SUB, LANES))
+def coupled(triple, tiles):
+    fibres = tiles[0].shape[1]
+    high, low = split(jnp.concatenate(tiles, axis=1))
+    out = jnp.dot(
+        triple, jnp.concatenate([high, high, low], axis=0), preferred_element_type=jnp.float32
+    )
+    return [out[:, i * fibres:(i + 1) * fibres] for i in range(len(tiles))]
 
 
 def advanced(values, drive, param_ref, voltage):
-    drive = drive + param_ref[1] * voltage[None]
+    drive = drive + param_ref[1] * voltage
     values = param_ref[0] * values + time_step * jnp.tanh(drive)
-    return values, jnp.sum(param_ref[2] * values, axis=0)
+    return values, jnp.sum(param_ref[2] * values, axis=0, keepdims=True)
 
 
 def cable(voltage, current, fires, step, table_ref, shard, shards):
@@ -219,47 +143,117 @@
     return rise_ref[here, :] * above + fall_ref[here, :] * below
 
 
-def first_step(shards, states, voltage, big, param, misc, table):
-    count, nodes, fibres = states.shape
-
-    def body(states_ref, voltage_ref, big_ref, param_ref, misc_ref, table_ref,
-             states_out, solved_ref, current_ref, sums_ref):
-        shard = lax.axis_index("len")
-        big = big_ref[...]
-        for start in range(0, nodes, 2 * SUB):
-            one, two = pl.ds(start, SUB), pl.ds(start + SUB, SUB)
-            first, second = states_ref[:, one, :], states_ref[:, two, :]
-            for here, values, drive in zip((one, two), (first, second), coupled(big, first, second)):
-                values, current = advanced(values, drive, param_ref, voltage_ref[here, :])
-                states_out[:, here, :] = values
-                current_ref[here, :] = current
+def first_step(sizes, states, voltage, tissue, tables, coupling, decay, gain, weight, unit, fire, home,
+               cell):
+    shards, emg, rows, depth = sizes
+    number, nodes, fibres = states.shape
+    tall = -(-number // 16) * 16
+    full = number // SUB * SUB
+    mu = fire.shape[1]
+    small = [coupling, decay, gain, weight, unit, fire, voltage, tables[0]]
+    large = [tissue, *tables[1:], home, cell]
+    count = len(small) + len(large)
+    chunk = PART
+
+    def body(*refs):
+        small_refs, refs = refs[:len(small)], refs[len(small):]
+        large_refs, refs = refs[:len(large)], refs[len(large):]
+        states_ref, refs = refs[0], refs[1:]
+        states_out, solved_ref, current_ref, sums_ref, triple_ref, param_ref, misc_ref = refs[:7]
+        table_out, tissue_out, rise_out, fall_out = refs[7:11]
+        *stages, home_ref, cell_ref, nodes_ref, sems = refs[11:]
+        nodes_ref[:, full:, :] = jnp.zeros((nodes, tall - full, fibres), jnp.float32)
+        copies = [
+            pltpu.make_async_copy(source, target, sems.at[i])
+            for i, (source, target) in enumerate(
+                zip(
+                    (*small_refs, *large_refs),
+                    (*stages, table_out, tissue_out, rise_out, fall_out, home_ref, cell_ref),
+                )
+            )
+        ]
+        loads = [
+            pltpu.make_async_copy(
+                states_ref.at[:, n, :], nodes_ref.at[n, pl.ds(0, number), :], sems.at[count + n // chunk]
+            )
+            for n in range(nodes)
+        ]
+        for copy in (*copies[:len(small)], *loads, *copies[len(small):]):
+            copy.start()
+        for copy in copies[:len(small)]:
+            copy.wait()
+        coupling_ref, decay_ref, gain_ref, weight_ref, unit_ref, fire_ref, voltage_ref = stages
+        own = iota((tall, number), 0) == iota((tall, number), 1)
+        place = own.astype(jnp.bfloat16)
+        blank = jnp.zeros((tall, number), jnp.bfloat16)
+        triple = 0.0
+        for part, spots in zip(split(coupling_ref[...]), ((place, blank, place), (blank, place, blank))):
+            part = jnp.dot(place, part, preferred_element_type=jnp.float32).astype(jnp.bfloat16)
+            triple = triple + dot_nt(part, jnp.concatenate(spots, axis=0))
+        triple = triple.astype(jnp.bfloat16)
+        triple_ref[...] = triple
+        for i, row in enumerate((1.0 - time_step * decay_ref[...], gain_ref[...], weight_ref[...])):
+            column = jnp.sum(jnp.where(own, row, 0.0), axis=1, keepdims=True)
+            param_ref[i] = jnp.broadcast_to(column, (tall, fibres))
+        match = (iota((mu, fibres), 0) == unit_ref[...]).astype(jnp.bfloat16)
+        fires = jnp.broadcast_to(fire_ref[...].astype(jnp.float32), (SUB, mu)).astype(jnp.bfloat16)
+        fires = jnp.dot(fires, match, preferred_element_type=jnp.float32)
+        for begin in range(0, nodes, chunk):
+            here = nodes_ref.at[pl.ds(begin, chunk), pl.ds(0, number), :]
+            pltpu.make_async_copy(here, here, sems.at[count + begin // chunk]).wait()
+            for start in range(begin, begin + chunk, SUB):
+                tiles = [nodes_ref[n] for n in range(start, start + SUB)]
+                for n, tile, drive in zip(range(start, start + SUB), tiles, coupled(triple, tiles)):
+                    states_out[n], current_ref[n:n + 1, :] = advanced(
+                        tile, drive, param_ref, voltage_ref[n:n + 1, :]
+                    )
         solved = cable(
-            voltage_ref[...], current_ref[...], misc_ref[2:3, :], 0, table_ref, shard, shards
+            voltage_ref[...], current_ref[...], fires[0:1], 0, table_out, lax.axis_index("len"), shards
         )
         solved_ref[...] = solved[:nodes]
         sums_ref[...] = solved[nodes:]
-
+        for copy in copies[len(small):]:
+            copy.wait()
+        brick, spot = home_ref[...], cell_ref[...]
+        row = (brick // emg) * rows + spot // depth
+        column = (brick % emg) * depth + spot % depth
+        line = iota((SUB, fibres), 0)
+        out = jnp.where(line == 0, row.astype(jnp.float32), column.astype(jnp.float32))
+        misc_ref[...] = jnp.where(line == 2, fires, out)
+
+    args = (*small, *large, states)
     return kernel_call(
         body,
-        [(count, nodes, fibres), (nodes, fibres), (nodes, fibres), (SUB, fibres)],
-        states, voltage, big, param, misc, table,
-    )
-
-
-def coupled_all(states, big):
-    def body(states_ref, big_ref, out_ref):
-        big = big_ref[...]
-        for start in range(0, states.shape[1], 2 * SUB):
-            one, two = pl.ds(start, SUB), pl.ds(start + SUB, SUB)
-            out_ref[:, one, :], out_ref[:, two, :] = coupled(
-                big, states_ref[:, one, :], states_ref[:, two, :]
-            )
-
-    return kernel_call(body, [states.shape], states, big)[0]
+        [(nodes, tall, fibres), (nodes, fibres), (nodes, fibres), (SUB, fibres),
+         ((tall, 3 * tall), jnp.bfloat16), (3, tall, fibres), (SUB, fibres),
+         tables[0].shape, tissue.shape, *(t.shape for t in tables[1:])],
+        *args,
+        hbm_ins=range(len(args)),
+        scratch=[
+            *(pltpu.VMEM(a.shape, a.dtype) for a in small[:-1]),
+            pltpu.VMEM(home.shape, home.dtype),
+            pltpu.VMEM(cell.shape, cell.dtype),
+            pltpu.VMEM((nodes, tall, fibres), jnp.float32),
+            pltpu.SemaphoreType.DMA((count + nodes // chunk,)),
+        ],
+    )
+
+
+def coupled_all(states, triple):
+    nodes = states.shape[0]
+
+    def body(states_ref, triple_ref, out_ref):
+        triple = triple_ref[...]
+        for start in range(0, nodes, SUB):
+            drives = coupled(triple, [states_ref[n] for n in range(start, start + SUB)])
+            for n, drive in zip(range(start, start + SUB), drives):
+                out_ref[n] = drive
+
+    return kernel_call(body, [states.shape], states, triple)[0]
 
 
 def second_step(states, drive, solved, current, param, misc, table, rise, fall, near):
-    count, nodes, fibres = states.shape
+    nodes, tall, fibres = states.shape
     cells = nodes // NPC
     shards = len(near)
 
@@ -275,13 +269,10 @@
             rise_ref, fall_ref, SUB + shard * nodes, nodes, below, above
         )
         line_ref[0:nodes, :] = current_ref[...]
-        for start in range(0, nodes, SUB):
-            here = pl.ds(start, SUB)
-            values, flow = advanced(
-                states_ref[:, here, :], drive_ref[:, here, :], param_ref, volt_ref[here, :]
+        for n in range(nodes):
+            states_out[n], line_ref[nodes + n:nodes + n + 1, :] = advanced(
+                states_ref[n], drive_ref[n], param_ref, volt_ref[n:n + 1, :]
             )
-            states_out[:, here, :] = values
-            line_ref[nodes + start:nodes + start + SUB, :] = flow
         binned = line_ref[pl.ds(0, STEPS * cells, stride=NPC), :]
         for k in range(1, NPC):
             binned = binned + line_ref[pl.ds(k, STEPS * cells, stride=NPC), :]
@@ -303,7 +294,7 @@
     edge = (SUB + STEPS * EDGE, fibres)
     return kernel_call(
         body,
-        [(count, nodes, fibres), (nodes, fibres), (STEPS * cells, fibres), (SUB, fibres)]
+        [states.shape, (nodes, fibres), (STEPS * cells, fibres), (SUB, fibres)]
         + [edge] * len(facing(shards)),
         states, drive, solved, current, param, misc, table, rise, fall, *near,
         scratch=[
@@ -346,14 +337,12 @@
     )
 
 
-def finished(states, solved, rise, fall, near):
+def last_voltage(solved, rise, fall, near):
     nodes, fibres = solved.shape
     shards = len(near)
 
-    def body(states_ref, solved_ref, rise_ref, fall_ref, *rest):
-        near_refs, (states_out, voltage_out, volt_ref, sems) = rest[:shards], rest[shards:]
-        move = pltpu.make_async_copy(states_ref, states_out, sems.at[0])
-        move.start()
+    def body(solved_ref, rise_ref, fall_ref, *rest):
+        near_refs, (voltage_out, volt_ref, sem) = rest[:shards], rest[shards:]
         shard = lax.axis_index("len")
         rows = [ref[0:SUB, :] for ref in near_refs]
         owners = [jnp.bitwise_xor(shard, k) for k in range(shards)]
@@ -361,18 +350,17 @@
         volt_ref[...] = solved_ref[...] + from_far(
             rise_ref, fall_ref, SUB + shard * nodes, nodes, below, above
         )
-        place = pltpu.make_async_copy(volt_ref, voltage_out, sems.at[1])
-        place.start()
+        move = pltpu.make_async_copy(volt_ref, voltage_out, sem)
+        move.start()
         move.wait()
-        place.wait()
 
     return kernel_call(
         body,
-        [states.shape, (nodes, fibres)],
-        states, solved, rise, fall, *near,
-        hbm_outs=(0, 1),
-        scratch=[pltpu.VMEM((nodes, fibres), jnp.float32), pltpu.SemaphoreType.DMA((2,))],
-    )
+        [(nodes, fibres)],
+        solved, rise, fall, *near,
+        hbm_outs=(0,),
+        scratch=[pltpu.VMEM((nodes, fibres), jnp.float32), pltpu.SemaphoreType.DMA],
+    )[0]
 
 
 def facing(count):
@@ -435,6 +423,11 @@
     return kernel_call(body, [(rows * long, depth), (long, depth)], tissue, *near)
 
 
+def halo_lanes(place, depth):
+    upper = jnp.where(place < depth + depth // 2, depth - 1 - place, 3 * depth - 1 - place)
+    return jnp.where(place < depth, place, upper)
+
+
 def operator_terms(sizes, wide, blocks, rows):
     shards, fib, emg = sizes
     long = wide.shape[0] // rows
@@ -475,17 +468,17 @@
             side = jnp.zeros((long, depth), jnp.float32)
             if -2 < y < rows + 1:
                 before, after = under if y < 0 else over if y >= rows else own
-                k = y % rows
-                after = pltpu.roll(after, depth - 8 * k, 1) if k else after
-                before = pltpu.roll(before, depth - 4 - 8 * k, 1)
-                side = jnp.where(spot < 2, after, jnp.where(spot >= depth - 2, before, side))
+                k = 8 * (y % rows)
+                for to, source, lane in (
+                    (0, before, k + 3), (1, before, k + 2), (depth - 1, after, k), (depth - 2, after, k + 1)
+                ):
+                    side = jnp.where(spot == to, pltpu.roll(source, (to - lane) % depth, 1), side)
             whole = jnp.concatenate([main, side], axis=1) + (6.0 - middle)
             base = (y + 2) * tall
             for step in range(STEPS):
                 diag_ref[base + step * long:base + (step + 1) * long, :] = whole
         x = lax.rem(iota((tall, lanes), 0), long) - EDGE + shard * cells
-        z = iota((tall, lanes), 1)
-        z = jnp.where(z < lanes - depth // 2, z, z - lanes) + place * depth
+        z = halo_lanes(iota((tall, lanes), 1), depth) + place * depth
         mask_ref[...] = (
             (x >= 0) & (x < shards * cells) & (z >= 0) & (z < emg * depth)
         ).astype(jnp.float32)
@@ -497,23 +490,19 @@
     )
 
 
-def potentials(fib, got, diag, mask, rows):
-    tall, lanes = mask.shape
+def sources(sizes, got, rows, earlier=()):
+    tall, depth = sizes
+    lanes = 2 * depth
     fibres = got[0].shape[1]
     groups = len(got)
     long = tall // STEPS
-    depth = lanes // 2
-    cells = long - 2 * EDGE
     slabs = rows + 2 * REACH
-    coefs = polynomial()
-    scale = [c / coefs[-1] for c in coefs]
+    wide_k = groups * fibres
 
     def body(*refs):
-        got_refs = refs[:groups]
-        diag_ref, mask_ref, out_ref, hot_ref, left_ref, src_ref, one_ref, two_ref = refs[groups:]
+        got_refs, (*add_refs, out_ref, hot_ref, left_ref) = refs[:groups], refs[groups:]
         mine, place = lax.axis_index("fib"), lax.axis_index("emg")
-        lane = iota((lanes, fibres), 0)
-        lane = jnp.where(lane < lanes - depth // 2, lane, lane - lanes)
+        lane = halo_lanes(iota((lanes, fibres), 0), depth)
         lane = jnp.where((lane >= -REACH) & (lane < depth + REACH), lane, -lanes)
         for g, got_ref in enumerate(got_refs):
             column = got_ref[long - 1:long, :].astype(jnp.int32) - place * depth
@@ -526,55 +515,121 @@
         product = dot_nt(left_ref[...], hot_ref[...])
         for y in range(slabs):
             base = y * 2 * tall
-            src_ref[y * tall:(y + 1) * tall, :] = (
-                product[base:base + tall] + product[base + tall:base + 2 * tall]
+            here = slice(y * tall, (y + 1) * tall)
+            out = product[base:base + tall] + product[base + tall:base + 2 * tall]
+            for ref in add_refs:
+                out = out + ref[here, :]
+            out_ref[here, :] = out
+
+    return kernel_call(
+        body,
+        [(slabs * tall, lanes)],
+        *got, *earlier,
+        limit=(12 << 20) + slabs * 2 * tall * wide_k * 2,
+        scratch=[
+            pltpu.VMEM((lanes, wide_k), jnp.bfloat16),
+            pltpu.VMEM((slabs * 2 * tall, wide_k), jnp.bfloat16),
+        ],
+    )
+
+
+def potentials(fib, source, diag, mask, rows, number, states):
+    tall, lanes = mask.shape
+    long = tall // STEPS
+    depth = lanes // 2
+    cells = long - 2 * EDGE
+    slabs = rows + 2 * REACH
+    coefs = polynomial()
+    scale = [c / coefs[-1] for c in coefs]
+
+    def body(src_ref, diag_ref, mask_ref, states_ref, out_ref, states_out, one_ref, two_ref, stage_ref, sems):
+        for i in range(number):
+            pltpu.make_async_copy(states_ref.at[:, i, :], states_out.at[i], sems.at[STEPS]).start()
+        mine = lax.axis_index("fib")
+        brick, halo = slice(0, depth), slice(depth, lanes)
+        gap = iota((depth, depth), 0) - iota((depth, depth), 1)
+        near = ((gap == 1) | (gap == -1)).astype(jnp.float32).astype(jnp.bfloat16)
+        near = jnp.concatenate([near, near], axis=0)
+        lane = iota((tall, depth), 1)
+        low, high = lane == 0, lane == depth - 1
+        ends = (low | high).astype(jnp.float32)
+
+        def sweep(ref, y, constant, part, along, begin=0, end=tall):
+            here = lambda ref, y: ref[y * tall + begin:y * tall + end, part]
+            size = end - begin
+            centre = here(ref, y + REACH)
+            beside = here(ref, y + REACH - 1) + here(ref, y + REACH + 1) + along
+            beside = beside + pltpu.roll(centre, 1, 0) + pltpu.roll(centre, size - 1, 0)
+            return here(diag_ref, y + 2) * centre - beside + constant * here(src_ref, y + REACH)
+
+        def along_brick(ref, y, begin=0, end=tall):
+            here = slice((y + REACH) * tall + begin, (y + REACH) * tall + end)
+            inner, outer = ref[here, brick], ref[here, halo]
+            size = end - begin
+            return jnp.where(low[:size], outer, pltpu.roll(inner, 1, 1)) + jnp.where(
+                high[:size], outer, pltpu.roll(inner, depth - 1, 1)
             )
 
-        def sweep(ref, y, constant):
-            here = lambda k: ref[(k + REACH) * tall:(k + REACH + 1) * tall, :]
-            centre = here(y)
-            beside = here(y - 1) + here(y + 1)
-            beside = beside + pltpu.roll(centre, 1, 0) + pltpu.roll(centre, tall - 1, 0)
-            beside = beside + pltpu.roll(centre, 1, 1) + pltpu.roll(centre, lanes - 1, 1)
-            diag = diag_ref[(y + 2) * tall:(y + 3) * tall, :]
-            source = src_ref[(y + REACH) * tall:(y + REACH + 1) * tall, :]
-            return diag * centre - beside + constant * source
+        def domain(value, part):
+            pieces, at = [], 0
+            for step in range(STEPS):
+                base = step * long
+                for begin, end in ((base, base + EDGE), (base + long - EDGE, base + long)):
+                    begin, end = begin // SUB * SUB, -(-end // SUB) * SUB
+                    begin = max(begin, at)
+                    pieces += [value[at:begin]] if begin > at else []
+                    pieces += [value[begin:end] * mask_ref[begin:end, part]] if end > begin else []
+                    at = max(at, end)
+            return jnp.concatenate(pieces + ([value[at:]] if at < tall else []), axis=0)
 
         for k, (source, target) in enumerate(((src_ref, one_ref), (one_ref, two_ref))):
             reach = REACH - 1 - k
+            outer = source[(REACH - reach) * tall:(rows + reach + REACH) * tall, halo]
+            outer = jnp.dot(
+                jnp.concatenate(split(outer), axis=1), near, preferred_element_type=jnp.float32
+            )
             for y in range(-reach, rows + reach):
-                value = sweep(source, y, scale[2 - k]) * mask_ref[...]
-                if y < 0:
-                    value = value * (mine > 0).astype(jnp.float32)
-                if y >= rows:
-                    value = value * (mine < fib - 1).astype(jnp.float32)
-                target[(y + REACH) * tall:(y + REACH + 1) * tall, :] = value
-        for y in range(rows):
-            value = sweep(two_ref, y, scale[0])[:, :depth] * coefs[-1]
-            for step in range(STEPS):
-                begin = step * long + EDGE
-                out_ref[pl.ds(step * cells * rows + y, cells, stride=rows), :] = value[
-                    begin:begin + cells
-                ]
-
-    f32, b16 = jnp.float32, jnp.bfloat16
-    wide_k = groups * fibres
-    return pl.pallas_call(
+                here = slice((y + REACH) * tall, (y + REACH + 1) * tall)
+                along = outer[(y + reach) * tall:(y + reach + 1) * tall] + ends * source[here, brick]
+                inner = sweep(source, y, scale[2 - k], brick, along_brick(source, y))
+                inner = domain(inner, brick)
+                along = sweep(source, y, scale[2 - k], halo, along) * mask_ref[:, halo]
+                if y < 0 or y >= rows:
+                    keep = (mine > 0 if y < 0 else mine < fib - 1).astype(jnp.float32)
+                    inner, along = inner * keep, along * keep
+                target[here, brick] = inner
+                target[here, halo] = along
+        size = cells * rows
+        copies = []
+        for step in range(STEPS):
+            begin, end = step * long, (step + 1) * long
+            for y in range(rows):
+                value = sweep(
+                    two_ref, y, scale[0], brick, along_brick(two_ref, y, begin, end), begin, end
+                )
+                stage_ref[pl.ds(step * size + y, cells, stride=rows), :] = (
+                    value[EDGE:EDGE + cells] * coefs[-1]
+                )
+            here = pl.ds(step * size, size)
+            copies.append(pltpu.make_async_copy(stage_ref.at[here], out_ref.at[here], sems.at[step]))
+            copies[-1].start()
+        copies.append(pltpu.make_async_copy(states_out, states_out, sems.at[STEPS]))
+        for copy in copies:
+            copy.wait()
+
+    scratch = pltpu.VMEM((slabs * tall, lanes), jnp.float32)
+    return kernel_call(
         body,
-        out_shape=jax.ShapeDtypeStruct((STEPS * cells * rows, depth), f32),
-        in_specs=[VMEM] * (groups + 2),
-        out_specs=VMEM,
-        scratch_shapes=[
-            pltpu.VMEM((lanes, wide_k), b16),
-            pltpu.VMEM((slabs * 2 * tall, wide_k), b16),
-            pltpu.VMEM((slabs * tall, lanes), f32),
-            pltpu.VMEM((slabs * tall, lanes), f32),
-            pltpu.VMEM((slabs * tall, lanes), f32),
+        [(STEPS * cells * rows, depth), (number, states.shape[0], states.shape[2])],
+        source, diag, mask, states,
+        hbm_outs=(0, 1),
+        scratch=[
+            scratch,
+            scratch,
+            pltpu.VMEM((STEPS * cells * rows, depth), jnp.float32),
+            pltpu.SemaphoreType.DMA((STEPS + 1,)),
         ],
-        compiler_params=pltpu.CompilerParams(
-            vmem_limit_bytes=(20 << 20) + slabs * 2 * tall * wide_k * 2
-        ),
-    )(*(pltpu.with_memory_space_constraint(a, pltpu.VMEM) for a in (*got, diag, mask)))
+    )
 
 
 def xor_swap(value, axis, k):
@@ -603,32 +658,35 @@
     count, nodes, fibres = states.shape
     cells, rows, depth = tissue.shape
     shards, fib, emg = (lax.axis_size(a) for a in ("len", "fib", "emg"))
-    groups = fib * emg
     line = lambda v: v.reshape(1, v.size)
     tables = [jnp.asarray(t) for t in cable_tables(nodes * shards, shards)]
-    (big, param, misc), kept = prepare(
-        states, voltage, tissue.reshape(cells * rows, depth), tables,
+    states, solved, current, sums, triple, param, misc, table, flat, rise, fall = first_step(
+        (shards, emg, rows, depth), states, voltage, tissue.reshape(cells * rows, depth), tables,
         coupling, line(decay_rates), line(volt_gain), line(current_weights),
-        line(motor_unit), line(stim_step), line(fibre_home), line(cross_cell), emg, rows, depth,
-    )
-    states, voltage, flat, table, rise, fall = kept
-    states, solved, current, sums = first_step(shards, states, voltage, big, param, misc, table)
+        line(motor_unit), line(stim_step), line(fibre_home), line(cross_cell),
+    )
     near = swaps("len", sums, with_faces(shards, sums, flat, rows))
-    drive = coupled_all(states, big)
+    drive = coupled_all(states, triple)
     states, solved, flows, sums, *faces = second_step(
         states, drive, solved, current, param, misc, table, rise, fall, near
     )
     wide, ends = widened(flat, near, rows)
     near = swaps("len", sums, faces)
+    near, wide, ends = lax.optimization_barrier((near, wide, ends))
     send, with_ends, *with_layers = packed(fib, flows, misc, near, wide, ends, rows)
     blocks = {(k, 0): block for k, block in enumerate(swaps("fib", send, with_layers))}
     across = swaps("emg", send, [with_ends] * len(facing(emg)))
     for m in range(1, emg):
         for k, block in enumerate(swaps("fib", across[m], [across[m]] * len(facing(fib)))):
             blocks[k, m] = block
-    states, voltage = finished(states, solved, rise, fall, near)
+    tall = STEPS * (cells + 2 * EDGE)
+    keys = sorted(blocks)
+    early = [blocks[key] for key in keys if not all(key)]
+    source = sources((tall, depth), early, rows)
+    source = sources((tall, depth), [blocks[key] for key in keys if all(key)], rows, source)[0]
+    voltage = last_voltage(solved, rise, fall, near)
     diag, mask = operator_terms((shards, fib, emg), wide, blocks, rows)
-    potential = potentials(fib, [blocks[key] for key in sorted(blocks)], diag, mask, rows)
+    potential, states = potentials(fib, source, diag, mask, rows, count, states)
     return states, voltage, potential.reshape(STEPS, cells, rows, depth)
 
 

time: 36.3 us -> 32.8 us (0.904)
  Pallas kernels: 12.6 us -> 9.8 us
  waiting for transfers between devices: 8.39 us -> 7.11 us
  starting transfers between devices: 14.3 us -> 15 us
    pallas_call x1 -> x0, Pallas kernels: 3.53 us -> none  [potentials(): pl.pallas_call(body, out_shape=jax.ShapeDtypeStruct((STEPS * cells * rows...]
    ppermute x13, waiting for transfers between devices: 8.39 us -> 7.11 us  [xor_swap(): lax.ppermute(value, axis, [(i, i ^ k) for i in range(lax.axis_size(axis))])]
    pallas_call x9 -> x11, Pallas kernels: 9.11 us -> 9.8 us  [kernel_call(): pl.pallas_call(body, out_shape=shapes, in_specs=[HBM if i in hbm_ins else...]
    ppermute x13, starting transfers between devices: 14.3 us -> 15 us  [xor_swap(): lax.ppermute(value, axis, [(i, i ^ k) for i in range(lax.axis_size(axis))])]
  transfers between devices with their start and end apart: 13 -> 13, of which waited for: 5 -> 7; matrix products, arithmetic and copies ran while one was open for 0% -> 0% of each run, Pallas kernels for 9% -> 9%
where the time goes in v2:
time: 32.8 us; the launch traced here: 32.7 us
  starting transfers between devices  15 us (46%)
  Pallas kernels  9.8 us (30%)
  waiting for transfers between devices  7.11 us (22%)
  between operations  0.74 us (2%)
    ppermute x13, starting transfers between devices, xor_swap(): lax.ppermute(value, axis, [(i, i ^ k) for i in range(lax.axis_size(axis))])  15 us
    pallas_call x11, Pallas kernels, kernel_call(): pl.pallas_call(body, out_shape=shapes, in_specs=[HBM if i in hbm_ins else...  9.8 us
    ppermute x13, waiting for transfers between devices, xor_swap(): lax.ppermute(value, axis, [(i, i ^ k) for i in range(lax.axis_size(axis))])  7.11 us
  transfers between devices with their start and end apart: 13, of which 7 were waited for; matrix products, arithmetic and copies ran while one was open for 0% of the time, Pallas kernels for 9%

profile of v2, /device:TPU:0, one launch (start us, length us, event | category | flops | bytes accessed | tf_op | source)
XLA Modules:
  0.0 32.7 jit_solution(13492709521870397121)
XLA Ops:
  0.6 3.0 %shard_map.157 = (f32[64,64,128]{2,1,0:T(8,128)S(1)}, f32[64,128]{1,0:T(8,128)S(1)}, f32[64,128]{1,0:T(8,128)S(1)}, f32[8,128]{1,0:T(8,128)S(1)}, bf16[64,192]{1...) custom-call(f32[57,57]{1,0:T(8,128)} %refs_0_.1, ...), custom_call_target="tpu_custom_call" | custom-call | tf_op jit(solution)/shard_map/pallas_call | solution.py:43
  3.6 0.5 %collective-permute-start = (f32[24,128]{1,0:T(8,128)S(1)}, f32[24,128]{1,0:T(8,128)S(1)}, u32[]{:S(2)}, u32[]{:S(2)}) collective-permute-start(f32[24,128]{1,0:T(8,128)S(1)} %get-tuple-element.48), channel_id=1, source_target_pairs={{0,4},{4,0},{8,12},{12,8},{1,5},{5,1},{9,13},{13,9},{2,6},{6,2},{1... | collective-permute-start | bytes 36872 | tf_op jit(solution)/shard_map/ppermute | solution.py:636
  4.1 2.6 %collective-permute-start.2 = (f32[24,128]{1,0:T(8,128)S(1)}, f32[24,128]{1,0:T(8,128)S(1)}, u32[]{:S(2)}, u32[]{:S(2)}) collective-permute-start(f32[24,128]{1,0:T(8,128)S(1)} %get-tuple-element.49), channel_id=1, source_target_pairs={{0,12},{4,8},{8,4},{12,0},{1,13},{5,9},{9,5},{13,1},{2,14},{6,10},... | collective-permute-start | bytes 36872 | tf_op jit(solution)/shard_map/ppermute | solution.py:636
  6.7 0.0 collective-permute-start.1
  6.8 0.7 %shard_map.158.drive_ref = f32[64,64,128]{2,1,0:T(8,128)S(1)} custom-call(f32[64,64,128]{2,1,0:T(8,128)S(1)} %get-tuple-element.37.states_ref, bf16[64,192]{1,0:T(8,128)(2,1)S(1)} %get-tuple-element.38.triple_ref), custom_call_target="tpu_custom_call" | custom-call | tf_op jit(solution)/shard_map/pallas_call | solution.py:43
  7.5 2.9 %collective-permute-done.1.rest_2_ = f32[8,128]{1,0:T(8,128)S(1)} collective-permute-done((f32[8,128]{1,0:T(8,128)S(1)}, f32[8,128]{1,0:T(8,128)S(1)}, u32[]{:S(2)}, u32[]{:S(2)}) %collective-permute-start.1) | collective-permute-done | bytes 4128 | tf_op jit(solution)/shard_map/ppermute | solution.py:636
  10.4 0.0 collective-permute-done.rest_1_
  10.4 0.0 collective-permute-done.2.rest_3_
  10.4 0.9 %shard_map.160 = (f32[64,64,128]{2,1,0:T(8,128)S(1)}, f32[64,128]{1,0:T(8,128)S(1)}, f32[64,128]{1,0:T(8,128)S(1)}, f32[8,128]{1,0:T(8,128)S(1)}, f32[16,128]{1,0:T(8,128)S(1)}, /*index=5*/f32[16,128]{1,0:T(8,128)S(1)}) custom-call(f32[64,64,128]{2,1,0:T(8,128)S(1)} %get-tuple-element.37.states_ref, f32[64,64,128]{2,1,0:T(8,128)S(1)} %shard_map.158.drive_ref, ...), custom_call_target="tpu_custom_call" | custom-call | tf_op jit(solution)/shard_map/pallas_call | solution.py:43
  11.3 0.1 collective-permute-start.3
  11.3 0.2 collective-permute-start.5
  11.6 1.9 %collective-permute-start.4 = (f32[8,128]{1,0:T(8,128)S(1)}, f32[8,128]{1,0:T(8,128)S(1)}, u32[]{:S(2)}, u32[]{:S(2)}) collective-permute-start(f32[8,128]{1,0:T(8,128)S(1)} %get-tuple-element.58.rest_0_), channel_id=1, source_target_pairs={{0,8},{4,12},{8,0},{12,4},{1,9},{5,13},{9,1},{13,5},{2,10},{6,14},... | collective-permute-start | bytes 12296 | tf_op jit(solution)/shard_map/ppermute | solution.py:636
  13.5 0.2 shard_map.161
  13.6 1.5 %collective-permute-done.4.rest_2_ = f32[8,128]{1,0:T(8,128)S(1)} collective-permute-done((f32[8,128]{1,0:T(8,128)S(1)}, f32[8,128]{1,0:T(8,128)S(1)}, u32[]{:S(2)}, u32[]{:S(2)}) %collective-permute-start.4) | collective-permute-done | bytes 4128 | tf_op jit(solution)/shard_map/ppermute | solution.py:636
  15.2 0.0 collective-permute-done.3.rest_1_
  15.2 0.0 collective-permute-done.5.rest_3_
  15.2 4.1 %collective-permute-start.10 = (f32[120,128]{1,0:T(8,128)S(1)}, f32[120,128]{1,0:T(8,128)S(1)}, u32[]{:S(2)}, u32[]{:S(2)}) collective-permute-start(f32[120,128]{1,0:T(8,128)S(1)} %get-tuple-element.62), channel_id=1, source_target_pairs={{0,3},{1,2},{2,1},{3,0},{4,7},{5,6},{6,5},{7,4},{8,11},{9,10},{10,... | collective-permute-start | bytes 184328 | tf_op jit(solution)/shard_map/ppermute | solution.py:636
  19.3 0.0 collective-permute-start.6
  19.3 1.5 %collective-permute-start.12 = (f32[160,128]{1,0:T(8,128)S(1)}, f32[160,128]{1,0:T(8,128)S(1)}, u32[]{:S(2)}, u32[]{:S(2)}) collective-permute-start(f32[160,128]{1,0:T(8,128)S(1)} %get-tuple-element.64), channel_id=1, source_target_pairs={{0,16},{16,0},{1,17},{17,1},{2,18},{18,2},{3,19},{19,3},{4,20},{20... | collective-permute-start | bytes 245768 | tf_op jit(solution)/shard_map/ppermute | solution.py:636
  20.8 0.8 %collective-permute-start.8 = (f32[80,128]{1,0:T(8,128)S(1)}, f32[80,128]{1,0:T(8,128)S(1)}, u32[]{:S(2)}, u32[]{:S(2)}) collective-permute-start(f32[80,128]{1,0:T(8,128)S(1)} %get-tuple-element.63.refs_0_), channel_id=1, source_target_pairs={{0,2},{1,3},{2,0},{3,1},{4,6},{5,7},{6,4},{7,5},{8,10},{9,11},{10,... | collective-permute-start | bytes 122888 | tf_op jit(solution)/shard_map/ppermute | solution.py:636
  21.6 0.1 collective-permute-done.10.refs_3_.refs_1_
  21.7 1.7 %collective-permute-start.11 = (f32[120,128]{1,0:T(8,128)S(1)}, f32[120,128]{1,0:T(8,128)S(1)}, u32[]{:S(2)}, u32[]{:S(2)}) collective-permute-start(f32[120,128]{1,0:T(8,128)S(1)} %collective-permute-done.10.refs_3_.refs_1_), channel_id=1, source_target_pairs={{0,16},{16,0},{1,17},{17,1},{2,18},{18,2},{3,19},{19,3},{4,20},{20... | collective-permute-start | bytes 184328 | tf_op jit(solution)/shard_map/ppermute | solution.py:636
  23.3 0.6 %collective-permute-done.6.refs_1_.refs_0_ = f32[120,128]{1,0:T(8,128)S(1)} collective-permute-done((f32[120,128]{1,0:T(8,128)S(1)}, f32[120,128]{1,0:T(8,128)S(1)}, u32[]{:S(2)}, u32[]{:S(2)}) %collective-permute-start.6) | collective-permute-done | bytes 61472 | tf_op jit(solution)/shard_map/ppermute | solution.py:636
  24.0 1.1 %collective-permute-start.7 = (f32[120,128]{1,0:T(8,128)S(1)}, f32[120,128]{1,0:T(8,128)S(1)}, u32[]{:S(2)}, u32[]{:S(2)}) collective-permute-start(f32[120,128]{1,0:T(8,128)S(1)} %collective-permute-done.6.refs_1_.refs_0_), channel_id=1, source_target_pairs={{0,16},{16,0},{1,17},{17,1},{2,18},{18,2},{3,19},{19,3},{4,20},{20... | collective-permute-start | bytes 184328 | tf_op jit(solution)/shard_map/ppermute | solution.py:636
  25.0 0.7 %collective-permute-done.8.refs_2_ = f32[80,128]{1,0:T(8,128)S(1)} collective-permute-done((f32[80,128]{1,0:T(8,128)S(1)}, f32[80,128]{1,0:T(8,128)S(1)}, u32[]{:S(2)}, u32[]{:S(2)}) %collective-permute-start.8) | collective-permute-done | bytes 40992 | tf_op jit(solution)/shard_map/ppermute | solution.py:636
  25.7 0.5 %collective-permute-start.9 = (f32[80,128]{1,0:T(8,128)S(1)}, f32[80,128]{1,0:T(8,128)S(1)}, u32[]{:S(2)}, u32[]{:S(2)}) collective-permute-start(f32[80,128]{1,0:T(8,128)S(1)} %collective-permute-done.8.refs_2_), channel_id=1, source_target_pairs={{0,16},{16,0},{1,17},{17,1},{2,18},{18,2},{3,19},{19,3},{4,20},{20... | collective-permute-start | bytes 122888 | tf_op jit(solution)/shard_map/ppermute | solution.py:636
  26.2 0.6 %shard_map.167 = f32[64,128]{1,0:T(8,128)} custom-call(f32[64,128]{1,0:T(8,128)S(1)} %get-tuple-element.69.solved_ref, f32[272,128]{1,0:T(8,128)S(1)} %get-tuple-element.44.rise_ref, f32[272,128]{1,0:T(8,128)S(1)} %get-tuple-element.45.fall_ref, f32[8,128]{1,0:T(8,128)S(1)} %get-tuple-element.58.rest_0_, f32[16,128]{1,0:T(8,128)S(1)} %collective-permute-done.3.rest_1_, ...), custom_call_target="tpu_custom_call" | custom-call | tf_op jit(solution)/shard_map/pallas_call | solution.py:43
  26.9 0.0 collective-permute-done.12.refs_4_.refs_2_
  26.9 1.2 %shard_map.163.refs_3_ = f32[1120,256]{1,0:T(8,128)S(1)} custom-call(f32[80,128]{1,0:T(8,128)S(1)} %get-tuple-element.63.refs_0_, f32[120,128]{1,0:T(8,128)S(1)} %collective-permute-done.6.refs_1_.refs_0_, f32[80,128]{1,0:T(8,128)S(1)} %collective-permute-done.8.refs_2_, f32[120,128]{1,0:T(8,128)S(1)} %collective-permute-done.10.refs_3_.refs_1_, ...), custom_call_target="tpu_custom_call" | custom-call | tf_op jit(solution)/shard_map/pallas_call | solution.py:43
  28.1 0.0 collective-permute-done.11.refs_2_.refs_4_
  28.1 0.1 collective-permute-done.7.refs_0_.refs_3_
  28.2 0.3 shard_map.165
  28.5 1.2 %collective-permute-done.9.refs_1_ = f32[80,128]{1,0:T(8,128)S(1)} collective-permute-done((f32[80,128]{1,0:T(8,128)S(1)}, f32[80,128]{1,0:T(8,128)S(1)}, u32[]{:S(2)}, u32[]{:S(2)}) %collective-permute-start.9) | collective-permute-done | bytes 40992 | tf_op jit(solution)/shard_map/ppermute | solution.py:636
  29.7 0.8 %shard_map.164.src_ref = f32[1120,256]{1,0:T(8,128)S(1)} custom-call(f32[120,128]{1,0:T(8,128)S(1)} %collective-permute-done.7.refs_0_.refs_3_, f32[80,128]{1,0:T(8,128)S(1)} %collective-permute-done.9.refs_1_, f32[120,128]{1,0:T(8,128)S(1)} %collective-permute-done.11.refs_2_.refs_4_, f32[1120,256]{1,0:T(8,128)S(1)} %shard_map.163.refs_3_), custom_call_target="tpu_custom_call" | custom-call | tf_op jit(solution)/shard_map/pallas_call | solution.py:43
  30.5 2.1 %shard_map.166 = (f32[512,128]{1,0:T(8,128)}, f32[57,64,128]{2,1,0:T(8,128)}) custom-call(f32[1120,256]{1,0:T(8,128)S(1)} %shard_map.164.src_ref, f32[960,256]{1,0:T(8,128)S(1)} %get-tuple-element.65.diag_ref, f32[80,256]{1,0:T(8,128)S(1)} %get-tuple-element.66.mask_ref, f32[64,64,128]{2,1,0:T(8,128)S(1)} %get-tuple-element.67.states_ref), custom_call_target="tpu_custom_call" | custom-call | tf_op jit(solution)/shard_map/pallas_call | solution.py:43
  (2 shorter events, 0.0 us)
Async XLA Ops:
  3.6 6.7 %collective-permute-start = (f32[24,128]{1,0:T(8,128)S(1)}, f32[24,128]{1,0:T(8,128)S(1)}, u32[]{:S(2)}, u32[]{:S(2)}) collective-permute-start(f32[24,128]{1,0:T(8,128)S(1)} %get-tuple-element.48), channel_id=1, source_target_pairs={{0,4},{4,0},{8,12},{12,8},{1,5},{5,1},{9,13},{13,9},{2,6},{6,2},{1... | collective-permute-start | bytes 36872 | tf_op jit(solution)/shard_map/ppermute | solution.py:636
  4.1 6.2 %collective-permute-start.2 = (f32[24,128]{1,0:T(8,128)S(1)}, f32[24,128]{1,0:T(8,128)S(1)}, u32[]{:S(2)}, u32[]{:S(2)}) collective-permute-start(f32[24,128]{1,0:T(8,128)S(1)} %get-tuple-element.49), channel_id=1, source_target_pairs={{0,12},{4,8},{8,4},{12,0},{1,13},{5,9},{9,5},{13,1},{2,14},{6,10},... | collective-permute-start | bytes 36872 | tf_op jit(solution)/shard_map/ppermute | solution.py:636
  6.7 3.6 %collective-permute-start.1 = (f32[8,128]{1,0:T(8,128)S(1)}, f32[8,128]{1,0:T(8,128)S(1)}, u32[]{:S(2)}, u32[]{:S(2)}) collective-permute-start(f32[8,128]{1,0:T(8,128)S(1)} %get-tuple-element.46.sums_ref.rest_0_), channel_id=1, source_target_pairs={{0,8},{4,12},{8,0},{12,4},{1,9},{5,13},{9,1},{13,5},{2,10},{6,14},... | collective-permute-start | bytes 12296 | tf_op jit(solution)/shard_map/ppermute | solution.py:636
  11.3 3.9 %collective-permute-start.3 = (f32[16,128]{1,0:T(8,128)S(1)}, f32[16,128]{1,0:T(8,128)S(1)}, u32[]{:S(2)}, u32[]{:S(2)}) collective-permute-start(f32[16,128]{1,0:T(8,128)S(1)} %get-tuple-element.52), channel_id=1, source_target_pairs={{0,4},{4,0},{8,12},{12,8},{1,5},{5,1},{9,13},{13,9},{2,6},{6,2},{1... | collective-permute-start | bytes 24584 | tf_op jit(solution)/shard_map/ppermute | solution.py:636
  11.3 3.9 %collective-permute-start.5 = (f32[16,128]{1,0:T(8,128)S(1)}, f32[16,128]{1,0:T(8,128)S(1)}, u32[]{:S(2)}, u32[]{:S(2)}) collective-permute-start(f32[16,128]{1,0:T(8,128)S(1)} %get-tuple-element.53), channel_id=1, source_target_pairs={{0,12},{4,8},{8,4},{12,0},{1,13},{5,9},{9,5},{13,1},{2,14},{6,10},... | collective-permute-start | bytes 24584 | tf_op jit(solution)/shard_map/ppermute | solution.py:636
  11.6 3.6 %collective-permute-start.4 = (f32[8,128]{1,0:T(8,128)S(1)}, f32[8,128]{1,0:T(8,128)S(1)}, u32[]{:S(2)}, u32[]{:S(2)}) collective-permute-start(f32[8,128]{1,0:T(8,128)S(1)} %get-tuple-element.58.rest_0_), channel_id=1, source_target_pairs={{0,8},{4,12},{8,0},{12,4},{1,9},{5,13},{9,1},{13,5},{2,10},{6,14},... | collective-permute-start | bytes 12296 | tf_op jit(solution)/shard_map/ppermute | solution.py:636
  15.2 6.5 %collective-permute-start.10 = (f32[120,128]{1,0:T(8,128)S(1)}, f32[120,128]{1,0:T(8,128)S(1)}, u32[]{:S(2)}, u32[]{:S(2)}) collective-permute-start(f32[120,128]{1,0:T(8,128)S(1)} %get-tuple-element.62), channel_id=1, source_target_pairs={{0,3},{1,2},{2,1},{3,0},{4,7},{5,6},{6,5},{7,4},{8,11},{9,10},{10,... | collective-permute-start | bytes 184328 | tf_op jit(solution)/shard_map/ppermute | solution.py:636
  19.3 4.7 %collective-permute-start.6 = (f32[120,128]{1,0:T(8,128)S(1)}, f32[120,128]{1,0:T(8,128)S(1)}, u32[]{:S(2)}, u32[]{:S(2)}) collective-permute-start(f32[120,128]{1,0:T(8,128)S(1)} %get-tuple-element.62), channel_id=1, source_target_pairs={{0,1},{1,0},{2,3},{3,2},{4,5},{5,4},{6,7},{7,6},{8,9},{9,8},{10,11... | collective-permute-start | bytes 184328 | tf_op jit(solution)/shard_map/ppermute | solution.py:636
  19.3 7.6 %collective-permute-start.12 = (f32[160,128]{1,0:T(8,128)S(1)}, f32[160,128]{1,0:T(8,128)S(1)}, u32[]{:S(2)}, u32[]{:S(2)}) collective-permute-start(f32[160,128]{1,0:T(8,128)S(1)} %get-tuple-element.64), channel_id=1, source_target_pairs={{0,16},{16,0},{1,17},{17,1},{2,18},{18,2},{3,19},{19,3},{4,20},{20... | collective-permute-start | bytes 245768 | tf_op jit(solution)/shard_map/ppermute | solution.py:636
  20.8 4.9 %collective-permute-start.8 = (f32[80,128]{1,0:T(8,128)S(1)}, f32[80,128]{1,0:T(8,128)S(1)}, u32[]{:S(2)}, u32[]{:S(2)}) collective-permute-start(f32[80,128]{1,0:T(8,128)S(1)} %get-tuple-element.63.refs_0_), channel_id=1, source_target_pairs={{0,2},{1,3},{2,0},{3,1},{4,6},{5,7},{6,4},{7,5},{8,10},{9,11},{10,... | collective-permute-start | bytes 122888 | tf_op jit(solution)/shard_map/ppermute | solution.py:636
  21.7 6.4 %collective-permute-start.11 = (f32[120,128]{1,0:T(8,128)S(1)}, f32[120,128]{1,0:T(8,128)S(1)}, u32[]{:S(2)}, u32[]{:S(2)}) collective-permute-start(f32[120,128]{1,0:T(8,128)S(1)} %collective-permute-done.10.refs_3_.refs_1_), channel_id=1, source_target_pairs={{0,16},{16,0},{1,17},{17,1},{2,18},{18,2},{3,19},{19,3},{4,20},{20... | collective-permute-start | bytes 184328 | tf_op jit(solution)/shard_map/ppermute | solution.py:636
  24.0 4.2 %collective-permute-start.7 = (f32[120,128]{1,0:T(8,128)S(1)}, f32[120,128]{1,0:T(8,128)S(1)}, u32[]{:S(2)}, u32[]{:S(2)}) collective-permute-start(f32[120,128]{1,0:T(8,128)S(1)} %collective-permute-done.6.refs_1_.refs_0_), channel_id=1, source_target_pairs={{0,16},{16,0},{1,17},{17,1},{2,18},{18,2},{3,19},{19,3},{4,20},{20... | collective-permute-start | bytes 184328 | tf_op jit(solution)/shard_map/ppermute | solution.py:636
  25.7 4.0 %collective-permute-start.9 = (f32[80,128]{1,0:T(8,128)S(1)}, f32[80,128]{1,0:T(8,128)S(1)}, u32[]{:S(2)}, u32[]{:S(2)}) collective-permute-start(f32[80,128]{1,0:T(8,128)S(1)} %collective-permute-done.8.refs_2_), channel_id=1, source_target_pairs={{0,16},{16,0},{1,17},{17,1},{2,18},{18,2},{3,19},{19,3},{4,20},{20... | collective-permute-start | bytes 122888 | tf_op jit(solution)/shard_map/ppermute | solution.py:636

commit v3 on v2

--- a/solution.py
+++ b/solution.py
@@ -23,12 +23,12 @@
 EDGE = SUB // NPC
 REACH = SWEEPS - 1
 HIGHEST = lax.Precision.HIGHEST
-PART = 32
+FLOPS = 1e9
 VMEM = pl.BlockSpec(memory_space=pltpu.VMEM)
 HBM = pl.BlockSpec(memory_space=pl.ANY)
 
 
-def kernel_call(body, outs, *args, limit=16 << 20, scratch=(), hbm_ins=(), hbm_outs=()):
+def kernel_call(body, outs, *args, cost=None, limit=16 << 20, scratch=(), hbm_ins=(), hbm_outs=()):
     f32 = jnp.float32
     shapes = []
     for i, out in enumerate(outs):
@@ -47,6 +47,9 @@
         out_specs=[HBM if i in hbm_outs else VMEM for i in range(len(outs))],
         scratch_shapes=list(scratch),
         compiler_params=pltpu.CompilerParams(vmem_limit_bytes=limit),
+        cost_estimate=cost and pl.CostEstimate(
+            flops=int(cost * FLOPS), bytes_accessed=1 << 16, transcendentals=0
+        ),
     )(*args)
 
 
@@ -132,9 +135,14 @@
     return jnp.dot(table, right, preferred_element_type=jnp.float32, precision=HIGHEST)
 
 
-def far_sums(rows, owners, target):
-    below = sum(jnp.where(owner < target, row[0:1], 0.0) for row, owner in zip(rows, owners))
-    above = sum(jnp.where(owner > target, row[1:2], 0.0) for row, owner in zip(rows, owners))
+def far_sums(sums, target):
+    below = above = 0.0
+    shard = lax.axis_index("len")
+    for offset, row in sums.items():
+        for i in range(row.shape[0] // 2):
+            owner = jnp.bitwise_xor(shard, offset ^ i)
+            below = below + jnp.where(owner < target, row[2 * i:2 * i + 1], 0.0)
+            above = above + jnp.where(owner > target, row[2 * i + 1:2 * i + 2], 0.0)
     return below, above
 
 
@@ -153,7 +161,7 @@
     small = [coupling, decay, gain, weight, unit, fire, voltage, tables[0]]
     large = [tissue, *tables[1:], home, cell]
     count = len(small) + len(large)
-    chunk = PART
+    chunk = nodes // 2
 
     def body(*refs):
         small_refs, refs = refs[:len(small)], refs[len(small):]
@@ -249,22 +257,24 @@
             for n, drive in zip(range(start, start + SUB), drives):
                 out_ref[n] = drive
 
-    return kernel_call(body, [states.shape], states, triple)[0]
-
-
-def second_step(states, drive, solved, current, param, misc, table, rise, fall, near):
+    return kernel_call(body, [states.shape], states, triple, cost=0.7)[0]
+
+
+def second_step(fib, states, drive, solved, current, param, misc, rise, fall, near, wide, ends, rows):
     nodes, tall, fibres = states.shape
     cells = nodes // NPC
     shards = len(near)
-
-    def body(states_ref, drive_ref, solved_ref, current_ref, param_ref, misc_ref, table_ref, rise_ref,
-             fall_ref, *rest):
+    long = ends.shape[0]
+    layers = 2 * long
+    flows = STEPS * cells
+    size = flows + SUB
+
+    def body(states_ref, drive_ref, solved_ref, current_ref, param_ref, misc_ref, rise_ref, fall_ref,
+             wide_ref, lanes_ref, *rest):
         near_refs, rest = rest[:shards], rest[shards:]
-        states_out, next_ref, flows_ref, sums_ref, *face_refs, volt_ref, line_ref = rest
+        states_out, volt_ref, flow_ref, send_ref, ends_ref, *face_refs, line_ref = rest
         shard = lax.axis_index("len")
-        rows = [ref[0:SUB, :] for ref in near_refs]
-        owners = [jnp.bitwise_xor(shard, k) for k in range(shards)]
-        below, above = far_sums(rows, owners, shard)
+        below, above = far_sums({k: ref[0:2, :] for k, ref in enumerate(near_refs)}, shard)
         volt_ref[...] = solved_ref[...] + from_far(
             rise_ref, fall_ref, SUB + shard * nodes, nodes, below, above
         )
@@ -273,93 +283,81 @@
             states_out[n], line_ref[nodes + n:nodes + n + 1, :] = advanced(
                 states_ref[n], drive_ref[n], param_ref, volt_ref[n:n + 1, :]
             )
-        binned = line_ref[pl.ds(0, STEPS * cells, stride=NPC), :]
+        flow_ref[...] = line_ref[nodes:, :]
+        binned = line_ref[pl.ds(0, flows, stride=NPC), :]
         for k in range(1, NPC):
-            binned = binned + line_ref[pl.ds(k, STEPS * cells, stride=NPC), :]
-        flows_ref[...] = binned
-        solved = cable(
-            volt_ref[...], line_ref[nodes:2 * nodes, :], misc_ref[2:3, :], 1, table_ref, shard, shards
-        )
-        next_ref[...] = solved[:nodes]
-        sums = solved[nodes:]
-        sums_ref[...] = sums
-        first = jnp.concatenate([binned[t * cells:t * cells + EDGE] for t in range(STEPS)], axis=0)
-        last = jnp.concatenate(
-            [binned[(t + 1) * cells - EDGE:(t + 1) * cells] for t in range(STEPS)], axis=0
-        )
-        for ref, k in zip(face_refs, facing(shards)):
-            ref[0:SUB, :] = sums
-            ref[SUB:, :] = for_partner(shard, k, first, last)
-
-    edge = (SUB + STEPS * EDGE, fibres)
+            binned = binned + line_ref[pl.ds(k, flows, stride=NPC), :]
+        for ref in (send_ref, ends_ref, *face_refs):
+            ref[0:flows, :] = binned
+            ref[flows:size, :] = misc_ref[...]
+        ends_ref[size:, :] = lanes_ref[...]
+        first, last = wide_ref[0:layers, :], wide_ref[rows * long - layers:, :]
+        for ref, k in zip(face_refs, facing(fib)):
+            ref[size:, :] = for_partner(lax.axis_index("fib"), k, first, last)
+
     return kernel_call(
         body,
-        [states.shape, (nodes, fibres), (STEPS * cells, fibres), (SUB, fibres)]
-        + [edge] * len(facing(shards)),
-        states, drive, solved, current, param, misc, table, rise, fall, *near,
-        scratch=[
-            pltpu.VMEM((nodes, fibres), jnp.float32),
-            pltpu.VMEM((STEPS * nodes, fibres), jnp.float32),
-        ],
-    )
-
-
-def packed(fib, flows, misc, near, wide, ends, rows):
-    shards = len(near)
-    cells = flows.shape[0] // STEPS
-    fibres = flows.shape[1]
-    long = cells + 2 * EDGE
-    tall = STEPS * long
-    layers = 2 * long
-
-    def body(flows_ref, misc_ref, wide_ref, lanes_ref, *rest):
-        near_refs, (send_ref, ends_ref, *face_refs) = rest[:shards], rest[shards:]
-        before, after = beside("len", near_refs, slice(SUB, None))
-        for t in range(STEPS):
-            base = t * long
-            part = slice(t * EDGE, (t + 1) * EDGE)
-            send_ref[base:base + EDGE, :] = before[part]
-            send_ref[base + EDGE:base + EDGE + cells, :] = flows_ref[t * cells:(t + 1) * cells, :]
-            send_ref[base + EDGE + cells:base + long, :] = after[part]
-        send_ref[0:1, :] = misc_ref[0:1, :]
-        send_ref[long - 1:long, :] = misc_ref[1:2, :]
-        ends_ref[0:tall, :] = send_ref[...]
-        ends_ref[tall:, :] = lanes_ref[...]
-        first, last = wide_ref[0:layers, :], wide_ref[rows * long - layers:, :]
-        for ref, k in zip(face_refs, facing(fib)):
-            ref[0:tall, :] = send_ref[...]
-            ref[tall:, :] = for_partner(lax.axis_index("fib"), k, first, last)
+        [states.shape, (nodes, fibres), (nodes, fibres), (size, fibres), (size + long, fibres)]
+        + [(size + layers, fibres)] * len(facing(fib)),
+        states, drive, solved, current, param, misc, rise, fall, wide, ends, *near,
+        scratch=[pltpu.VMEM((STEPS * nodes, fibres), jnp.float32)],
+    )
+
+
+def last_solve(shards, voltage, current, misc, table):
+    nodes, fibres = voltage.shape
+
+    def body(voltage_ref, current_ref, misc_ref, table_ref, solved_ref, sums_ref):
+        solved = cable(
+            voltage_ref[...], current_ref[...], misc_ref[2:3, :], STEPS - 1, table_ref,
+            lax.axis_index("len"), shards,
+        )
+        solved_ref[...] = solved[:nodes]
+        sums_ref[...] = solved[nodes:]
+
+    return kernel_call(body, [(nodes, fibres), (SUB, fibres)], voltage, current, misc, table)
+
+
+def paired(sums, other):
+    def body(sums_ref, other_ref, out_ref):
+        out_ref[...] = sums_ref[...]
+        out_ref[2:4, :] = other_ref[0:2, :]
+
+    return kernel_call(body, [sums.shape], sums, other)[0]
+
+
+def edge_cells(shards, cells, sums, got):
+    fibres = sums.shape[1]
+    side = STEPS * EDGE
+
+    def body(sums_ref, *refs):
+        got_refs, refs = refs[:len(got)], refs[len(got):]
+        for ref, k in zip(refs, facing(shards)):
+            ref[0:SUB, :] = sums_ref[...]
+            for g, got_ref in enumerate(got_refs):
+                first, last = (
+                    jnp.concatenate(
+                        [got_ref[t * cells + at:t * cells + at + EDGE, :] for t in range(STEPS)], axis=0
+                    )
+                    for at in (0, cells - EDGE)
+                )
+                begin = SUB + g * side
+                ref[begin:begin + side, :] = for_partner(lax.axis_index("len"), k, first, last)
+
+    shape = (SUB + len(got) * side, fibres)
+    return kernel_call(body, [shape] * len(facing(shards)), sums, *got)
+
+
+def moved(number, states):
+    nodes, _, fibres = states.shape
+
+    def body(states_ref, states_out, sem):
+        for i in range(number):
+            pltpu.make_async_copy(states_ref.at[:, i, :], states_out.at[i], sem).start()
+        pltpu.make_async_copy(states_out, states_out, sem).wait()
 
     return kernel_call(
-        body,
-        [(tall, fibres), (tall + long, fibres)] + [(tall + layers, fibres)] * len(facing(fib)),
-        flows, misc, wide, ends, *near,
-    )
-
-
-def last_voltage(solved, rise, fall, near):
-    nodes, fibres = solved.shape
-    shards = len(near)
-
-    def body(solved_ref, rise_ref, fall_ref, *rest):
-        near_refs, (voltage_out, volt_ref, sem) = rest[:shards], rest[shards:]
-        shard = lax.axis_index("len")
-        rows = [ref[0:SUB, :] for ref in near_refs]
-        owners = [jnp.bitwise_xor(shard, k) for k in range(shards)]
-        below, above = far_sums(rows, owners, shard)
-        volt_ref[...] = solved_ref[...] + from_far(
-            rise_ref, fall_ref, SUB + shard * nodes, nodes, below, above
-        )
-        move = pltpu.make_async_copy(volt_ref, voltage_out, sem)
-        move.start()
-        move.wait()
-
-    return kernel_call(
-        body,
-        [(nodes, fibres)],
-        solved, rise, fall, *near,
-        hbm_outs=(0,),
-        scratch=[pltpu.VMEM((nodes, fibres), jnp.float32), pltpu.SemaphoreType.DMA],
+        body, [(number, nodes, fibres)], states, hbm_outs=(0,), scratch=[pltpu.SemaphoreType.DMA]
     )[0]
 
 
@@ -408,12 +406,13 @@
         lane = iota((long, depth), 1)
         out = jnp.zeros((long, depth), jnp.float32)
         for y in range(rows):
-            base = y * long + EDGE
+            base = y * long
             wide_ref[base:base + cells, :] = tissue_ref[pl.ds(y, cells, stride=rows), :]
             for k in range(2):
                 row = k * rows + y
-                wide_ref[base - 2 + k:base - 1 + k, :] = before[row:row + 1]
-                wide_ref[base + cells + k:base + cells + k + 1, :] = after[row:row + 1]
+                low, high = base + long - 2 + k, base + cells + k
+                wide_ref[low:low + 1, :] = before[row:row + 1]
+                wide_ref[high:high + 1, :] = after[row:row + 1]
             slab = wide_ref[y * long:(y + 1) * long, :]
             spot = lane - 8 * y
             out = jnp.where((spot >= 0) & (spot < 2), pltpu.roll(slab, 8 * y, 1) if y else slab, out)
@@ -428,7 +427,7 @@
     return jnp.where(place < depth, place, upper)
 
 
-def operator_terms(sizes, wide, blocks, rows):
+def operator_terms(sizes, size, wide, blocks, rows):
     shards, fib, emg = sizes
     long = wide.shape[0] // rows
     depth = wide.shape[1]
@@ -442,12 +441,12 @@
         block, (diag_ref, mask_ref) = dict(zip(needed, refs)), refs[len(needed):]
         shard, mine, place = (lax.axis_index(a) for a in ("len", "fib", "emg"))
         below, above = beside(
-            "fib", [block.get((k, 0)) for k in range(fib)], slice(tall, tall + 2 * long)
+            "fib", [block.get((k, 0)) for k in range(fib)], slice(size, size + 2 * long)
         )
 
         def end_lanes(k):
             line = [block.get((k, m)) for m in range(emg)]
-            return beside("emg", line, slice(tall, tall + long))
+            return beside("emg", line, slice(size, size + long))
 
         def of(side):
             parts = [
@@ -477,7 +476,8 @@
             base = (y + 2) * tall
             for step in range(STEPS):
                 diag_ref[base + step * long:base + (step + 1) * long, :] = whole
-        x = lax.rem(iota((tall, lanes), 0), long) - EDGE + shard * cells
+        x = lax.rem(iota((tall, lanes), 0), long)
+        x = jnp.where(x < cells + EDGE, x, x - long) + shard * cells
         z = halo_lanes(iota((tall, lanes), 1), depth) + place * depth
         mask_ref[...] = (
             (x >= 0) & (x < shards * cells) & (z >= 0) & (z < emg * depth)
@@ -490,76 +490,128 @@
     )
 
 
-def sources(sizes, got, rows, earlier=()):
-    tall, depth = sizes
-    lanes = 2 * depth
+def one_hot(column, depth):
+    lanes, fibres = 2 * depth, column.shape[1]
+    lane = halo_lanes(iota((lanes, fibres), 0), depth)
+    lane = jnp.where((lane >= -REACH) & (lane < depth + REACH), lane, -lanes)
+    return (lane == column - lax.axis_index("emg") * depth).astype(jnp.bfloat16)
+
+
+def scattered(values, places, slabs, rows, hot_refs, left_ref):
+    height, fibres = values[0].shape
+    for g, (value, place) in enumerate(zip(values, places)):
+        here = slice(g * fibres, (g + 1) * fibres)
+        both = jnp.concatenate(split(value), axis=0)
+        row = place[0:1].astype(jnp.int32) - lax.axis_index("fib") * rows + REACH
+        for y in range(slabs):
+            pick = (row == y).astype(jnp.float32).astype(jnp.bfloat16)
+            left_ref[y * 2 * height:(y + 1) * 2 * height, here] = both * pick
+    product, at = 0.0, 0
+    for hot_ref in hot_refs:
+        product = product + dot_nt(left_ref[:, at:at + hot_ref.shape[1]], hot_ref[...])
+        at += hot_ref.shape[1]
+    return [
+        product[base:base + height] + product[base + height:base + 2 * height]
+        for base in range(0, slabs * 2 * height, 2 * height)
+    ]
+
+
+def sources(flows, got, rows, depth, earlier=()):
     fibres = got[0].shape[1]
-    groups = len(got)
-    long = tall // STEPS
     slabs = rows + 2 * REACH
-    wide_k = groups * fibres
+    wide_k = len(got) * fibres
 
     def body(*refs):
-        got_refs, (*add_refs, out_ref, hot_ref, left_ref) = refs[:groups], refs[groups:]
-        mine, place = lax.axis_index("fib"), lax.axis_index("emg")
-        lane = halo_lanes(iota((lanes, fibres), 0), depth)
-        lane = jnp.where((lane >= -REACH) & (lane < depth + REACH), lane, -lanes)
-        for g, got_ref in enumerate(got_refs):
-            column = got_ref[long - 1:long, :].astype(jnp.int32) - place * depth
-            hot_ref[:, g * fibres:(g + 1) * fibres] = (lane == column).astype(jnp.bfloat16)
-            both = jnp.concatenate(split(got_ref[0:tall, :]), axis=0)
-            row = got_ref[0:1, :].astype(jnp.int32) - mine * rows + REACH
-            for y in range(slabs):
-                pick = (row == y).astype(jnp.float32).astype(jnp.bfloat16)
-                left_ref[y * 2 * tall:(y + 1) * 2 * tall, g * fibres:(g + 1) * fibres] = both * pick
-        product = dot_nt(left_ref[...], hot_ref[...])
-        for y in range(slabs):
-            base = y * 2 * tall
-            here = slice(y * tall, (y + 1) * tall)
-            out = product[base:base + tall] + product[base + tall:base + 2 * tall]
+        got_refs, (*add_refs, out_ref, hot_ref, left_ref) = refs[:len(got)], refs[len(got):]
+        places = [ref[flows:flows + SUB, :] for ref in got_refs]
+        for g, place in enumerate(places):
+            hot_ref[:, g * fibres:(g + 1) * fibres] = one_hot(place[1:2].astype(jnp.int32), depth)
+        out = scattered(
+            [ref[0:flows, :] for ref in got_refs], places, slabs, rows, [hot_ref], left_ref
+        )
+        for y, value in enumerate(out):
+            here = slice(y * flows, (y + 1) * flows)
             for ref in add_refs:
-                out = out + ref[here, :]
-            out_ref[here, :] = out
+                value = value + ref[here, :]
+            out_ref[here, :] = value
 
     return kernel_call(
         body,
-        [(slabs * tall, lanes)],
+        [(slabs * flows, 2 * depth), ((2 * depth, wide_k), jnp.bfloat16)],
         *got, *earlier,
-        limit=(12 << 20) + slabs * 2 * tall * wide_k * 2,
-        scratch=[
-            pltpu.VMEM((lanes, wide_k), jnp.bfloat16),
-            pltpu.VMEM((slabs * 2 * tall, wide_k), jnp.bfloat16),
-        ],
-    )
-
-
-def potentials(fib, source, diag, mask, rows, number, states):
+        limit=(12 << 20) + slabs * 2 * flows * wide_k * 2,
+        scratch=[pltpu.VMEM((slabs * 2 * flows, wide_k), jnp.bfloat16)],
+    )
+
+
+def potentials(sizes, source, got, hot, sums, near, diag, mask, rows, solved, rise, fall):
+    shards, fib, _ = sizes
     tall, lanes = mask.shape
     long = tall // STEPS
     depth = lanes // 2
     cells = long - 2 * EDGE
     slabs = rows + 2 * REACH
+    side = STEPS * EDGE
+    fibres = got[0].shape[1]
+    nodes = solved.shape[0]
+    groups = len(got)
     coefs = polynomial()
     scale = [c / coefs[-1] for c in coefs]
 
-    def body(src_ref, diag_ref, mask_ref, states_ref, out_ref, states_out, one_ref, two_ref, stage_ref, sems):
-        for i in range(number):
-            pltpu.make_async_copy(states_ref.at[:, i, :], states_out.at[i], sems.at[STEPS]).start()
+    def body(own_ref, diag_ref, mask_ref, solved_ref, rise_ref, fall_ref, *rest):
+        got_refs, hot_refs, rest = rest[:groups], rest[groups:groups + len(hot)], rest[groups + len(hot):]
+        sums_ref, *near_refs = rest[:1 + len(near)]
+        rest = rest[1 + len(near):]
+        near_refs = dict(zip(near, near_refs))
+        pair_refs = {k: ref for k, ref in near_refs.items() if k > 1}
+        near_refs = [near_refs.get(k) for k in range(shards)]
+        out_ref, voltage_out, *rest = rest
+        src_ref, one_ref, two_ref, stage_ref, volt_ref, left_ref, sems = rest
+        shard = lax.axis_index("len")
+        below, far = far_sums(
+            {**{k: ref[0:4, :] for k, ref in pair_refs.items()}, 0: sums_ref[0:4, :]}, shard
+        )
+        volt_ref[...] = solved_ref[...] + from_far(
+            rise_ref, fall_ref, SUB + shard * nodes, nodes, below, far
+        )
+        copies = [pltpu.make_async_copy(volt_ref, voltage_out, sems.at[STEPS])]
+        copies[0].start()
+        before, after = beside("len", near_refs, slice(SUB, None))
+        values = [
+            jnp.concatenate(
+                [
+                    part[g * side + t * EDGE:g * side + (t + 1) * EDGE]
+                    for t in range(STEPS) for part in (after, before)
+                ],
+                axis=0,
+            )
+            for g in range(groups)
+        ]
+        flows = STEPS * cells
+        places = [ref[flows:flows + SUB, :] for ref in got_refs]
+        for y, value in enumerate(scattered(values, places, slabs, rows, hot_refs, left_ref)):
+            for t in range(STEPS):
+                base, own = y * tall + t * long, y * flows + t * cells
+                src_ref[base:base + cells, :] = own_ref[own:own + cells, :]
+                src_ref[base + cells:base + long, :] = value[t * 2 * EDGE:(t + 1) * 2 * EDGE]
+
         mine = lax.axis_index("fib")
         brick, halo = slice(0, depth), slice(depth, lanes)
         gap = iota((depth, depth), 0) - iota((depth, depth), 1)
-        near = ((gap == 1) | (gap == -1)).astype(jnp.float32).astype(jnp.bfloat16)
-        near = jnp.concatenate([near, near], axis=0)
+        beside_lane = ((gap == 1) | (gap == -1)).astype(jnp.float32).astype(jnp.bfloat16)
+        beside_lane = jnp.concatenate([beside_lane, beside_lane], axis=0)
         lane = iota((tall, depth), 1)
         low, high = lane == 0, lane == depth - 1
         ends = (low | high).astype(jnp.float32)
 
         def sweep(ref, y, constant, part, along, begin=0, end=tall):
             here = lambda ref, y: ref[y * tall + begin:y * tall + end, part]
-            size = end - begin
             centre = here(ref, y + REACH)
             beside = here(ref, y + REACH - 1) + here(ref, y + REACH + 1) + along
-            beside = beside + pltpu.roll(centre, 1, 0) + pltpu.roll(centre, size - 1, 0)
+            steps = [centre[i:i + long] for i in range(0, end - begin, long)]
+            for shift in (1, long - 1):
+                moved = [pltpu.roll(step, shift, 0) for step in steps]
+                beside = beside + (jnp.concatenate(moved, axis=0) if len(moved) > 1 else moved[0])
             return here(diag_ref, y + 2) * centre - beside + constant * here(src_ref, y + REACH)
 
         def along_brick(ref, y, begin=0, end=tall):
@@ -570,29 +622,23 @@
                 high[:size], outer, pltpu.roll(inner, depth - 1, 1)
             )
 
-        def domain(value, part):
-            pieces, at = [], 0
-            for step in range(STEPS):
-                base = step * long
-                for begin, end in ((base, base + EDGE), (base + long - EDGE, base + long)):
-                    begin, end = begin // SUB * SUB, -(-end // SUB) * SUB
-                    begin = max(begin, at)
-                    pieces += [value[at:begin]] if begin > at else []
-                    pieces += [value[begin:end] * mask_ref[begin:end, part]] if end > begin else []
-                    at = max(at, end)
-            return jnp.concatenate(pieces + ([value[at:]] if at < tall else []), axis=0)
+        def domain(value):
+            pieces = []
+            for base in range(0, tall, long):
+                end = slice(base + cells, base + long)
+                pieces += [value[base:base + cells], value[end] * mask_ref[end, brick]]
+            return jnp.concatenate(pieces, axis=0)
 
         for k, (source, target) in enumerate(((src_ref, one_ref), (one_ref, two_ref))):
             reach = REACH - 1 - k
             outer = source[(REACH - reach) * tall:(rows + reach + REACH) * tall, halo]
             outer = jnp.dot(
-                jnp.concatenate(split(outer), axis=1), near, preferred_element_type=jnp.float32
+                jnp.concatenate(split(outer), axis=1), beside_lane, preferred_element_type=jnp.float32
             )
             for y in range(-reach, rows + reach):
                 here = slice((y + REACH) * tall, (y + REACH + 1) * tall)
                 along = outer[(y + reach) * tall:(y + reach + 1) * tall] + ends * source[here, brick]
-                inner = sweep(source, y, scale[2 - k], brick, along_brick(source, y))
-                inner = domain(inner, brick)
+                inner = domain(sweep(source, y, scale[2 - k], brick, along_brick(source, y)))
                 along = sweep(source, y, scale[2 - k], halo, along) * mask_ref[:, halo]
                 if y < 0 or y >= rows:
                     keep = (mine > 0 if y < 0 else mine < fib - 1).astype(jnp.float32)
@@ -600,33 +646,33 @@
                 target[here, brick] = inner
                 target[here, halo] = along
         size = cells * rows
-        copies = []
         for step in range(STEPS):
             begin, end = step * long, (step + 1) * long
             for y in range(rows):
                 value = sweep(
                     two_ref, y, scale[0], brick, along_brick(two_ref, y, begin, end), begin, end
                 )
-                stage_ref[pl.ds(step * size + y, cells, stride=rows), :] = (
-                    value[EDGE:EDGE + cells] * coefs[-1]
-                )
+                stage_ref[pl.ds(step * size + y, cells, stride=rows), :] = value[:cells] * coefs[-1]
             here = pl.ds(step * size, size)
             copies.append(pltpu.make_async_copy(stage_ref.at[here], out_ref.at[here], sems.at[step]))
             copies[-1].start()
-        copies.append(pltpu.make_async_copy(states_out, states_out, sems.at[STEPS]))
         for copy in copies:
             copy.wait()
 
     scratch = pltpu.VMEM((slabs * tall, lanes), jnp.float32)
     return kernel_call(
         body,
-        [(STEPS * cells * rows, depth), (number, states.shape[0], states.shape[2])],
-        source, diag, mask, states,
+        [(STEPS * cells * rows, depth), (nodes, fibres)],
+        source, diag, mask, solved, rise, fall, *got, *hot, sums, *near.values(),
+        limit=(16 << 20) + (slabs * 4 * side + lanes) * groups * fibres * 4,
         hbm_outs=(0, 1),
         scratch=[
             scratch,
             scratch,
+            scratch,
             pltpu.VMEM((STEPS * cells * rows, depth), jnp.float32),
+            pltpu.VMEM((nodes, fibres), jnp.float32),
+            pltpu.VMEM((slabs * 4 * side, groups * fibres), jnp.bfloat16),
             pltpu.SemaphoreType.DMA((STEPS + 1,)),
         ],
     )
@@ -665,28 +711,42 @@
         coupling, line(decay_rates), line(volt_gain), line(current_weights),
         line(motor_unit), line(stim_step), line(fibre_home), line(cross_cell),
     )
-    near = swaps("len", sums, with_faces(shards, sums, flat, rows))
     drive = coupled_all(states, triple)
-    states, solved, flows, sums, *faces = second_step(
-        states, drive, solved, current, param, misc, table, rise, fall, near
-    )
+    faces = list(with_faces(shards, sums, flat, rows))
+    near = swaps("len", sums, faces)
+    flows = STEPS * cells
     wide, ends = widened(flat, near, rows)
-    near = swaps("len", sums, faces)
-    near, wide, ends = lax.optimization_barrier((near, wide, ends))
-    send, with_ends, *with_layers = packed(fib, flows, misc, near, wide, ends, rows)
+    size = flows + SUB
+    states, volt, flow, send, with_ends, *with_layers = second_step(
+        fib, states, drive, solved, current, param, misc, rise, fall, near, wide, ends, rows
+    )
     blocks = {(k, 0): block for k, block in enumerate(swaps("fib", send, with_layers))}
     across = swaps("emg", send, [with_ends] * len(facing(emg)))
     for m in range(1, emg):
         for k, block in enumerate(swaps("fib", across[m], [across[m]] * len(facing(fib)))):
             blocks[k, m] = block
-    tall = STEPS * (cells + 2 * EDGE)
-    keys = sorted(blocks)
-    early = [blocks[key] for key in keys if not all(key)]
-    source = sources((tall, depth), early, rows)
-    source = sources((tall, depth), [blocks[key] for key in keys if all(key)], rows, source)[0]
-    voltage = last_voltage(solved, rise, fall, near)
-    diag, mask = operator_terms((shards, fib, emg), wide, blocks, rows)
-    potential, states = potentials(fib, source, diag, mask, rows, count, states)
+    flows = STEPS * cells
+    keys = sorted(blocks, key=lambda key: (all(key), key))
+    count_early = sum(not all(key) for key in keys)
+    got = [blocks[key] for key in keys]
+    solved, sums = last_solve(shards, volt, flow, misc, table)
+    diag, mask = operator_terms((shards, fib, emg), size, wide, blocks, rows)
+    _, ahead = lax.optimization_barrier((across, sums))
+    other = xor_swap(ahead, "len", 1)
+    source, hot = sources(flows, got[:count_early], rows, depth)
+    got, source, other = lax.optimization_barrier((got, source, other))
+    sums = paired(sums, other)
+    edges = edge_cells(shards, cells, sums, got)
+    edges, states = lax.optimization_barrier((edges, states))
+    edges = dict(zip(facing(shards), edges))
+    offsets = sorted({*facing(shards), *(k for k in range(2, shards, 2) if k + 1 not in facing(shards))})
+    near = {k: xor_swap(edges.get(k, sums), "len", k) for k in reversed(offsets)}
+    source, late = sources(flows, got[count_early:], rows, depth, [source])
+    states = moved(count, states)
+    source, states = lax.optimization_barrier((source, states))
+    potential, voltage = potentials(
+        (shards, fib, emg), source, got, (hot, late), sums, near, diag, mask, rows, solved, rise, fall
+    )
     return states, voltage, potential.reshape(STEPS, cells, rows, depth)
 
 

time: 32.8 us -> 31.4 us (0.957)
  starting transfers between devices: 15 us -> 13.7 us
  waiting for transfers between devices: 7.11 us -> 6.18 us
  Pallas kernels: 9.8 us -> 10.6 us
    ppermute x13, starting transfers between devices: 15 us -> 13.7 us  [xor_swap(): lax.ppermute(value, axis, [(i, i ^ k) for i in range(lax.axis_size(axis))])]
    ppermute x13, waiting for transfers between devices: 7.11 us -> 6.18 us  [xor_swap(): lax.ppermute(value, axis, [(i, i ^ k) for i in range(lax.axis_size(axis))])]
    pallas_call x11 -> x13, Pallas kernels: 9.8 us -> 10.6 us  [kernel_call(): pl.pallas_call(body, out_shape=shapes, in_specs=[HBM if i in hbm_ins else...]
  transfers between devices with their start and end apart: 13 -> 13, of which waited for: 7 -> 7; matrix products, arithmetic and copies ran while one was open for 0% -> 0% of each run, Pallas kernels for 9% -> 13%
where the time goes in v3:
time: 31.4 us; the launch traced here: 31.2 us
  starting transfers between devices  13.7 us (44%)
  Pallas kernels  10.6 us (34%)
  waiting for transfers between devices  6.18 us (20%)
  between operations  0.74 us (2%)
    ppermute x13, starting transfers between devices, xor_swap(): lax.ppermute(value, axis, [(i, i ^ k) for i in range(lax.axis_size(axis))])  13.7 us
    pallas_call x13, Pallas kernels, kernel_call(): pl.pallas_call(body, out_shape=shapes, in_specs=[HBM if i in hbm_ins else...  10.6 us
    ppermute x13, waiting for transfers between devices, xor_swap(): lax.ppermute(value, axis, [(i, i ^ k) for i in range(lax.axis_size(axis))])  6.18 us
  transfers between devices with their start and end apart: 13, of which 7 were waited for; matrix products, arithmetic and copies ran while one was open for 0% of the time, Pallas kernels for 13%

profile of v3, /device:TPU:0, one launch (start us, length us, event | category | flops | bytes accessed | tf_op | source)
XLA Modules:
  0.0 31.2 jit_solution(2753883263556535701)
XLA Ops:
  0.6 2.9 %shard_map.157 = (f32[64,64,128]{2,1,0:T(8,128)S(1)}, f32[64,128]{1,0:T(8,128)S(1)}, f32[64,128]{1,0:T(8,128)S(1)}, f32[8,128]{1,0:T(8,128)S(1)}, bf16[64,192]{1...) custom-call(f32[57,57]{1,0:T(8,128)} %refs_0_.1, ...), custom_call_target="tpu_custom_call" | custom-call | tf_op jit(solution)/shard_map/pallas_call | solution.py:43
  3.6 3.0 %collective-permute-start.1 = (f32[8,128]{1,0:T(8,128)S(1)}, f32[8,128]{1,0:T(8,128)S(1)}, u32[]{:S(2)}, u32[]{:S(2)}) collective-permute-start(f32[8,128]{1,0:T(8,128)S(1)} %get-tuple-element.61.sums_ref.rest_0_), channel_id=1, source_target_pairs={{0,8},{4,12},{8,0},{12,4},{1,9},{5,13},{9,1},{13,5},{2,10},{6,14},... | collective-permute-start | bytes 12296 | tf_op jit(solution)/shard_map/ppermute | solution.py:682
  6.6 0.0 collective-permute-start
  6.6 0.2 collective-permute-start.2
  6.8 0.7 %shard_map.158.drive_ref = f32[64,64,128]{2,1,0:T(8,128)S(1)} custom-call(f32[64,64,128]{2,1,0:T(8,128)S(1)} %get-tuple-element.52.states_ref, bf16[64,192]{1,0:T(8,128)(2,1)S(1)} %get-tuple-element.53.triple_ref), custom_call_target="tpu_custom_call" | custom-call | flops 700000000 | bytes 65536 | tf_op jit(solution)/shard_map/pallas_call | solution.py:43
  7.5 0.6 %collective-permute-done.1.rest_2_ = f32[8,128]{1,0:T(8,128)S(1)} collective-permute-done((f32[8,128]{1,0:T(8,128)S(1)}, f32[8,128]{1,0:T(8,128)S(1)}, u32[]{:S(2)}, u32[]{:S(2)}) %collective-permute-start.1) | collective-permute-done | bytes 4128 | tf_op jit(solution)/shard_map/ppermute | solution.py:682
  8.2 0.0 collective-permute-done.rest_1_
  8.2 1.6 %collective-permute-done.2.rest_3_ = f32[24,128]{1,0:T(8,128)S(1)} collective-permute-done((f32[24,128]{1,0:T(8,128)S(1)}, f32[24,128]{1,0:T(8,128)S(1)}, u32[]{:S(2)}, u32[]{:S(2)}) %collective-permute-start.2) | collective-permute-done | bytes 12320 | tf_op jit(solution)/shard_map/ppermute | solution.py:682
  9.8 0.2 shard_map.160
  9.9 0.7 %shard_map.161 = (f32[64,64,128]{2,1,0:T(8,128)S(1)}, f32[64,128]{1,0:T(8,128)S(1)}, f32[64,128]{1,0:T(8,128)S(1)}, f32[72,128]{1,0:T(8,128)S(1)}, f32[112,128]{1,0:T(8,128)S(1)}, /*index=5*/f32[152,128]{1,0:T(8,128)S(1)}) custom-call(f32[64,64,128]{2,1,0:T(8,128)S(1)} %get-tuple-element.52.states_ref, f32[64,64,128]{2,1,0:T(8,128)S(1)} %shard_map.158.drive_ref, ...), custom_call_target="tpu_custom_call" | custom-call | tf_op jit(solution)/shard_map/pallas_call | solution.py:43
  10.6 3.7 %collective-permute-start.5 = (f32[112,128]{1,0:T(8,128)S(1)}, f32[112,128]{1,0:T(8,128)S(1)}, u32[]{:S(2)}, u32[]{:S(2)}) collective-permute-start(f32[112,128]{1,0:T(8,128)S(1)} %get-tuple-element.67), channel_id=1, source_target_pairs={{0,3},{1,2},{2,1},{3,0},{4,7},{5,6},{6,5},{7,4},{8,11},{9,10},{10,... | collective-permute-start | bytes 172040 | tf_op jit(solution)/shard_map/ppermute | solution.py:682
  14.3 0.0 collective-permute-start.3
  14.3 1.5 %collective-permute-start.6 = (f32[152,128]{1,0:T(8,128)S(1)}, f32[152,128]{1,0:T(8,128)S(1)}, u32[]{:S(2)}, u32[]{:S(2)}) collective-permute-start(f32[152,128]{1,0:T(8,128)S(1)} %get-tuple-element.68), channel_id=1, source_target_pairs={{0,16},{16,0},{1,17},{17,1},{2,18},{18,2},{3,19},{19,3},{4,20},{20... | collective-permute-start | bytes 233480 | tf_op jit(solution)/shard_map/ppermute | solution.py:682
  15.8 0.8 %collective-permute-start.4 = (f32[72,128]{1,0:T(8,128)S(1)}, f32[72,128]{1,0:T(8,128)S(1)}, u32[]{:S(2)}, u32[]{:S(2)}) collective-permute-start(f32[72,128]{1,0:T(8,128)S(1)} %get-tuple-element.81.refs_0_.rest_0_), channel_id=1, source_target_pairs={{0,2},{1,3},{2,0},{3,1},{4,6},{5,7},{6,4},{7,5},{8,10},{9,11},{10,... | collective-permute-start | bytes 110600 | tf_op jit(solution)/shard_map/ppermute | solution.py:682
  16.6 0.6 %collective-permute-done.5.refs_3_.refs_1_.rest_3_ = f32[112,128]{1,0:T(8,128)S(1)} collective-permute-done((f32[112,128]{1,0:T(8,128)S(1)}, f32[112,128]{1,0:T(8,128)S(1)}, u32[]{:S(2)}, u32[]{:S(2)}) %collective-permute-start.5) | collective-permute-done | bytes 57376 | tf_op jit(solution)/shard_map/ppermute | solution.py:682
  17.2 1.5 %collective-permute-start.9 = (f32[112,128]{1,0:T(8,128)S(1)}, f32[112,128]{1,0:T(8,128)S(1)}, u32[]{:S(2)}, u32[]{:S(2)}) collective-permute-start(f32[112,128]{1,0:T(8,128)S(1)} %collective-permute-done.5.refs_3_.refs_1_.rest_3_), channel_id=1, source_target_pairs={{0,16},{16,0},{1,17},{17,1},{2,18},{18,2},{3,19},{19,3},{4,20},{20... | collective-permute-start | bytes 172040 | tf_op jit(solution)/shard_map/ppermute | solution.py:682
  18.7 0.0 collective-permute-done.3.refs_1_.refs_0_.rest_1_
  18.7 1.6 %collective-permute-start.7 = (f32[112,128]{1,0:T(8,128)S(1)}, f32[112,128]{1,0:T(8,128)S(1)}, u32[]{:S(2)}, u32[]{:S(2)}) collective-permute-start(f32[112,128]{1,0:T(8,128)S(1)} %collective-permute-done.3.refs_1_.refs_0_.rest_1_), channel_id=1, source_target_pairs={{0,16},{16,0},{1,17},{17,1},{2,18},{18,2},{3,19},{19,3},{4,20},{20... | collective-permute-start | bytes 172040 | tf_op jit(solution)/shard_map/ppermute | solution.py:682
  20.4 0.7 %collective-permute-done.4.refs_2_.rest_2_ = f32[72,128]{1,0:T(8,128)S(1)} collective-permute-done((f32[72,128]{1,0:T(8,128)S(1)}, f32[72,128]{1,0:T(8,128)S(1)}, u32[]{:S(2)}, u32[]{:S(2)}) %collective-permute-start.4) | collective-permute-done | bytes 36896 | tf_op jit(solution)/shard_map/ppermute | solution.py:682
  21.1 0.5 %collective-permute-start.8 = (f32[72,128]{1,0:T(8,128)S(1)}, f32[72,128]{1,0:T(8,128)S(1)}, u32[]{:S(2)}, u32[]{:S(2)}) collective-permute-start(f32[72,128]{1,0:T(8,128)S(1)} %collective-permute-done.4.refs_2_.rest_2_), channel_id=1, source_target_pairs={{0,16},{16,0},{1,17},{17,1},{2,18},{18,2},{3,19},{19,3},{4,20},{20... | collective-permute-start | bytes 110600 | tf_op jit(solution)/shard_map/ppermute | solution.py:682
  21.6 0.2 shard_map.163
  21.8 0.1 collective-permute-start.10
  21.9 0.0 collective-permute-done.6.refs_4_.refs_2_.rest_4_
  21.9 1.0 %shard_map.162 = (f32[896,256]{1,0:T(8,128)S(1)}, bf16[256,640]{1,0:T(8,128)(2,1)S(1)}) custom-call(f32[72,128]{1,0:T(8,128)S(1)} %get-tuple-element.81.refs_0_.rest_0_, f32[112,128]{1,0:T(8,128)S(1)} %collective-permute-done.3.refs_1_.refs_0_.rest_1_, f32[72,128]{1,0:T(8,128)S(1)} %collective-permute-done.4.refs_2_.rest_2_, ...), custom_call_target="tpu_custom_call" | custom-call | tf_op jit(solution)/shard_map/pallas_call | solution.py:43
  22.8 0.2 collective-permute-done.10.other_ref
  23.0 2.0 %collective-permute-done.8.refs_1_.refs_6_.rest_6_ = f32[72,128]{1,0:T(8,128)S(1)} collective-permute-done((f32[72,128]{1,0:T(8,128)S(1)}, f32[72,128]{1,0:T(8,128)S(1)}, u32[]{:S(2)}, u32[]{:S(2)}) %collective-permute-start.8) | collective-permute-done | bytes 36896 | tf_op jit(solution)/shard_map/ppermute | solution.py:682
  25.0 0.0 collective-permute-done.9.refs_2_.refs_7_.refs_4_.rest_7_
  25.0 0.0 collective-permute-done.7.refs_0_.refs_5_.refs_3_.rest_5_
  25.1 0.1 collective-permute-start.11
  25.1 0.7 %collective-permute-start.12 = (f32[72,128]{1,0:T(8,128)S(1)}, f32[72,128]{1,0:T(8,128)S(1)}, u32[]{:S(2)}, u32[]{:S(2)}) collective-permute-start(f32[72,128]{1,0:T(8,128)S(1)} %get-tuple-element.98), channel_id=1, source_target_pairs={{0,4},{4,0},{8,12},{12,8},{1,5},{5,1},{9,13},{13,9},{2,6},{6,2},{1... | collective-permute-start | bytes 110600 | tf_op jit(solution)/shard_map/ppermute | solution.py:682
  25.8 1.2 %shard_map.167 = f32[57,64,128]{2,1,0:T(8,128)} custom-call(f32[64,64,128]{2,1,0:T(8,128)S(1)} %get-tuple-element.89.states_ref), custom_call_target="tpu_custom_call" | custom-call | tf_op jit(solution)/shard_map/pallas_call | solution.py:43
  27.0 0.7 %shard_map.164 = (f32[896,256]{1,0:T(8,128)S(1)}, bf16[256,384]{1,0:T(8,128)(2,1)S(1)}) custom-call(f32[112,128]{1,0:T(8,128)S(1)} %collective-permute-done.7.refs_0_.refs_5_.refs_3_.rest_5_, f32[72,128]{1,0:T(8,128)S(1)} %collective-permute-done.8.refs_1_.refs_6_.rest_6_, f32[112,128]{1,0:T(8,128)S(1)} %collective-permute-done.9.refs_2_.refs_7_.refs_4_.rest_7_, ...), custom_call_target="tpu_custom_call" | custom-call | tf_op jit(solution)/shard_map/pallas_call | solution.py:43
  27.7 0.3 %shard_map.168 = (f32[960,256]{1,0:T(8,128)S(1)}, f32[80,256]{1,0:T(8,128)S(1)}) custom-call(f32[320,128]{1,0:T(8,128)S(1)} %get-tuple-element.64.wide_ref, f32[112,128]{1,0:T(8,128)S(1)} %collective-permute-done.3.refs_1_.refs_0_.rest_1_, f32[112,128]{1,0:T(8,128)S(1)} %collective-permute-done.5.refs_3_.refs_1_.rest_3_, ...), custom_call_target="tpu_custom_call" | custom-call | tf_op jit(solution)/shard_map/pallas_call | solution.py:43
  28.1 0.5 %collective-permute-done.11.rest_11_ = f32[72,128]{1,0:T(8,128)S(1)} collective-permute-done((f32[72,128]{1,0:T(8,128)S(1)}, f32[72,128]{1,0:T(8,128)S(1)}, u32[]{:S(2)}, u32[]{:S(2)}) %collective-permute-start.11) | collective-permute-done | bytes 36896 | tf_op jit(solution)/shard_map/ppermute | solution.py:682
  28.5 0.0 collective-permute-done.12.rest_12_
  28.5 2.7 %shard_map.169 = (f32[512,128]{1,0:T(8,128)}, f32[64,128]{1,0:T(8,128)}) custom-call(f32[896,256]{1,0:T(8,128)S(1)} %get-tuple-element.91.own_ref, f32[960,256]{1,0:T(8,128)S(1)} %get-tuple-element.92.diag_ref, f32[80,256]{1,0:T(8,128)S(1)} %get-tuple-element.93.mask_ref, f32[64,128]{1,0:T(8,128)S(1)} %get-tuple-element.94.solved_ref, ...), custom_call_target="tpu_custom_call" | custom-call | tf_op jit(solution)/shard_map/pallas_call | solution.py:43
  (3 shorter events, 0.0 us)
Async XLA Ops:
  3.6 4.6 %collective-permute-start.1 = (f32[8,128]{1,0:T(8,128)S(1)}, f32[8,128]{1,0:T(8,128)S(1)}, u32[]{:S(2)}, u32[]{:S(2)}) collective-permute-start(f32[8,128]{1,0:T(8,128)S(1)} %get-tuple-element.61.sums_ref.rest_0_), channel_id=1, source_target_pairs={{0,8},{4,12},{8,0},{12,4},{1,9},{5,13},{9,1},{13,5},{2,10},{6,14},... | collective-permute-start | bytes 12296 | tf_op jit(solution)/shard_map/ppermute | solution.py:682
  6.6 1.6 %collective-permute-start = (f32[24,128]{1,0:T(8,128)S(1)}, f32[24,128]{1,0:T(8,128)S(1)}, u32[]{:S(2)}, u32[]{:S(2)}) collective-permute-start(f32[24,128]{1,0:T(8,128)S(1)} %get-tuple-element.62), channel_id=1, source_target_pairs={{0,4},{4,0},{8,12},{12,8},{1,5},{5,1},{9,13},{13,9},{2,6},{6,2},{1... | collective-permute-start | bytes 36872 | tf_op jit(solution)/shard_map/ppermute | solution.py:682
  6.6 3.2 %collective-permute-start.2 = (f32[24,128]{1,0:T(8,128)S(1)}, f32[24,128]{1,0:T(8,128)S(1)}, u32[]{:S(2)}, u32[]{:S(2)}) collective-permute-start(f32[24,128]{1,0:T(8,128)S(1)} %get-tuple-element.63), channel_id=1, source_target_pairs={{0,12},{4,8},{8,4},{12,0},{1,13},{5,9},{9,5},{13,1},{2,14},{6,10},... | collective-permute-start | bytes 36872 | tf_op jit(solution)/shard_map/ppermute | solution.py:682
  10.6 6.6 %collective-permute-start.5 = (f32[112,128]{1,0:T(8,128)S(1)}, f32[112,128]{1,0:T(8,128)S(1)}, u32[]{:S(2)}, u32[]{:S(2)}) collective-permute-start(f32[112,128]{1,0:T(8,128)S(1)} %get-tuple-element.67), channel_id=1, source_target_pairs={{0,3},{1,2},{2,1},{3,0},{4,7},{5,6},{6,5},{7,4},{8,11},{9,10},{10,... | collective-permute-start | bytes 172040 | tf_op jit(solution)/shard_map/ppermute | solution.py:682
  14.3 4.5 %collective-permute-start.3 = (f32[112,128]{1,0:T(8,128)S(1)}, f32[112,128]{1,0:T(8,128)S(1)}, u32[]{:S(2)}, u32[]{:S(2)}) collective-permute-start(f32[112,128]{1,0:T(8,128)S(1)} %get-tuple-element.67), channel_id=1, source_target_pairs={{0,1},{1,0},{2,3},{3,2},{4,5},{5,4},{6,7},{7,6},{8,9},{9,8},{10,11... | collective-permute-start | bytes 172040 | tf_op jit(solution)/shard_map/ppermute | solution.py:682
  14.3 7.6 %collective-permute-start.6 = (f32[152,128]{1,0:T(8,128)S(1)}, f32[152,128]{1,0:T(8,128)S(1)}, u32[]{:S(2)}, u32[]{:S(2)}) collective-permute-start(f32[152,128]{1,0:T(8,128)S(1)} %get-tuple-element.68), channel_id=1, source_target_pairs={{0,16},{16,0},{1,17},{17,1},{2,18},{18,2},{3,19},{19,3},{4,20},{20... | collective-permute-start | bytes 233480 | tf_op jit(solution)/shard_map/ppermute | solution.py:682
  15.8 5.3 %collective-permute-start.4 = (f32[72,128]{1,0:T(8,128)S(1)}, f32[72,128]{1,0:T(8,128)S(1)}, u32[]{:S(2)}, u32[]{:S(2)}) collective-permute-start(f32[72,128]{1,0:T(8,128)S(1)} %get-tuple-element.81.refs_0_.rest_0_), channel_id=1, source_target_pairs={{0,2},{1,3},{2,0},{3,1},{4,6},{5,7},{6,4},{7,5},{8,10},{9,11},{10,... | collective-permute-start | bytes 110600 | tf_op jit(solution)/shard_map/ppermute | solution.py:682
  17.2 7.8 %collective-permute-start.9 = (f32[112,128]{1,0:T(8,128)S(1)}, f32[112,128]{1,0:T(8,128)S(1)}, u32[]{:S(2)}, u32[]{:S(2)}) collective-permute-start(f32[112,128]{1,0:T(8,128)S(1)} %collective-permute-done.5.refs_3_.refs_1_.rest_3_), channel_id=1, source_target_pairs={{0,16},{16,0},{1,17},{17,1},{2,18},{18,2},{3,19},{19,3},{4,20},{20... | collective-permute-start | bytes 172040 | tf_op jit(solution)/shard_map/ppermute | solution.py:682
  18.7 6.3 %collective-permute-start.7 = (f32[112,128]{1,0:T(8,128)S(1)}, f32[112,128]{1,0:T(8,128)S(1)}, u32[]{:S(2)}, u32[]{:S(2)}) collective-permute-start(f32[112,128]{1,0:T(8,128)S(1)} %collective-permute-done.3.refs_1_.refs_0_.rest_1_), channel_id=1, source_target_pairs={{0,16},{16,0},{1,17},{17,1},{2,18},{18,2},{3,19},{19,3},{4,20},{20... | collective-permute-start | bytes 172040 | tf_op jit(solution)/shard_map/ppermute | solution.py:682
  21.1 4.0 %collective-permute-start.8 = (f32[72,128]{1,0:T(8,128)S(1)}, f32[72,128]{1,0:T(8,128)S(1)}, u32[]{:S(2)}, u32[]{:S(2)}) collective-permute-start(f32[72,128]{1,0:T(8,128)S(1)} %collective-permute-done.4.refs_2_.rest_2_), channel_id=1, source_target_pairs={{0,16},{16,0},{1,17},{17,1},{2,18},{18,2},{3,19},{19,3},{4,20},{20... | collective-permute-start | bytes 110600 | tf_op jit(solution)/shard_map/ppermute | solution.py:682
  21.8 1.2 %collective-permute-start.10 = (f32[8,128]{1,0:T(8,128)S(1)}, f32[8,128]{1,0:T(8,128)S(1)}, u32[]{:S(2)}, u32[]{:S(2)}) collective-permute-start(f32[8,128]{1,0:T(8,128)S(1)} %get-tuple-element.74.sums_ref), channel_id=1, source_target_pairs={{0,4},{4,0},{8,12},{12,8},{1,5},{5,1},{9,13},{13,9},{2,6},{6,2},{1... | collective-permute-start | bytes 12296 | tf_op jit(solution)/shard_map/ppermute | solution.py:682
  25.1 3.4 %collective-permute-start.11 = (f32[72,128]{1,0:T(8,128)S(1)}, f32[72,128]{1,0:T(8,128)S(1)}, u32[]{:S(2)}, u32[]{:S(2)}) collective-permute-start(f32[72,128]{1,0:T(8,128)S(1)} %get-tuple-element.97), channel_id=1, source_target_pairs={{0,12},{4,8},{8,4},{12,0},{1,13},{5,9},{9,5},{13,1},{2,14},{6,10},... | collective-permute-start | bytes 110600 | tf_op jit(solution)/shard_map/ppermute | solution.py:682
  25.1 3.4 %collective-permute-start.12 = (f32[72,128]{1,0:T(8,128)S(1)}, f32[72,128]{1,0:T(8,128)S(1)}, u32[]{:S(2)}, u32[]{:S(2)}) collective-permute-start(f32[72,128]{1,0:T(8,128)S(1)} %get-tuple-element.98), channel_id=1, source_target_pairs={{0,4},{4,0},{8,12},{12,8},{1,5},{5,1},{9,13},{13,9},{2,6},{6,2},{1... | collective-permute-start | bytes 110600 | tf_op jit(solution)/shard_map/ppermute | solution.py:682

commit v4 on v3

--- a/solution.py
+++ b/solution.py
@@ -158,8 +158,8 @@
     tall = -(-number // 16) * 16
     full = number // SUB * SUB
     mu = fire.shape[1]
-    small = [coupling, decay, gain, weight, unit, fire, voltage, tables[0]]
-    large = [tissue, *tables[1:], home, cell]
+    small = [coupling, decay, gain, weight, unit, fire, voltage]
+    large = [*tables, tissue, home, cell]
     count = len(small) + len(large)
     chunk = nodes // 2
 
@@ -176,7 +176,7 @@
             for i, (source, target) in enumerate(
                 zip(
                     (*small_refs, *large_refs),
-                    (*stages, table_out, tissue_out, rise_out, fall_out, home_ref, cell_ref),
+                    (*stages, table_out, rise_out, fall_out, tissue_out, home_ref, cell_ref),
                 )
             )
         ]
@@ -215,13 +215,13 @@
                     states_out[n], current_ref[n:n + 1, :] = advanced(
                         tile, drive, param_ref, voltage_ref[n:n + 1, :]
                     )
+        for copy in copies[len(small):]:
+            copy.wait()
         solved = cable(
             voltage_ref[...], current_ref[...], fires[0:1], 0, table_out, lax.axis_index("len"), shards
         )
         solved_ref[...] = solved[:nodes]
         sums_ref[...] = solved[nodes:]
-        for copy in copies[len(small):]:
-            copy.wait()
         brick, spot = home_ref[...], cell_ref[...]
         row = (brick // emg) * rows + spot // depth
         column = (brick % emg) * depth + spot % depth
@@ -238,7 +238,7 @@
         *args,
         hbm_ins=range(len(args)),
         scratch=[
-            *(pltpu.VMEM(a.shape, a.dtype) for a in small[:-1]),
+            *(pltpu.VMEM(a.shape, a.dtype) for a in small),
             pltpu.VMEM(home.shape, home.dtype),
             pltpu.VMEM(cell.shape, cell.dtype),
             pltpu.VMEM((nodes, tall, fibres), jnp.float32),
@@ -264,10 +264,11 @@
     nodes, tall, fibres = states.shape
     cells = nodes // NPC
     shards = len(near)
-    long = ends.shape[0]
+    long = wide.shape[0] // rows
     layers = 2 * long
     flows = STEPS * cells
     size = flows + SUB
+    both = size + ends.shape[0]
 
     def body(states_ref, drive_ref, solved_ref, current_ref, param_ref, misc_ref, rise_ref, fall_ref,
              wide_ref, lanes_ref, *rest):
@@ -290,15 +291,16 @@
         for ref in (send_ref, ends_ref, *face_refs):
             ref[0:flows, :] = binned
             ref[flows:size, :] = misc_ref[...]
-        ends_ref[size:, :] = lanes_ref[...]
+        for ref in (ends_ref, *face_refs):
+            ref[size:both, :] = lanes_ref[...]
         first, last = wide_ref[0:layers, :], wide_ref[rows * long - layers:, :]
         for ref, k in zip(face_refs, facing(fib)):
-            ref[size:, :] = for_partner(lax.axis_index("fib"), k, first, last)
+            ref[both:, :] = for_partner(lax.axis_index("fib"), k, first, last)
 
     return kernel_call(
         body,
-        [states.shape, (nodes, fibres), (nodes, fibres), (size, fibres), (size + long, fibres)]
-        + [(size + layers, fibres)] * len(facing(fib)),
+        [states.shape, (nodes, fibres), (nodes, fibres), (size, fibres), (both, fibres)]
+        + [(both + layers, fibres)] * len(facing(fib)),
         states, drive, solved, current, param, misc, rise, fall, wide, ends, *near,
         scratch=[pltpu.VMEM((STEPS * nodes, fibres), jnp.float32)],
     )
@@ -398,6 +400,8 @@
     cells = tissue.shape[0] // rows
     long = cells + 2 * EDGE
     depth = tissue.shape[1]
+
+    per = depth // (4 * rows)
 
     def body(tissue_ref, *rest):
         near_refs, (wide_ref, lanes_ref) = rest[:shards], rest[shards:]
@@ -414,12 +418,16 @@
                 wide_ref[low:low + 1, :] = before[row:row + 1]
                 wide_ref[high:high + 1, :] = after[row:row + 1]
             slab = wide_ref[y * long:(y + 1) * long, :]
-            spot = lane - 8 * y
-            out = jnp.where((spot >= 0) & (spot < 2), pltpu.roll(slab, 8 * y, 1) if y else slab, out)
-            out = jnp.where((spot >= 2) & (spot < 4), pltpu.roll(slab, 8 * y + 4, 1), out)
-        lanes_ref[...] = out
-
-    return kernel_call(body, [(rows * long, depth), (long, depth)], tissue, *near)
+            spot = lane - 4 * y
+            out = jnp.where((spot >= 0) & (spot < 2), pltpu.roll(slab, 4 * y, 1) if y else slab, out)
+            out = jnp.where((spot >= 2) & (spot < 4), pltpu.roll(slab, 4 * y + 4, 1), out)
+        lanes_ref[...] = jnp.zeros_like(lanes_ref)
+        for i in range(long // SUB):
+            tile, at = out[i * SUB:(i + 1) * SUB], i // per * SUB
+            shift = i % per * 4 * rows
+            lanes_ref[at:at + SUB, :] += pltpu.roll(tile, shift, 1) if shift else tile
+
+    return kernel_call(body, [(rows * long, depth), (-(-long // SUB // per) * SUB, depth)], tissue, *near)
 
 
 def halo_lanes(place, depth):
@@ -427,12 +435,13 @@
     return jnp.where(place < depth, place, upper)
 
 
-def operator_terms(sizes, size, wide, blocks, rows):
+def operator_terms(sizes, size, ends, wide, blocks, rows):
     shards, fib, emg = sizes
     long = wide.shape[0] // rows
     depth = wide.shape[1]
     cells = long - 2 * EDGE
     tall, lanes = STEPS * long, 2 * depth
+    per = depth // (4 * rows)
     needed = sorted(
         (k, m) for k in (0, *facing(fib)) for m in (0, *facing(emg)) if k or m
     )
@@ -441,12 +450,22 @@
         block, (diag_ref, mask_ref) = dict(zip(needed, refs)), refs[len(needed):]
         shard, mine, place = (lax.axis_index(a) for a in ("len", "fib", "emg"))
         below, above = beside(
-            "fib", [block.get((k, 0)) for k in range(fib)], slice(size, size + 2 * long)
+            "fib", [block.get((k, 0)) for k in range(fib)], slice(size + ends, size + ends + 2 * long)
         )
 
         def end_lanes(k):
             line = [block.get((k, m)) for m in range(emg)]
-            return beside("emg", line, slice(size, size + long))
+            return [
+                jnp.concatenate(
+                    [
+                        pltpu.roll(tile[i // per * SUB:i // per * SUB + SUB], -i % per * 4 * rows, 1)
+                        if i % per else tile[i // per * SUB:i // per * SUB + SUB]
+                        for i in range(long // SUB)
+                    ],
+                    axis=0,
+                )
+                for tile in beside("emg", line, slice(size, size + ends))
+            ]
 
         def of(side):
             parts = [
@@ -467,7 +486,7 @@
             side = jnp.zeros((long, depth), jnp.float32)
             if -2 < y < rows + 1:
                 before, after = under if y < 0 else over if y >= rows else own
-                k = 8 * (y % rows)
+                k = 4 * (y % rows)
                 for to, source, lane in (
                     (0, before, k + 3), (1, before, k + 2), (depth - 1, after, k), (depth - 2, after, k + 1)
                 ):
@@ -678,6 +697,13 @@
     )
 
 
+def trimmed(size, block):
+    def body(block_ref, out_ref):
+        out_ref[...] = block_ref[0:size, :]
+
+    return kernel_call(body, [(size, block.shape[1])], block)[0]
+
+
 def xor_swap(value, axis, k):
     return lax.ppermute(value, axis, [(i, i ^ k) for i in range(lax.axis_size(axis))])
 
@@ -723,14 +749,17 @@
     blocks = {(k, 0): block for k, block in enumerate(swaps("fib", send, with_layers))}
     across = swaps("emg", send, [with_ends] * len(facing(emg)))
     for m in range(1, emg):
-        for k, block in enumerate(swaps("fib", across[m], [across[m]] * len(facing(fib)))):
-            blocks[k, m] = block
-    flows = STEPS * cells
+        blocks[0, m] = across[m]
+        for k in range(1, fib):
+            if m == 1 and k in facing(fib):
+                blocks[k, m] = xor_swap(trimmed(with_ends.shape[0], blocks[k, 0]), "emg", m)
+            else:
+                blocks[k, m] = xor_swap(across[m], "fib", k)
     keys = sorted(blocks, key=lambda key: (all(key), key))
     count_early = sum(not all(key) for key in keys)
     got = [blocks[key] for key in keys]
     solved, sums = last_solve(shards, volt, flow, misc, table)
-    diag, mask = operator_terms((shards, fib, emg), size, wide, blocks, rows)
+    diag, mask = operator_terms((shards, fib, emg), size, ends.shape[0], wide, blocks, rows)
     _, ahead = lax.optimization_barrier((across, sums))
     other = xor_swap(ahead, "len", 1)
     source, hot = sources(flows, got[:count_early], rows, depth)

time: 31.4 us -> 30.9 us (0.984)
  starting transfers between devices: 13.7 us -> 12.2 us
  waiting for transfers between devices: 6.18 us -> 7.25 us
    ppermute x13, starting transfers between devices: 13.7 us -> 12.2 us  [xor_swap(): lax.ppermute(value, axis, [(i, i ^ k) for i in range(lax.axis_size(axis))])]
    ppermute x13, waiting for transfers between devices: 6.18 us -> 7.25 us  [xor_swap(): lax.ppermute(value, axis, [(i, i ^ k) for i in range(lax.axis_size(axis))])]
    pallas_call x13 -> x14, Pallas kernels: 10.6 us -> 10.5 us  [kernel_call(): pl.pallas_call(body, out_shape=shapes, in_specs=[HBM if i in hbm_ins else...]
where the time goes in v4:
time: 30.9 us; the launch traced here: 30.7 us
  starting transfers between devices  12.2 us (39%)
  Pallas kernels  10.5 us (34%)
  waiting for transfers between devices  7.25 us (23%)
  between operations  0.74 us (2%)
    ppermute x13, starting transfers between devices, xor_swap(): lax.ppermute(value, axis, [(i, i ^ k) for i in range(lax.axis_size(axis))])  12.2 us
    pallas_call x14, Pallas kernels, kernel_call(): pl.pallas_call(body, out_shape=shapes, in_specs=[HBM if i in hbm_ins else...  10.5 us
    ppermute x13, waiting for transfers between devices, xor_swap(): lax.ppermute(value, axis, [(i, i ^ k) for i in range(lax.axis_size(axis))])  7.25 us
  transfers between devices with their start and end apart: 13, of which 7 were waited for; matrix products, arithmetic and copies ran while one was open for 0% of the time, Pallas kernels for 13%

profile of v4, /device:TPU:0, one launch (start us, length us, event | category | flops | bytes accessed | tf_op | source)
XLA Modules:
  0.0 30.7 jit_solution(9822764893590926527)
XLA Ops:
  0.6 2.9 %shard_map.157 = (f32[64,64,128]{2,1,0:T(8,128)S(1)}, f32[64,128]{1,0:T(8,128)S(1)}, f32[64,128]{1,0:T(8,128)S(1)}, f32[8,128]{1,0:T(8,128)S(1)}, bf16[64,192]{1...) custom-call(f32[57,57]{1,0:T(8,128)} %refs_0_.1, ...), custom_call_target="tpu_custom_call" | custom-call | tf_op jit(solution)/shard_map/pallas_call | solution.py:43
  3.5 3.0 %collective-permute-start.1 = (f32[8,128]{1,0:T(8,128)S(1)}, f32[8,128]{1,0:T(8,128)S(1)}, u32[]{:S(2)}, u32[]{:S(2)}) collective-permute-start(f32[8,128]{1,0:T(8,128)S(1)} %get-tuple-element.61.sums_ref.rest_0_), channel_id=1, source_target_pairs={{0,8},{4,12},{8,0},{12,4},{1,9},{5,13},{9,1},{13,5},{2,10},{6,14},... | collective-permute-start | bytes 12296 | tf_op jit(solution)/shard_map/ppermute | solution.py:708
  6.5 0.0 collective-permute-start
  6.5 0.2 collective-permute-start.2
  6.8 0.7 %shard_map.158.drive_ref = f32[64,64,128]{2,1,0:T(8,128)S(1)} custom-call(f32[64,64,128]{2,1,0:T(8,128)S(1)} %get-tuple-element.52.states_ref, bf16[64,192]{1,0:T(8,128)(2,1)S(1)} %get-tuple-element.53.triple_ref), custom_call_target="tpu_custom_call" | custom-call | flops 700000000 | bytes 65536 | tf_op jit(solution)/shard_map/pallas_call | solution.py:43
  7.5 0.6 %collective-permute-done.1.rest_2_ = f32[8,128]{1,0:T(8,128)S(1)} collective-permute-done((f32[8,128]{1,0:T(8,128)S(1)}, f32[8,128]{1,0:T(8,128)S(1)}, u32[]{:S(2)}, u32[]{:S(2)}) %collective-permute-start.1) | collective-permute-done | bytes 4128 | tf_op jit(solution)/shard_map/ppermute | solution.py:708
  8.1 0.0 collective-permute-done.rest_1_
  8.1 1.6 %collective-permute-done.2.rest_3_ = f32[24,128]{1,0:T(8,128)S(1)} collective-permute-done((f32[24,128]{1,0:T(8,128)S(1)}, f32[24,128]{1,0:T(8,128)S(1)}, u32[]{:S(2)}, u32[]{:S(2)}) %collective-permute-start.2) | collective-permute-done | bytes 12320 | tf_op jit(solution)/shard_map/ppermute | solution.py:708
  9.7 0.2 shard_map.160
  9.9 0.7 %shard_map.161 = (f32[64,64,128]{2,1,0:T(8,128)S(1)}, f32[64,128]{1,0:T(8,128)S(1)}, f32[64,128]{1,0:T(8,128)S(1)}, f32[72,128]{1,0:T(8,128)S(1)}, f32[88,128]{1,0:T(8,128)S(1)}, /*index=5*/f32[168,128]{1,0:T(8,128)S(1)}) custom-call(f32[64,64,128]{2,1,0:T(8,128)S(1)} %get-tuple-element.52.states_ref, f32[64,64,128]{2,1,0:T(8,128)S(1)} %shard_map.158.drive_ref, ...), custom_call_target="tpu_custom_call" | custom-call | tf_op jit(solution)/shard_map/pallas_call | solution.py:43
  10.6 1.6 %collective-permute-start.6 = (f32[168,128]{1,0:T(8,128)S(1)}, f32[168,128]{1,0:T(8,128)S(1)}, u32[]{:S(2)}, u32[]{:S(2)}) collective-permute-start(f32[168,128]{1,0:T(8,128)S(1)} %get-tuple-element.68), channel_id=1, source_target_pairs={{0,16},{16,0},{1,17},{17,1},{2,18},{18,2},{3,19},{19,3},{4,20},{20... | collective-permute-start | bytes 258056 | tf_op jit(solution)/shard_map/ppermute | solution.py:708
  12.2 3.6 %collective-permute-start.5 = (f32[88,128]{1,0:T(8,128)S(1)}, f32[88,128]{1,0:T(8,128)S(1)}, u32[]{:S(2)}, u32[]{:S(2)}) collective-permute-start(f32[88,128]{1,0:T(8,128)S(1)} %get-tuple-element.67), channel_id=1, source_target_pairs={{0,3},{1,2},{2,1},{3,0},{4,7},{5,6},{6,5},{7,4},{8,11},{9,10},{10,... | collective-permute-start | bytes 135176 | tf_op jit(solution)/shard_map/ppermute | solution.py:708
  15.8 0.0 collective-permute-start.4
  15.8 0.8 %collective-permute-start.3 = (f32[88,128]{1,0:T(8,128)S(1)}, f32[88,128]{1,0:T(8,128)S(1)}, u32[]{:S(2)}, u32[]{:S(2)}) collective-permute-start(f32[88,128]{1,0:T(8,128)S(1)} %get-tuple-element.67), channel_id=1, source_target_pairs={{0,1},{1,0},{2,3},{3,2},{4,5},{5,4},{6,7},{7,6},{8,9},{9,8},{10,11... | collective-permute-start | bytes 135176 | tf_op jit(solution)/shard_map/ppermute | solution.py:708
  16.6 1.5 %collective-permute-done.5.refs_3_.refs_1_.rest_3_ = f32[88,128]{1,0:T(8,128)S(1)} collective-permute-done((f32[88,128]{1,0:T(8,128)S(1)}, f32[88,128]{1,0:T(8,128)S(1)}, u32[]{:S(2)}, u32[]{:S(2)}) %collective-permute-start.5) | collective-permute-done | bytes 45088 | tf_op jit(solution)/shard_map/ppermute | solution.py:708
  18.1 0.5 %collective-permute-start.9 = (f32[88,128]{1,0:T(8,128)S(1)}, f32[88,128]{1,0:T(8,128)S(1)}, u32[]{:S(2)}, u32[]{:S(2)}) collective-permute-start(f32[88,128]{1,0:T(8,128)S(1)} %collective-permute-done.5.refs_3_.refs_1_.rest_3_), channel_id=1, source_target_pairs={{0,16},{16,0},{1,17},{17,1},{2,18},{18,2},{3,19},{19,3},{4,20},{20... | collective-permute-start | bytes 135176 | tf_op jit(solution)/shard_map/ppermute | solution.py:708
  18.6 0.0 collective-permute-done.6.block_ref.refs_4_.refs_2_.rest_4_
  18.6 1.2 %collective-permute-start.7 = (f32[88,128]{1,0:T(8,128)S(1)}, f32[88,128]{1,0:T(8,128)S(1)}, u32[]{:S(2)}, u32[]{:S(2)}) collective-permute-start(f32[88,128]{1,0:T(8,128)S(1)} %shard_map.162), channel_id=1, source_target_pairs={{0,1},{1,0},{2,3},{3,2},{4,5},{5,4},{6,7},{7,6},{8,9},{9,8},{10,11... | collective-permute-start | bytes 135176 | tf_op jit(solution)/shard_map/ppermute | solution.py:708
  19.7 0.9 %collective-permute-done.4.refs_2_.rest_2_ = f32[72,128]{1,0:T(8,128)S(1)} collective-permute-done((f32[72,128]{1,0:T(8,128)S(1)}, f32[72,128]{1,0:T(8,128)S(1)}, u32[]{:S(2)}, u32[]{:S(2)}) %collective-permute-start.4) | collective-permute-done | bytes 36896 | tf_op jit(solution)/shard_map/ppermute | solution.py:708
  20.7 0.6 %collective-permute-start.8 = (f32[72,128]{1,0:T(8,128)S(1)}, f32[72,128]{1,0:T(8,128)S(1)}, u32[]{:S(2)}, u32[]{:S(2)}) collective-permute-start(f32[72,128]{1,0:T(8,128)S(1)} %collective-permute-done.4.refs_2_.rest_2_), channel_id=1, source_target_pairs={{0,16},{16,0},{1,17},{17,1},{2,18},{18,2},{3,19},{19,3},{4,20},{20... | collective-permute-start | bytes 110600 | tf_op jit(solution)/shard_map/ppermute | solution.py:708
  21.3 0.2 shard_map.164
  21.5 0.0 collective-permute-done.3.refs_1_.refs_0_.rest_1_
  21.5 0.1 collective-permute-start.10
  21.6 1.0 %shard_map.163 = (f32[896,256]{1,0:T(8,128)S(1)}, bf16[256,640]{1,0:T(8,128)(2,1)S(1)}) custom-call(f32[72,128]{1,0:T(8,128)S(1)} %get-tuple-element.81.refs_0_.rest_0_, f32[88,128]{1,0:T(8,128)S(1)} %collective-permute-done.3.refs_1_.refs_0_.rest_1_, f32[72,128]{1,0:T(8,128)S(1)} %collective-permute-done.4.refs_2_.rest_2_, ...), custom_call_target="tpu_custom_call" | custom-call | tf_op jit(solution)/shard_map/pallas_call | solution.py:43
  22.5 0.2 collective-permute-done.10.other_ref
  22.7 1.9 %collective-permute-done.8.refs_1_.refs_6_.rest_6_ = f32[72,128]{1,0:T(8,128)S(1)} collective-permute-done((f32[72,128]{1,0:T(8,128)S(1)}, f32[72,128]{1,0:T(8,128)S(1)}, u32[]{:S(2)}, u32[]{:S(2)}) %collective-permute-start.8) | collective-permute-done | bytes 36896 | tf_op jit(solution)/shard_map/ppermute | solution.py:708
  24.6 0.0 collective-permute-done.9.refs_2_.refs_7_.refs_4_.rest_7_
  24.6 0.0 collective-permute-done.7.refs_0_.refs_5_.refs_3_.rest_5_
  24.7 0.1 collective-permute-start.11
  24.8 0.7 %collective-permute-start.12 = (f32[72,128]{1,0:T(8,128)S(1)}, f32[72,128]{1,0:T(8,128)S(1)}, u32[]{:S(2)}, u32[]{:S(2)}) collective-permute-start(f32[72,128]{1,0:T(8,128)S(1)} %get-tuple-element.98), channel_id=1, source_target_pairs={{0,4},{4,0},{8,12},{12,8},{1,5},{5,1},{9,13},{13,9},{2,6},{6,2},{1... | collective-permute-start | bytes 110600 | tf_op jit(solution)/shard_map/ppermute | solution.py:708
  25.4 1.2 %shard_map.168 = f32[57,64,128]{2,1,0:T(8,128)} custom-call(f32[64,64,128]{2,1,0:T(8,128)S(1)} %get-tuple-element.89.states_ref), custom_call_target="tpu_custom_call" | custom-call | tf_op jit(solution)/shard_map/pallas_call | solution.py:43
  26.6 0.7 %shard_map.165 = (f32[896,256]{1,0:T(8,128)S(1)}, bf16[256,384]{1,0:T(8,128)(2,1)S(1)}) custom-call(f32[88,128]{1,0:T(8,128)S(1)} %collective-permute-done.7.refs_0_.refs_5_.refs_3_.rest_5_, f32[72,128]{1,0:T(8,128)S(1)} %collective-permute-done.8.refs_1_.refs_6_.rest_6_, f32[88,128]{1,0:T(8,128)S(1)} %collective-permute-done.9.refs_2_.refs_7_.refs_4_.rest_7_, ...), custom_call_target="tpu_custom_call" | custom-call | tf_op jit(solution)/shard_map/pallas_call | solution.py:43
  27.3 0.3 %shard_map.169 = (f32[960,256]{1,0:T(8,128)S(1)}, f32[80,256]{1,0:T(8,128)S(1)}) custom-call(f32[320,128]{1,0:T(8,128)S(1)} %get-tuple-element.64.wide_ref, f32[88,128]{1,0:T(8,128)S(1)} %collective-permute-done.3.refs_1_.refs_0_.rest_1_, f32[88,128]{1,0:T(8,128)S(1)} %collective-permute-done.5.refs_3_.refs_1_.rest_3_, ...), custom_call_target="tpu_custom_call" | custom-call | tf_op jit(solution)/shard_map/pallas_call | solution.py:43
  27.7 0.4 %collective-permute-done.11.rest_11_ = f32[72,128]{1,0:T(8,128)S(1)} collective-permute-done((f32[72,128]{1,0:T(8,128)S(1)}, f32[72,128]{1,0:T(8,128)S(1)}, u32[]{:S(2)}, u32[]{:S(2)}) %collective-permute-start.11) | collective-permute-done | bytes 36896 | tf_op jit(solution)/shard_map/ppermute | solution.py:708
  28.1 0.0 collective-permute-done.12.rest_12_
  28.1 2.6 %shard_map.170 = (f32[512,128]{1,0:T(8,128)}, f32[64,128]{1,0:T(8,128)}) custom-call(f32[896,256]{1,0:T(8,128)S(1)} %get-tuple-element.91.own_ref, f32[960,256]{1,0:T(8,128)S(1)} %get-tuple-element.92.diag_ref, f32[80,256]{1,0:T(8,128)S(1)} %get-tuple-element.93.mask_ref, f32[64,128]{1,0:T(8,128)S(1)} %get-tuple-element.94.solved_ref, ...), custom_call_target="tpu_custom_call" | custom-call | tf_op jit(solution)/shard_map/pallas_call | solution.py:43
  (4 shorter events, 0.0 us)
Async XLA Ops:
  3.5 4.6 %collective-permute-start.1 = (f32[8,128]{1,0:T(8,128)S(1)}, f32[8,128]{1,0:T(8,128)S(1)}, u32[]{:S(2)}, u32[]{:S(2)}) collective-permute-start(f32[8,128]{1,0:T(8,128)S(1)} %get-tuple-element.61.sums_ref.rest_0_), channel_id=1, source_target_pairs={{0,8},{4,12},{8,0},{12,4},{1,9},{5,13},{9,1},{13,5},{2,10},{6,14},... | collective-permute-start | bytes 12296 | tf_op jit(solution)/shard_map/ppermute | solution.py:708
  6.5 1.6 %collective-permute-start = (f32[24,128]{1,0:T(8,128)S(1)}, f32[24,128]{1,0:T(8,128)S(1)}, u32[]{:S(2)}, u32[]{:S(2)}) collective-permute-start(f32[24,128]{1,0:T(8,128)S(1)} %get-tuple-element.62), channel_id=1, source_target_pairs={{0,4},{4,0},{8,12},{12,8},{1,5},{5,1},{9,13},{13,9},{2,6},{6,2},{1... | collective-permute-start | bytes 36872 | tf_op jit(solution)/shard_map/ppermute | solution.py:708
  6.5 3.2 %collective-permute-start.2 = (f32[24,128]{1,0:T(8,128)S(1)}, f32[24,128]{1,0:T(8,128)S(1)}, u32[]{:S(2)}, u32[]{:S(2)}) collective-permute-start(f32[24,128]{1,0:T(8,128)S(1)} %get-tuple-element.63), channel_id=1, source_target_pairs={{0,12},{4,8},{8,4},{12,0},{1,13},{5,9},{9,5},{13,1},{2,14},{6,10},... | collective-permute-start | bytes 36872 | tf_op jit(solution)/shard_map/ppermute | solution.py:708
  10.6 8.0 %collective-permute-start.6 = (f32[168,128]{1,0:T(8,128)S(1)}, f32[168,128]{1,0:T(8,128)S(1)}, u32[]{:S(2)}, u32[]{:S(2)}) collective-permute-start(f32[168,128]{1,0:T(8,128)S(1)} %get-tuple-element.68), channel_id=1, source_target_pairs={{0,16},{16,0},{1,17},{17,1},{2,18},{18,2},{3,19},{19,3},{4,20},{20... | collective-permute-start | bytes 258056 | tf_op jit(solution)/shard_map/ppermute | solution.py:708
  12.2 5.9 %collective-permute-start.5 = (f32[88,128]{1,0:T(8,128)S(1)}, f32[88,128]{1,0:T(8,128)S(1)}, u32[]{:S(2)}, u32[]{:S(2)}) collective-permute-start(f32[88,128]{1,0:T(8,128)S(1)} %get-tuple-element.67), channel_id=1, source_target_pairs={{0,3},{1,2},{2,1},{3,0},{4,7},{5,6},{6,5},{7,4},{8,11},{9,10},{10,... | collective-permute-start | bytes 135176 | tf_op jit(solution)/shard_map/ppermute | solution.py:708
  15.8 4.9 %collective-permute-start.4 = (f32[72,128]{1,0:T(8,128)S(1)}, f32[72,128]{1,0:T(8,128)S(1)}, u32[]{:S(2)}, u32[]{:S(2)}) collective-permute-start(f32[72,128]{1,0:T(8,128)S(1)} %get-tuple-element.81.refs_0_.rest_0_), channel_id=1, source_target_pairs={{0,2},{1,3},{2,0},{3,1},{4,6},{5,7},{6,4},{7,5},{8,10},{9,11},{10,... | collective-permute-start | bytes 110600 | tf_op jit(solution)/shard_map/ppermute | solution.py:708
  15.8 5.7 %collective-permute-start.3 = (f32[88,128]{1,0:T(8,128)S(1)}, f32[88,128]{1,0:T(8,128)S(1)}, u32[]{:S(2)}, u32[]{:S(2)}) collective-permute-start(f32[88,128]{1,0:T(8,128)S(1)} %get-tuple-element.67), channel_id=1, source_target_pairs={{0,1},{1,0},{2,3},{3,2},{4,5},{5,4},{6,7},{7,6},{8,9},{9,8},{10,11... | collective-permute-start | bytes 135176 | tf_op jit(solution)/shard_map/ppermute | solution.py:708
  18.1 6.6 %collective-permute-start.9 = (f32[88,128]{1,0:T(8,128)S(1)}, f32[88,128]{1,0:T(8,128)S(1)}, u32[]{:S(2)}, u32[]{:S(2)}) collective-permute-start(f32[88,128]{1,0:T(8,128)S(1)} %collective-permute-done.5.refs_3_.refs_1_.rest_3_), channel_id=1, source_target_pairs={{0,16},{16,0},{1,17},{17,1},{2,18},{18,2},{3,19},{19,3},{4,20},{20... | collective-permute-start | bytes 135176 | tf_op jit(solution)/shard_map/ppermute | solution.py:708
  18.6 6.1 %collective-permute-start.7 = (f32[88,128]{1,0:T(8,128)S(1)}, f32[88,128]{1,0:T(8,128)S(1)}, u32[]{:S(2)}, u32[]{:S(2)}) collective-permute-start(f32[88,128]{1,0:T(8,128)S(1)} %shard_map.162), channel_id=1, source_target_pairs={{0,1},{1,0},{2,3},{3,2},{4,5},{5,4},{6,7},{7,6},{8,9},{9,8},{10,11... | collective-permute-start | bytes 135176 | tf_op jit(solution)/shard_map/ppermute | solution.py:708
  20.7 4.0 %collective-permute-start.8 = (f32[72,128]{1,0:T(8,128)S(1)}, f32[72,128]{1,0:T(8,128)S(1)}, u32[]{:S(2)}, u32[]{:S(2)}) collective-permute-start(f32[72,128]{1,0:T(8,128)S(1)} %collective-permute-done.4.refs_2_.rest_2_), channel_id=1, source_target_pairs={{0,16},{16,0},{1,17},{17,1},{2,18},{18,2},{3,19},{19,3},{4,20},{20... | collective-permute-start | bytes 110600 | tf_op jit(solution)/shard_map/ppermute | solution.py:708
  21.5 1.2 %collective-permute-start.10 = (f32[8,128]{1,0:T(8,128)S(1)}, f32[8,128]{1,0:T(8,128)S(1)}, u32[]{:S(2)}, u32[]{:S(2)}) collective-permute-start(f32[8,128]{1,0:T(8,128)S(1)} %get-tuple-element.74.sums_ref), channel_id=1, source_target_pairs={{0,4},{4,0},{8,12},{12,8},{1,5},{5,1},{9,13},{13,9},{2,6},{6,2},{1... | collective-permute-start | bytes 12296 | tf_op jit(solution)/shard_map/ppermute | solution.py:708
  24.7 3.4 %collective-permute-start.11 = (f32[72,128]{1,0:T(8,128)S(1)}, f32[72,128]{1,0:T(8,128)S(1)}, u32[]{:S(2)}, u32[]{:S(2)}) collective-permute-start(f32[72,128]{1,0:T(8,128)S(1)} %get-tuple-element.97), channel_id=1, source_target_pairs={{0,12},{4,8},{8,4},{12,0},{1,13},{5,9},{9,5},{13,1},{2,14},{6,10},... | collective-permute-start | bytes 110600 | tf_op jit(solution)/shard_map/ppermute | solution.py:708
  24.8 3.4 %collective-permute-start.12 = (f32[72,128]{1,0:T(8,128)S(1)}, f32[72,128]{1,0:T(8,128)S(1)}, u32[]{:S(2)}, u32[]{:S(2)}) collective-permute-start(f32[72,128]{1,0:T(8,128)S(1)} %get-tuple-element.98), channel_id=1, source_target_pairs={{0,4},{4,0},{8,12},{12,8},{1,5},{5,1},{9,13},{13,9},{2,6},{6,2},{1... | collective-permute-start | bytes 110600 | tf_op jit(solution)/shard_map/ppermute | solution.py:708

commit v5 on v4

--- a/solution.py
+++ b/solution.py
@@ -101,11 +101,14 @@
     blocks = []
     for k in range(shards):
         mine = slice(k * local, (k + 1) * local)
-        tail = np.zeros((SUB, local))
+        tail = np.zeros((2 * SUB, local))
         tail[0], tail[1] = rise[mine], fall[mine]
         blocks.append(np.concatenate([inverse[mine, mine], tail]))
-    wide = lambda v: np.repeat(np.pad(v, SUB)[:, None], LANES, axis=1).astype(np.float32)
-    return np.concatenate(blocks).astype(np.float32), wide(rise), wide(fall)
+    wide = lambda v: np.repeat(v[:, None], LANES, axis=1).astype(np.float32)
+    table = np.concatenate(blocks).astype(np.float32)
+    high = table.astype(jnp.bfloat16)
+    low = (table - high.astype(np.float32)).astype(jnp.bfloat16)
+    return np.concatenate([high, low, high], axis=1), wide(rise), wide(fall)
 
 
 def coupled(triple, tiles):
@@ -130,9 +133,10 @@
     band = ((place >= centre - band_half) & (place < centre + band_half)).astype(jnp.float32)
     active = (fires == float(step)).astype(jnp.float32)
     right = voltage + time_step * (amplitude * band * active - current)
-    size = nodes + SUB
-    table = table_ref[pl.ds(pl.multiple_of(shard * size, SUB), size), :]
-    return jnp.dot(table, right, preferred_element_type=jnp.float32, precision=HIGHEST)
+    high, low = split(right)
+    return jnp.dot(
+        table_ref[...], jnp.concatenate([high, high, low], axis=0), preferred_element_type=jnp.float32
+    )
 
 
 def far_sums(sums, target):
@@ -146,39 +150,38 @@
     return below, above
 
 
-def from_far(rise_ref, fall_ref, start, count, below, above):
-    here = pl.ds(pl.multiple_of(start, SUB), count)
-    return rise_ref[here, :] * above + fall_ref[here, :] * below
-
-
-def first_step(sizes, states, voltage, tissue, tables, coupling, decay, gain, weight, unit, fire, home,
-               cell):
-    shards, emg, rows, depth = sizes
+def from_far(rise_ref, fall_ref, below, above):
+    return rise_ref[...] * above + fall_ref[...] * below
+
+
+def first_step(shards, states, voltage, tissue, table, rows, coupling, decay, gain, weight, unit, fire):
     number, nodes, fibres = states.shape
     tall = -(-number // 16) * 16
     full = number // SUB * SUB
     mu = fire.shape[1]
+    face = 2 * rows
+    own_rows = table.shape[0] // shards
     small = [coupling, decay, gain, weight, unit, fire, voltage]
-    large = [*tables, tissue, home, cell]
-    count = len(small) + len(large)
+    count = len(small) + 3
     chunk = nodes // 2
 
     def body(*refs):
         small_refs, refs = refs[:len(small)], refs[len(small):]
-        large_refs, refs = refs[:len(large)], refs[len(large):]
-        states_ref, refs = refs[0], refs[1:]
-        states_out, solved_ref, current_ref, sums_ref, triple_ref, param_ref, misc_ref = refs[:7]
-        table_out, tissue_out, rise_out, fall_out = refs[7:11]
-        *stages, home_ref, cell_ref, nodes_ref, sems = refs[11:]
+        table_ref, tissue_ref, states_ref, *refs = refs
+        states_out, solved_ref, current_ref, sums_ref, triple_ref, param_ref, fires_ref = refs[:7]
+        table_out, faces_ref, *stages, nodes_ref, sems = refs[7:]
+        shard = lax.axis_index("len")
         nodes_ref[:, full:, :] = jnp.zeros((nodes, tall - full, fibres), jnp.float32)
+        here = pl.ds(pl.multiple_of(shard * own_rows, 2 * SUB), own_rows)
+        pieces = [
+            *zip(small_refs, stages),
+            (table_ref.at[here], table_out),
+            (tissue_ref.at[pl.ds(0, face)], faces_ref.at[pl.ds(0, face)]),
+            (tissue_ref.at[pl.ds(tissue.shape[0] - face, face)], faces_ref.at[pl.ds(face, face)]),
+        ]
         copies = [
             pltpu.make_async_copy(source, target, sems.at[i])
-            for i, (source, target) in enumerate(
-                zip(
-                    (*small_refs, *large_refs),
-                    (*stages, table_out, rise_out, fall_out, tissue_out, home_ref, cell_ref),
-                )
-            )
+            for i, (source, target) in enumerate(pieces)
         ]
         loads = [
             pltpu.make_async_copy(
@@ -206,6 +209,7 @@
         match = (iota((mu, fibres), 0) == unit_ref[...]).astype(jnp.bfloat16)
         fires = jnp.broadcast_to(fire_ref[...].astype(jnp.float32), (SUB, mu)).astype(jnp.bfloat16)
         fires = jnp.dot(fires, match, preferred_element_type=jnp.float32)
+        fires_ref[...] = fires
         for begin in range(0, nodes, chunk):
             here = nodes_ref.at[pl.ds(begin, chunk), pl.ds(0, number), :]
             pltpu.make_async_copy(here, here, sems.at[count + begin // chunk]).wait()
@@ -217,68 +221,85 @@
                     )
         for copy in copies[len(small):]:
             copy.wait()
-        solved = cable(
-            voltage_ref[...], current_ref[...], fires[0:1], 0, table_out, lax.axis_index("len"), shards
-        )
+        solved = cable(voltage_ref[...], current_ref[...], fires[0:1], 0, table_out, shard, shards)
         solved_ref[...] = solved[:nodes]
-        sums_ref[...] = solved[nodes:]
-        brick, spot = home_ref[...], cell_ref[...]
-        row = (brick // emg) * rows + spot // depth
-        column = (brick % emg) * depth + spot % depth
-        line = iota((SUB, fibres), 0)
-        out = jnp.where(line == 0, row.astype(jnp.float32), column.astype(jnp.float32))
-        misc_ref[...] = jnp.where(line == 2, fires, out)
-
-    args = (*small, *large, states)
+        sums_ref[...] = solved[nodes:nodes + SUB]
+
+    args = (*small, table, tissue, states)
     return kernel_call(
         body,
         [(nodes, tall, fibres), (nodes, fibres), (nodes, fibres), (SUB, fibres),
          ((tall, 3 * tall), jnp.bfloat16), (3, tall, fibres), (SUB, fibres),
-         tables[0].shape, tissue.shape, *(t.shape for t in tables[1:])],
+         ((own_rows, table.shape[1]), table.dtype), (2 * face, tissue.shape[1])],
         *args,
         hbm_ins=range(len(args)),
         scratch=[
             *(pltpu.VMEM(a.shape, a.dtype) for a in small),
-            pltpu.VMEM(home.shape, home.dtype),
-            pltpu.VMEM(cell.shape, cell.dtype),
             pltpu.VMEM((nodes, tall, fibres), jnp.float32),
             pltpu.SemaphoreType.DMA((count + nodes // chunk,)),
         ],
     )
 
 
-def coupled_all(states, triple):
-    nodes = states.shape[0]
-
-    def body(states_ref, triple_ref, out_ref):
+def coupled_all(sizes, states, triple, tissue, tables, home, cell):
+    shards, emg, rows, depth = sizes
+    nodes, _, fibres = states.shape
+
+    def body(states_ref, triple_ref, *refs):
+        tissue_ref, rise_ref, fall_ref, home_ref, cell_ref, *refs = refs
+        out_ref, misc_ref, tissue_out, rise_out, fall_out, home_in, cell_in, sems = refs
+        here = pl.ds(pl.multiple_of(lax.axis_index("len") * nodes, SUB), nodes)
+        pieces = [
+            (home_ref, home_in), (cell_ref, cell_in), (tissue_ref, tissue_out),
+            (rise_ref.at[here], rise_out), (fall_ref.at[here], fall_out),
+        ]
+        copies = [
+            pltpu.make_async_copy(source, target, sems.at[i])
+            for i, (source, target) in enumerate(pieces)
+        ]
+        for copy in copies:
+            copy.start()
         triple = triple_ref[...]
         for start in range(0, nodes, SUB):
             drives = coupled(triple, [states_ref[n] for n in range(start, start + SUB)])
             for n, drive in zip(range(start, start + SUB), drives):
                 out_ref[n] = drive
-
-    return kernel_call(body, [states.shape], states, triple, cost=0.7)[0]
-
-
-def second_step(fib, states, drive, solved, current, param, misc, rise, fall, near, wide, ends, rows):
+        for copy in copies:
+            copy.wait()
+        brick, spot = home_in[...], cell_in[...]
+        row = (brick // emg) * rows + spot // depth
+        column = (brick % emg) * depth + spot % depth
+        line = iota((SUB, fibres), 0)
+        misc_ref[...] = jnp.where(line == 0, row.astype(jnp.float32), column.astype(jnp.float32))
+
+    return kernel_call(
+        body,
+        [states.shape, (SUB, fibres), tissue.shape, (nodes, fibres), (nodes, fibres)],
+        states, triple, tissue, *tables, home, cell,
+        cost=0.7,
+        hbm_ins=range(2, 7),
+        scratch=[
+            pltpu.VMEM(home.shape, home.dtype),
+            pltpu.VMEM(cell.shape, cell.dtype),
+            pltpu.SemaphoreType.DMA((5,)),
+        ],
+    )
+
+
+def second_step(states, drive, solved, current, param, misc, rise, fall, near, ends):
     nodes, tall, fibres = states.shape
     cells = nodes // NPC
     shards = len(near)
-    long = wide.shape[0] // rows
-    layers = 2 * long
     flows = STEPS * cells
     size = flows + SUB
-    both = size + ends.shape[0]
 
     def body(states_ref, drive_ref, solved_ref, current_ref, param_ref, misc_ref, rise_ref, fall_ref,
-             wide_ref, lanes_ref, *rest):
+             lanes_ref, *rest):
         near_refs, rest = rest[:shards], rest[shards:]
-        states_out, volt_ref, flow_ref, send_ref, ends_ref, *face_refs, line_ref = rest
+        states_out, volt_ref, flow_ref, send_ref, ends_ref, line_ref = rest
         shard = lax.axis_index("len")
         below, above = far_sums({k: ref[0:2, :] for k, ref in enumerate(near_refs)}, shard)
-        volt_ref[...] = solved_ref[...] + from_far(
-            rise_ref, fall_ref, SUB + shard * nodes, nodes, below, above
-        )
+        volt_ref[...] = solved_ref[...] + from_far(rise_ref, fall_ref, below, above)
         line_ref[0:nodes, :] = current_ref[...]
         for n in range(nodes):
             states_out[n], line_ref[nodes + n:nodes + n + 1, :] = advanced(
@@ -288,22 +309,30 @@
         binned = line_ref[pl.ds(0, flows, stride=NPC), :]
         for k in range(1, NPC):
             binned = binned + line_ref[pl.ds(k, flows, stride=NPC), :]
-        for ref in (send_ref, ends_ref, *face_refs):
+        for ref in (send_ref, ends_ref):
             ref[0:flows, :] = binned
             ref[flows:size, :] = misc_ref[...]
-        for ref in (ends_ref, *face_refs):
-            ref[size:both, :] = lanes_ref[...]
-        first, last = wide_ref[0:layers, :], wide_ref[rows * long - layers:, :]
-        for ref, k in zip(face_refs, facing(fib)):
-            ref[both:, :] = for_partner(lax.axis_index("fib"), k, first, last)
+        ends_ref[size:, :] = lanes_ref[...]
 
     return kernel_call(
         body,
-        [states.shape, (nodes, fibres), (nodes, fibres), (size, fibres), (both, fibres)]
-        + [(both + layers, fibres)] * len(facing(fib)),
-        states, drive, solved, current, param, misc, rise, fall, wide, ends, *near,
+        [states.shape, (nodes, fibres), (nodes, fibres), (size, fibres), (size + ends.shape[0], fibres)],
+        states, drive, solved, current, param, misc, rise, fall, ends, *near,
         scratch=[pltpu.VMEM((STEPS * nodes, fibres), jnp.float32)],
     )
+
+
+def with_outer(fib, block, wide, rows):
+    at, depth = block.shape
+    layers = 2 * (wide.shape[0] // rows)
+
+    def body(block_ref, wide_ref, *refs):
+        first, last = wide_ref[0:layers, :], wide_ref[wide.shape[0] - layers:, :]
+        for ref, k in zip(refs, facing(fib)):
+            ref[0:at, :] = block_ref[...]
+            ref[at:, :] = for_partner(lax.axis_index("fib"), k, first, last)
+
+    return kernel_call(body, [(at + layers, depth)] * len(facing(fib)), block, wide)
 
 
 def last_solve(shards, voltage, current, misc, table):
@@ -311,11 +340,11 @@
 
     def body(voltage_ref, current_ref, misc_ref, table_ref, solved_ref, sums_ref):
         solved = cable(
-            voltage_ref[...], current_ref[...], misc_ref[2:3, :], STEPS - 1, table_ref,
+            voltage_ref[...], current_ref[...], misc_ref[0:1, :], STEPS - 1, table_ref,
             lax.axis_index("len"), shards,
         )
         solved_ref[...] = solved[:nodes]
-        sums_ref[...] = solved[nodes:]
+        sums_ref[...] = solved[nodes:nodes + SUB]
 
     return kernel_call(body, [(nodes, fibres), (SUB, fibres)], voltage, current, misc, table)
 
@@ -382,17 +411,17 @@
     )
 
 
-def with_faces(shards, sums, tissue, rows):
-    face = 2 * rows
+def with_faces(shards, sums, ends):
+    face = ends.shape[0] // 2
 
     def body(sums_ref, tissue_ref, *refs):
-        first, last = tissue_ref[0:face, :], tissue_ref[tissue.shape[0] - face:, :]
+        first, last = tissue_ref[0:face, :], tissue_ref[face:, :]
         for ref, k in zip(refs, facing(shards)):
             ref[0:SUB, :] = sums_ref[...]
             ref[SUB:, :] = for_partner(lax.axis_index("len"), k, first, last)
 
-    edge = (SUB + face, tissue.shape[1])
-    return kernel_call(body, [edge] * len(facing(shards)), sums, tissue)
+    edge = (SUB + face, ends.shape[1])
+    return kernel_call(body, [edge] * len(facing(shards)), sums, ends)
 
 
 def widened(tissue, near, rows):
@@ -590,9 +619,7 @@
         below, far = far_sums(
             {**{k: ref[0:4, :] for k, ref in pair_refs.items()}, 0: sums_ref[0:4, :]}, shard
         )
-        volt_ref[...] = solved_ref[...] + from_far(
-            rise_ref, fall_ref, SUB + shard * nodes, nodes, below, far
-        )
+        volt_ref[...] = solved_ref[...] + from_far(rise_ref, fall_ref, below, far)
         copies = [pltpu.make_async_copy(volt_ref, voltage_out, sems.at[STEPS])]
         copies[0].start()
         before, after = beside("len", near_refs, slice(SUB, None))
@@ -732,20 +759,23 @@
     shards, fib, emg = (lax.axis_size(a) for a in ("len", "fib", "emg"))
     line = lambda v: v.reshape(1, v.size)
     tables = [jnp.asarray(t) for t in cable_tables(nodes * shards, shards)]
-    states, solved, current, sums, triple, param, misc, table, flat, rise, fall = first_step(
-        (shards, emg, rows, depth), states, voltage, tissue.reshape(cells * rows, depth), tables,
+    flat = tissue.reshape(cells * rows, depth)
+    states, solved, current, sums, triple, param, fires, table, faces = first_step(
+        shards, states, voltage, flat, tables[0], rows,
         coupling, line(decay_rates), line(volt_gain), line(current_weights),
-        line(motor_unit), line(stim_step), line(fibre_home), line(cross_cell),
-    )
-    drive = coupled_all(states, triple)
-    faces = list(with_faces(shards, sums, flat, rows))
-    near = swaps("len", sums, faces)
+        line(motor_unit), line(stim_step),
+    )
+    near = swaps("len", sums, with_faces(shards, sums, faces))
     flows = STEPS * cells
+    drive, misc, flat, rise, fall = coupled_all(
+        (shards, emg, rows, depth), states, triple, flat, tables[1:], line(fibre_home), line(cross_cell)
+    )
     wide, ends = widened(flat, near, rows)
     size = flows + SUB
-    states, volt, flow, send, with_ends, *with_layers = second_step(
-        fib, states, drive, solved, current, param, misc, rise, fall, near, wide, ends, rows
-    )
+    states, volt, flow, send, with_ends = second_step(
+        states, drive, solved, current, param, misc, rise, fall, near, ends
+    )
+    with_layers = with_outer(fib, with_ends, wide, rows)
     blocks = {(k, 0): block for k, block in enumerate(swaps("fib", send, with_layers))}
     across = swaps("emg", send, [with_ends] * len(facing(emg)))
     for m in range(1, emg):
@@ -758,7 +788,7 @@
     keys = sorted(blocks, key=lambda key: (all(key), key))
     count_early = sum(not all(key) for key in keys)
     got = [blocks[key] for key in keys]
-    solved, sums = last_solve(shards, volt, flow, misc, table)
+    solved, sums = last_solve(shards, volt, flow, fires, table)
     diag, mask = operator_terms((shards, fib, emg), size, ends.shape[0], wide, blocks, rows)
     _, ahead = lax.optimization_barrier((across, sums))
     other = xor_swap(ahead, "len", 1)

time: 30.9 us -> 30.8 us (level)
  waiting for transfers between devices: 7.25 us -> 6.46 us
  Pallas kernels: 10.5 us -> 11.1 us
    ppermute x13, waiting for transfers between devices: 7.25 us -> 6.46 us  [xor_swap(): lax.ppermute(value, axis, [(i, i ^ k) for i in range(lax.axis_size(axis))])]
    pallas_call x14 -> x15, Pallas kernels: 10.5 us -> 11.1 us  [kernel_call(): pl.pallas_call(body, out_shape=shapes, in_specs=[HBM if i in hbm_ins else...]
  transfers between devices with their start and end apart: 13 -> 13, of which waited for: 7 -> 6; matrix products, arithmetic and copies ran while one was open for 0% -> 0% of each run, Pallas kernels for 13% -> 16%
where the time goes in v5:
time: 30.8 us; the launch traced here: 30.6 us
  starting transfers between devices  12.2 us (40%)
  Pallas kernels  11.1 us (36%)
  waiting for transfers between devices  6.46 us (21%)
  between operations  0.75 us (2%)
    ppermute x13, starting transfers between devices, xor_swap(): lax.ppermute(value, axis, [(i, i ^ k) for i in range(lax.axis_size(axis))])  12.2 us
    pallas_call x15, Pallas kernels, kernel_call(): pl.pallas_call(body, out_shape=shapes, in_specs=[HBM if i in hbm_ins else...  11.1 us
    ppermute x13, waiting for transfers between devices, xor_swap(): lax.ppermute(value, axis, [(i, i ^ k) for i in range(lax.axis_size(axis))])  6.46 us
  transfers between devices with their start and end apart: 13, of which 6 were waited for; matrix products, arithmetic and copies ran while one was open for 0% of the time, Pallas kernels for 16%

profile of v5, /device:TPU:0, one launch (start us, length us, event | category | flops | bytes accessed | tf_op | source)
XLA Modules:
  0.0 30.6 jit_solution(3219638198434289091)
XLA Ops:
  0.6 2.8 %shard_map.157 = (f32[64,64,128]{2,1,0:T(8,128)S(1)}, f32[64,128]{1,0:T(8,128)S(1)}, f32[64,128]{1,0:T(8,128)S(1)}, f32[8,128]{1,0:T(8,128)S(1)}, bf16[64,192]{1...) custom-call(f32[57,57]{1,0:T(8,128)} %refs_0_.1, ...), custom_call_target="tpu_custom_call" | custom-call | tf_op jit(solution)/shard_map/pallas_call | solution.py:43
  3.4 3.0 %collective-permute-start.1 = (f32[8,128]{1,0:T(8,128)S(1)}, f32[8,128]{1,0:T(8,128)S(1)}, u32[]{:S(2)}, u32[]{:S(2)}) collective-permute-start(f32[8,128]{1,0:T(8,128)S(1)} %get-tuple-element.64.sums_ref.rest_0_), channel_id=1, source_target_pairs={{0,8},{4,12},{8,0},{12,4},{1,9},{5,13},{9,1},{13,5},{2,10},{6,14},... | collective-permute-start | bytes 12296 | tf_op jit(solution)/shard_map/ppermute | solution.py:735
  6.4 0.0 collective-permute-start
  6.4 0.2 collective-permute-start.2
  6.6 1.5 %shard_map.158 = (f32[64,64,128]{2,1,0:T(8,128)S(1)}, f32[8,128]{1,0:T(8,128)S(1)}, f32[256,128]{1,0:T(8,128)S(1)}, f32[64,128]{1,0:T(8,128)S(1)}, f32[64,128]{1,0:T(8,128)S(1)}) custom-call(f32[64,64,128]{2,1,0:T(8,128)S(1)} %get-tuple-element.54.states_ref, bf16[64,192]{1,0:T(8,128)(2,1)S(1)} %get-tuple-element.55.triple_ref, f32[256,128]{1,0:T(8,128)} %bitcast.10, ...), custom_call_target="tpu_custom_call" | custom-call | flops 700000000 | bytes 65536 | tf_op jit(solution)/shard_map/pallas_call | solution.py:43
  8.2 0.0 collective-permute-done.1.rest_2_
  8.2 0.0 collective-permute-done.rest_1_
  8.2 1.4 %collective-permute-done.2.rest_3_ = f32[24,128]{1,0:T(8,128)S(1)} collective-permute-done((f32[24,128]{1,0:T(8,128)S(1)}, f32[24,128]{1,0:T(8,128)S(1)}, u32[]{:S(2)}, u32[]{:S(2)}) %collective-permute-start.2) | collective-permute-done | bytes 12320 | tf_op jit(solution)/shard_map/ppermute | solution.py:735
  9.6 0.2 shard_map.160
  9.8 0.7 %shard_map.161 = (f32[64,64,128]{2,1,0:T(8,128)S(1)}, f32[64,128]{1,0:T(8,128)S(1)}, f32[64,128]{1,0:T(8,128)S(1)}, f32[72,128]{1,0:T(8,128)S(1)}, f32[88,128]{1,0:T(8,128)S(1)}) custom-call(f32[64,64,128]{2,1,0:T(8,128)S(1)} %get-tuple-element.54.states_ref, f32[64,64,128]{2,1,0:T(8,128)S(1)} %get-tuple-element.56.drive_ref, ...), custom_call_target="tpu_custom_call" | custom-call | tf_op jit(solution)/shard_map/pallas_call | solution.py:43
  10.5 1.6 %collective-permute-start.6 = (f32[168,128]{1,0:T(8,128)S(1)}, f32[168,128]{1,0:T(8,128)S(1)}, u32[]{:S(2)}, u32[]{:S(2)}) collective-permute-start(f32[168,128]{1,0:T(8,128)S(1)} %shard_map.162), channel_id=1, source_target_pairs={{0,16},{16,0},{1,17},{17,1},{2,18},{18,2},{3,19},{19,3},{4,20},{20... | collective-permute-start | bytes 258056 | tf_op jit(solution)/shard_map/ppermute | solution.py:735
  12.1 3.6 %collective-permute-start.5 = (f32[88,128]{1,0:T(8,128)S(1)}, f32[88,128]{1,0:T(8,128)S(1)}, u32[]{:S(2)}, u32[]{:S(2)}) collective-permute-start(f32[88,128]{1,0:T(8,128)S(1)} %get-tuple-element.70.block_ref), channel_id=1, source_target_pairs={{0,3},{1,2},{2,1},{3,0},{4,7},{5,6},{6,5},{7,4},{8,11},{9,10},{10,... | collective-permute-start | bytes 135176 | tf_op jit(solution)/shard_map/ppermute | solution.py:735
  15.7 0.0 collective-permute-start.4
  15.7 0.8 %collective-permute-start.3 = (f32[88,128]{1,0:T(8,128)S(1)}, f32[88,128]{1,0:T(8,128)S(1)}, u32[]{:S(2)}, u32[]{:S(2)}) collective-permute-start(f32[88,128]{1,0:T(8,128)S(1)} %get-tuple-element.70.block_ref), channel_id=1, source_target_pairs={{0,1},{1,0},{2,3},{3,2},{4,5},{5,4},{6,7},{7,6},{8,9},{9,8},{10,11... | collective-permute-start | bytes 135176 | tf_op jit(solution)/shard_map/ppermute | solution.py:735
  16.4 1.5 %collective-permute-done.5.refs_3_.refs_1_.rest_3_ = f32[88,128]{1,0:T(8,128)S(1)} collective-permute-done((f32[88,128]{1,0:T(8,128)S(1)}, f32[88,128]{1,0:T(8,128)S(1)}, u32[]{:S(2)}, u32[]{:S(2)}) %collective-permute-start.5) | collective-permute-done | bytes 45088 | tf_op jit(solution)/shard_map/ppermute | solution.py:735
  18.0 0.5 %collective-permute-start.9 = (f32[88,128]{1,0:T(8,128)S(1)}, f32[88,128]{1,0:T(8,128)S(1)}, u32[]{:S(2)}, u32[]{:S(2)}) collective-permute-start(f32[88,128]{1,0:T(8,128)S(1)} %collective-permute-done.5.refs_3_.refs_1_.rest_3_), channel_id=1, source_target_pairs={{0,16},{16,0},{1,17},{17,1},{2,18},{18,2},{3,19},{19,3},{4,20},{20... | collective-permute-start | bytes 135176 | tf_op jit(solution)/shard_map/ppermute | solution.py:735
  18.5 0.0 collective-permute-done.6.block_ref.refs_4_.refs_2_.rest_4_
  18.5 1.1 %collective-permute-start.7 = (f32[88,128]{1,0:T(8,128)S(1)}, f32[88,128]{1,0:T(8,128)S(1)}, u32[]{:S(2)}, u32[]{:S(2)}) collective-permute-start(f32[88,128]{1,0:T(8,128)S(1)} %shard_map.163), channel_id=1, source_target_pairs={{0,1},{1,0},{2,3},{3,2},{4,5},{5,4},{6,7},{7,6},{8,9},{9,8},{10,11... | collective-permute-start | bytes 135176 | tf_op jit(solution)/shard_map/ppermute | solution.py:735
  19.6 0.9 %collective-permute-done.4.refs_2_.rest_2_ = f32[72,128]{1,0:T(8,128)S(1)} collective-permute-done((f32[72,128]{1,0:T(8,128)S(1)}, f32[72,128]{1,0:T(8,128)S(1)}, u32[]{:S(2)}, u32[]{:S(2)}) %collective-permute-start.4) | collective-permute-done | bytes 36896 | tf_op jit(solution)/shard_map/ppermute | solution.py:735
  20.6 0.6 %collective-permute-start.8 = (f32[72,128]{1,0:T(8,128)S(1)}, f32[72,128]{1,0:T(8,128)S(1)}, u32[]{:S(2)}, u32[]{:S(2)}) collective-permute-start(f32[72,128]{1,0:T(8,128)S(1)} %collective-permute-done.4.refs_2_.rest_2_), channel_id=1, source_target_pairs={{0,16},{16,0},{1,17},{17,1},{2,18},{18,2},{3,19},{19,3},{4,20},{20... | collective-permute-start | bytes 110600 | tf_op jit(solution)/shard_map/ppermute | solution.py:735
  21.1 0.1 shard_map.165
  21.3 0.0 collective-permute-done.3.refs_1_.refs_0_.rest_1_
  21.3 0.1 collective-permute-start.10
  21.4 1.0 %shard_map.164 = (f32[896,256]{1,0:T(8,128)S(1)}, bf16[256,640]{1,0:T(8,128)(2,1)S(1)}) custom-call(f32[72,128]{1,0:T(8,128)S(1)} %get-tuple-element.85.refs_0_.rest_0_, f32[88,128]{1,0:T(8,128)S(1)} %collective-permute-done.3.refs_1_.refs_0_.rest_1_, f32[72,128]{1,0:T(8,128)S(1)} %collective-permute-done.4.refs_2_.rest_2_, ...), custom_call_target="tpu_custom_call" | custom-call | tf_op jit(solution)/shard_map/pallas_call | solution.py:43
  22.4 0.2 collective-permute-done.10.other_ref
  22.5 2.0 %collective-permute-done.8.refs_1_.refs_6_.rest_6_ = f32[72,128]{1,0:T(8,128)S(1)} collective-permute-done((f32[72,128]{1,0:T(8,128)S(1)}, f32[72,128]{1,0:T(8,128)S(1)}, u32[]{:S(2)}, u32[]{:S(2)}) %collective-permute-start.8) | collective-permute-done | bytes 36896 | tf_op jit(solution)/shard_map/ppermute | solution.py:735
  24.5 0.0 collective-permute-done.9.refs_2_.refs_7_.refs_4_.rest_7_
  24.5 0.0 collective-permute-done.7.refs_0_.refs_5_.refs_3_.rest_5_
  24.6 0.1 collective-permute-start.11
  24.6 0.7 %collective-permute-start.12 = (f32[72,128]{1,0:T(8,128)S(1)}, f32[72,128]{1,0:T(8,128)S(1)}, u32[]{:S(2)}, u32[]{:S(2)}) collective-permute-start(f32[72,128]{1,0:T(8,128)S(1)} %get-tuple-element.102), channel_id=1, source_target_pairs={{0,4},{4,0},{8,12},{12,8},{1,5},{5,1},{9,13},{13,9},{2,6},{6,2},{1... | collective-permute-start | bytes 110600 | tf_op jit(solution)/shard_map/ppermute | solution.py:735
  25.3 1.2 %shard_map.169 = f32[57,64,128]{2,1,0:T(8,128)} custom-call(f32[64,64,128]{2,1,0:T(8,128)S(1)} %get-tuple-element.93.states_ref), custom_call_target="tpu_custom_call" | custom-call | tf_op jit(solution)/shard_map/pallas_call | solution.py:43
  26.5 0.7 %shard_map.166 = (f32[896,256]{1,0:T(8,128)S(1)}, bf16[256,384]{1,0:T(8,128)(2,1)S(1)}) custom-call(f32[88,128]{1,0:T(8,128)S(1)} %collective-permute-done.7.refs_0_.refs_5_.refs_3_.rest_5_, f32[72,128]{1,0:T(8,128)S(1)} %collective-permute-done.8.refs_1_.refs_6_.rest_6_, f32[88,128]{1,0:T(8,128)S(1)} %collective-permute-done.9.refs_2_.refs_7_.refs_4_.rest_7_, ...), custom_call_target="tpu_custom_call" | custom-call | tf_op jit(solution)/shard_map/pallas_call | solution.py:43
  27.2 0.3 %shard_map.170 = (f32[960,256]{1,0:T(8,128)S(1)}, f32[80,256]{1,0:T(8,128)S(1)}) custom-call(f32[320,128]{1,0:T(8,128)S(1)} %get-tuple-element.71.wide_ref, f32[88,128]{1,0:T(8,128)S(1)} %collective-permute-done.3.refs_1_.refs_0_.rest_1_, f32[88,128]{1,0:T(8,128)S(1)} %collective-permute-done.5.refs_3_.refs_1_.rest_3_, ...), custom_call_target="tpu_custom_call" | custom-call | tf_op jit(solution)/shard_map/pallas_call | solution.py:43
  27.6 0.4 %collective-permute-done.11.rest_11_ = f32[72,128]{1,0:T(8,128)S(1)} collective-permute-done((f32[72,128]{1,0:T(8,128)S(1)}, f32[72,128]{1,0:T(8,128)S(1)}, u32[]{:S(2)}, u32[]{:S(2)}) %collective-permute-start.11) | collective-permute-done | bytes 36896 | tf_op jit(solution)/shard_map/ppermute | solution.py:735
  28.0 0.0 collective-permute-done.12.rest_12_
  28.0 2.5 %shard_map.171 = (f32[512,128]{1,0:T(8,128)}, f32[64,128]{1,0:T(8,128)}) custom-call(f32[896,256]{1,0:T(8,128)S(1)} %get-tuple-element.95.own_ref, f32[960,256]{1,0:T(8,128)S(1)} %get-tuple-element.96.diag_ref, f32[80,256]{1,0:T(8,128)S(1)} %get-tuple-element.97.mask_ref, f32[64,128]{1,0:T(8,128)S(1)} %get-tuple-element.98.solved_ref, ...), custom_call_target="tpu_custom_call" | custom-call | tf_op jit(solution)/shard_map/pallas_call | solution.py:43
  (5 shorter events, 0.0 us)
Async XLA Ops:
  3.4 4.8 %collective-permute-start.1 = (f32[8,128]{1,0:T(8,128)S(1)}, f32[8,128]{1,0:T(8,128)S(1)}, u32[]{:S(2)}, u32[]{:S(2)}) collective-permute-start(f32[8,128]{1,0:T(8,128)S(1)} %get-tuple-element.64.sums_ref.rest_0_), channel_id=1, source_target_pairs={{0,8},{4,12},{8,0},{12,4},{1,9},{5,13},{9,1},{13,5},{2,10},{6,14},... | collective-permute-start | bytes 12296 | tf_op jit(solution)/shard_map/ppermute | solution.py:735
  6.4 1.8 %collective-permute-start = (f32[24,128]{1,0:T(8,128)S(1)}, f32[24,128]{1,0:T(8,128)S(1)}, u32[]{:S(2)}, u32[]{:S(2)}) collective-permute-start(f32[24,128]{1,0:T(8,128)S(1)} %get-tuple-element.66), channel_id=1, source_target_pairs={{0,4},{4,0},{8,12},{12,8},{1,5},{5,1},{9,13},{13,9},{2,6},{6,2},{1... | collective-permute-start | bytes 36872 | tf_op jit(solution)/shard_map/ppermute | solution.py:735
  6.4 3.2 %collective-permute-start.2 = (f32[24,128]{1,0:T(8,128)S(1)}, f32[24,128]{1,0:T(8,128)S(1)}, u32[]{:S(2)}, u32[]{:S(2)}) collective-permute-start(f32[24,128]{1,0:T(8,128)S(1)} %get-tuple-element.67), channel_id=1, source_target_pairs={{0,12},{4,8},{8,4},{12,0},{1,13},{5,9},{9,5},{13,1},{2,14},{6,10},... | collective-permute-start | bytes 36872 | tf_op jit(solution)/shard_map/ppermute | solution.py:735
  10.5 8.0 %collective-permute-start.6 = (f32[168,128]{1,0:T(8,128)S(1)}, f32[168,128]{1,0:T(8,128)S(1)}, u32[]{:S(2)}, u32[]{:S(2)}) collective-permute-start(f32[168,128]{1,0:T(8,128)S(1)} %shard_map.162), channel_id=1, source_target_pairs={{0,16},{16,0},{1,17},{17,1},{2,18},{18,2},{3,19},{19,3},{4,20},{20... | collective-permute-start | bytes 258056 | tf_op jit(solution)/shard_map/ppermute | solution.py:735
  12.1 5.9 %collective-permute-start.5 = (f32[88,128]{1,0:T(8,128)S(1)}, f32[88,128]{1,0:T(8,128)S(1)}, u32[]{:S(2)}, u32[]{:S(2)}) collective-permute-start(f32[88,128]{1,0:T(8,128)S(1)} %get-tuple-element.70.block_ref), channel_id=1, source_target_pairs={{0,3},{1,2},{2,1},{3,0},{4,7},{5,6},{6,5},{7,4},{8,11},{9,10},{10,... | collective-permute-start | bytes 135176 | tf_op jit(solution)/shard_map/ppermute | solution.py:735
  15.7 4.9 %collective-permute-start.4 = (f32[72,128]{1,0:T(8,128)S(1)}, f32[72,128]{1,0:T(8,128)S(1)}, u32[]{:S(2)}, u32[]{:S(2)}) collective-permute-start(f32[72,128]{1,0:T(8,128)S(1)} %get-tuple-element.85.refs_0_.rest_0_), channel_id=1, source_target_pairs={{0,2},{1,3},{2,0},{3,1},{4,6},{5,7},{6,4},{7,5},{8,10},{9,11},{10,... | collective-permute-start | bytes 110600 | tf_op jit(solution)/shard_map/ppermute | solution.py:735
  15.7 5.6 %collective-permute-start.3 = (f32[88,128]{1,0:T(8,128)S(1)}, f32[88,128]{1,0:T(8,128)S(1)}, u32[]{:S(2)}, u32[]{:S(2)}) collective-permute-start(f32[88,128]{1,0:T(8,128)S(1)} %get-tuple-element.70.block_ref), channel_id=1, source_target_pairs={{0,1},{1,0},{2,3},{3,2},{4,5},{5,4},{6,7},{7,6},{8,9},{9,8},{10,11... | collective-permute-start | bytes 135176 | tf_op jit(solution)/shard_map/ppermute | solution.py:735
  18.0 6.6 %collective-permute-start.9 = (f32[88,128]{1,0:T(8,128)S(1)}, f32[88,128]{1,0:T(8,128)S(1)}, u32[]{:S(2)}, u32[]{:S(2)}) collective-permute-start(f32[88,128]{1,0:T(8,128)S(1)} %collective-permute-done.5.refs_3_.refs_1_.rest_3_), channel_id=1, source_target_pairs={{0,16},{16,0},{1,17},{17,1},{2,18},{18,2},{3,19},{19,3},{4,20},{20... | collective-permute-start | bytes 135176 | tf_op jit(solution)/shard_map/ppermute | solution.py:735
  18.5 6.1 %collective-permute-start.7 = (f32[88,128]{1,0:T(8,128)S(1)}, f32[88,128]{1,0:T(8,128)S(1)}, u32[]{:S(2)}, u32[]{:S(2)}) collective-permute-start(f32[88,128]{1,0:T(8,128)S(1)} %shard_map.163), channel_id=1, source_target_pairs={{0,1},{1,0},{2,3},{3,2},{4,5},{5,4},{6,7},{7,6},{8,9},{9,8},{10,11... | collective-permute-start | bytes 135176 | tf_op jit(solution)/shard_map/ppermute | solution.py:735
  20.6 4.0 %collective-permute-start.8 = (f32[72,128]{1,0:T(8,128)S(1)}, f32[72,128]{1,0:T(8,128)S(1)}, u32[]{:S(2)}, u32[]{:S(2)}) collective-permute-start(f32[72,128]{1,0:T(8,128)S(1)} %collective-permute-done.4.refs_2_.rest_2_), channel_id=1, source_target_pairs={{0,16},{16,0},{1,17},{17,1},{2,18},{18,2},{3,19},{19,3},{4,20},{20... | collective-permute-start | bytes 110600 | tf_op jit(solution)/shard_map/ppermute | solution.py:735
  21.3 1.2 %collective-permute-start.10 = (f32[8,128]{1,0:T(8,128)S(1)}, f32[8,128]{1,0:T(8,128)S(1)}, u32[]{:S(2)}, u32[]{:S(2)}) collective-permute-start(f32[8,128]{1,0:T(8,128)S(1)} %get-tuple-element.78.sums_ref), channel_id=1, source_target_pairs={{0,4},{4,0},{8,12},{12,8},{1,5},{5,1},{9,13},{13,9},{2,6},{6,2},{1... | collective-permute-start | bytes 12296 | tf_op jit(solution)/shard_map/ppermute | solution.py:735
  24.6 3.4 %collective-permute-start.11 = (f32[72,128]{1,0:T(8,128)S(1)}, f32[72,128]{1,0:T(8,128)S(1)}, u32[]{:S(2)}, u32[]{:S(2)}) collective-permute-start(f32[72,128]{1,0:T(8,128)S(1)} %get-tuple-element.101), channel_id=1, source_target_pairs={{0,12},{4,8},{8,4},{12,0},{1,13},{5,9},{9,5},{13,1},{2,14},{6,10},... | collective-permute-start | bytes 110600 | tf_op jit(solution)/shard_map/ppermute | solution.py:735
  24.6 3.4 %collective-permute-start.12 = (f32[72,128]{1,0:T(8,128)S(1)}, f32[72,128]{1,0:T(8,128)S(1)}, u32[]{:S(2)}, u32[]{:S(2)}) collective-permute-start(f32[72,128]{1,0:T(8,128)S(1)} %get-tuple-element.102), channel_id=1, source_target_pairs={{0,4},{4,0},{8,12},{12,8},{1,5},{5,1},{9,13},{13,9},{2,6},{6,2},{1... | collective-permute-start | bytes 110600 | tf_op jit(solution)/shard_map/ppermute | solution.py:735

commit v6 on v5

--- a/solution.py
+++ b/solution.py
@@ -781,7 +781,7 @@
     for m in range(1, emg):
         blocks[0, m] = across[m]
         for k in range(1, fib):
-            if m == 1 and k in facing(fib):
+            if m in facing(emg) and k in facing(fib):
                 blocks[k, m] = xor_swap(trimmed(with_ends.shape[0], blocks[k, 0]), "emg", m)
             else:
                 blocks[k, m] = xor_swap(across[m], "fib", k)

time: 30.8 us -> 29.9 us (0.971)
  waiting for transfers between devices: 6.46 us -> 3.77 us
  starting transfers between devices: 12.2 us -> 14 us
    ppermute x13, waiting for transfers between devices: 6.46 us -> 3.77 us  [xor_swap(): lax.ppermute(value, axis, [(i, i ^ k) for i in range(lax.axis_size(axis))])]
    ppermute x13, starting transfers between devices: 12.2 us -> 14 us  [xor_swap(): lax.ppermute(value, axis, [(i, i ^ k) for i in range(lax.axis_size(axis))])]
  transfers between devices with their start and end apart: 13 -> 13, of which waited for: 6 -> 5; matrix products, arithmetic and copies ran while one was open for 0% -> 0% of each run, Pallas kernels for 16% -> 17%
where the time goes in v6:
time: 29.9 us; the launch traced here: 29.7 us
  starting transfers between devices  14 us (47%)
  Pallas kernels  11.1 us (37%)
  waiting for transfers between devices  3.77 us (13%)
  between operations  0.75 us (3%)
    ppermute x13, starting transfers between devices, xor_swap(): lax.ppermute(value, axis, [(i, i ^ k) for i in range(lax.axis_size(axis))])  14 us
    pallas_call x15, Pallas kernels, kernel_call(): pl.pallas_call(body, out_shape=shapes, in_specs=[HBM if i in hbm_ins else...  11.1 us
    ppermute x13, waiting for transfers between devices, xor_swap(): lax.ppermute(value, axis, [(i, i ^ k) for i in range(lax.axis_size(axis))])  3.77 us
  transfers between devices with their start and end apart: 13, of which 5 were waited for; matrix products, arithmetic and copies ran while one was open for 0% of the time, Pallas kernels for 17%

profile of v6, /device:TPU:0, one launch (start us, length us, event | category | flops | bytes accessed | tf_op | source)
XLA Modules:
  0.0 29.7 jit_solution(13904654329065985147)
XLA Ops:
  0.6 2.8 %shard_map.157 = (f32[64,64,128]{2,1,0:T(8,128)S(1)}, f32[64,128]{1,0:T(8,128)S(1)}, f32[64,128]{1,0:T(8,128)S(1)}, f32[8,128]{1,0:T(8,128)S(1)}, bf16[64,192]{1...) custom-call(f32[57,57]{1,0:T(8,128)} %refs_0_.1, ...), custom_call_target="tpu_custom_call" | custom-call | tf_op jit(solution)/shard_map/pallas_call | solution.py:43
  3.4 3.0 %collective-permute-start.1 = (f32[8,128]{1,0:T(8,128)S(1)}, f32[8,128]{1,0:T(8,128)S(1)}, u32[]{:S(2)}, u32[]{:S(2)}) collective-permute-start(f32[8,128]{1,0:T(8,128)S(1)} %get-tuple-element.64.sums_ref.rest_0_), channel_id=1, source_target_pairs={{0,8},{4,12},{8,0},{12,4},{1,9},{5,13},{9,1},{13,5},{2,10},{6,14},... | collective-permute-start | bytes 12296 | tf_op jit(solution)/shard_map/ppermute | solution.py:735
  6.4 0.0 collective-permute-start
  6.4 0.2 collective-permute-start.2
  6.6 1.5 %shard_map.158 = (f32[64,64,128]{2,1,0:T(8,128)S(1)}, f32[8,128]{1,0:T(8,128)S(1)}, f32[256,128]{1,0:T(8,128)S(1)}, f32[64,128]{1,0:T(8,128)S(1)}, f32[64,128]{1,0:T(8,128)S(1)}) custom-call(f32[64,64,128]{2,1,0:T(8,128)S(1)} %get-tuple-element.54.states_ref, bf16[64,192]{1,0:T(8,128)(2,1)S(1)} %get-tuple-element.55.triple_ref, f32[256,128]{1,0:T(8,128)} %bitcast.10, ...), custom_call_target="tpu_custom_call" | custom-call | flops 700000000 | bytes 65536 | tf_op jit(solution)/shard_map/pallas_call | solution.py:43
  8.2 0.0 collective-permute-done.1.rest_2_
  8.2 0.0 collective-permute-done.rest_1_
  8.2 1.4 %collective-permute-done.2.rest_3_ = f32[24,128]{1,0:T(8,128)S(1)} collective-permute-done((f32[24,128]{1,0:T(8,128)S(1)}, f32[24,128]{1,0:T(8,128)S(1)}, u32[]{:S(2)}, u32[]{:S(2)}) %collective-permute-start.2) | collective-permute-done | bytes 12320 | tf_op jit(solution)/shard_map/ppermute | solution.py:735
  9.6 0.2 shard_map.160
  9.8 0.7 %shard_map.161 = (f32[64,64,128]{2,1,0:T(8,128)S(1)}, f32[64,128]{1,0:T(8,128)S(1)}, f32[64,128]{1,0:T(8,128)S(1)}, f32[72,128]{1,0:T(8,128)S(1)}, f32[88,128]{1,0:T(8,128)S(1)}) custom-call(f32[64,64,128]{2,1,0:T(8,128)S(1)} %get-tuple-element.54.states_ref, f32[64,64,128]{2,1,0:T(8,128)S(1)} %get-tuple-element.56.drive_ref, ...), custom_call_target="tpu_custom_call" | custom-call | tf_op jit(solution)/shard_map/pallas_call | solution.py:43
  10.5 1.6 %collective-permute-start.6 = (f32[168,128]{1,0:T(8,128)S(1)}, f32[168,128]{1,0:T(8,128)S(1)}, u32[]{:S(2)}, u32[]{:S(2)}) collective-permute-start(f32[168,128]{1,0:T(8,128)S(1)} %shard_map.162), channel_id=1, source_target_pairs={{0,16},{16,0},{1,17},{17,1},{2,18},{18,2},{3,19},{19,3},{4,20},{20... | collective-permute-start | bytes 258056 | tf_op jit(solution)/shard_map/ppermute | solution.py:735
  12.1 2.6 %collective-permute-start.4 = (f32[72,128]{1,0:T(8,128)S(1)}, f32[72,128]{1,0:T(8,128)S(1)}, u32[]{:S(2)}, u32[]{:S(2)}) collective-permute-start(f32[72,128]{1,0:T(8,128)S(1)} %get-tuple-element.85.refs_0_.rest_0_), channel_id=1, source_target_pairs={{0,2},{1,3},{2,0},{3,1},{4,6},{5,7},{6,4},{7,5},{8,10},{9,11},{10,... | collective-permute-start | bytes 110600 | tf_op jit(solution)/shard_map/ppermute | solution.py:735
  14.6 1.3 %collective-permute-start.5 = (f32[88,128]{1,0:T(8,128)S(1)}, f32[88,128]{1,0:T(8,128)S(1)}, u32[]{:S(2)}, u32[]{:S(2)}) collective-permute-start(f32[88,128]{1,0:T(8,128)S(1)} %get-tuple-element.70.block_ref), channel_id=1, source_target_pairs={{0,3},{1,2},{2,1},{3,0},{4,7},{5,6},{6,5},{7,4},{8,11},{9,10},{10,... | collective-permute-start | bytes 135176 | tf_op jit(solution)/shard_map/ppermute | solution.py:735
  16.0 0.2 collective-permute-start.3
  16.2 0.0 collective-permute-done.6.block_ref.refs_4_.refs_2_.rest_4_
  16.2 3.0 %collective-permute-start.9 = (f32[88,128]{1,0:T(8,128)S(1)}, f32[88,128]{1,0:T(8,128)S(1)}, u32[]{:S(2)}, u32[]{:S(2)}) collective-permute-start(f32[88,128]{1,0:T(8,128)S(1)} %shard_map.163), channel_id=1, source_target_pairs={{0,3},{1,2},{2,1},{3,0},{4,7},{5,6},{6,5},{7,4},{8,11},{9,10},{10,... | collective-permute-start | bytes 135176 | tf_op jit(solution)/shard_map/ppermute | solution.py:735
  19.2 0.5 %collective-permute-start.7 = (f32[88,128]{1,0:T(8,128)S(1)}, f32[88,128]{1,0:T(8,128)S(1)}, u32[]{:S(2)}, u32[]{:S(2)}) collective-permute-start(f32[88,128]{1,0:T(8,128)S(1)} %shard_map.163), channel_id=1, source_target_pairs={{0,1},{1,0},{2,3},{3,2},{4,5},{5,4},{6,7},{7,6},{8,9},{9,8},{10,11... | collective-permute-start | bytes 135176 | tf_op jit(solution)/shard_map/ppermute | solution.py:735
  19.7 0.0 collective-permute-done.4.refs_2_.rest_2_
  19.7 0.9 %collective-permute-start.8 = (f32[72,128]{1,0:T(8,128)S(1)}, f32[72,128]{1,0:T(8,128)S(1)}, u32[]{:S(2)}, u32[]{:S(2)}) collective-permute-start(f32[72,128]{1,0:T(8,128)S(1)} %collective-permute-done.4.refs_2_.rest_2_), channel_id=1, source_target_pairs={{0,16},{16,0},{1,17},{17,1},{2,18},{18,2},{3,19},{19,3},{4,20},{20... | collective-permute-start | bytes 110600 | tf_op jit(solution)/shard_map/ppermute | solution.py:735
  20.6 0.1 shard_map.165
  20.7 0.1 collective-permute-done.5.refs_3_.refs_1_.rest_3_
  20.8 0.0 collective-permute-done.3.refs_1_.refs_0_.rest_1_
  20.8 0.0 collective-permute-start.10
  20.8 1.0 %shard_map.164 = (f32[896,256]{1,0:T(8,128)S(1)}, bf16[256,640]{1,0:T(8,128)(2,1)S(1)}) custom-call(f32[72,128]{1,0:T(8,128)S(1)} %get-tuple-element.85.refs_0_.rest_0_, f32[88,128]{1,0:T(8,128)S(1)} %collective-permute-done.3.refs_1_.refs_0_.rest_1_, f32[72,128]{1,0:T(8,128)S(1)} %collective-permute-done.4.refs_2_.rest_2_, ...), custom_call_target="tpu_custom_call" | custom-call | tf_op jit(solution)/shard_map/pallas_call | solution.py:43
  21.8 0.2 collective-permute-done.10.other_ref
  22.0 1.7 %collective-permute-done.8.refs_1_.refs_6_.rest_6_ = f32[72,128]{1,0:T(8,128)S(1)} collective-permute-done((f32[72,128]{1,0:T(8,128)S(1)}, f32[72,128]{1,0:T(8,128)S(1)}, u32[]{:S(2)}, u32[]{:S(2)}) %collective-permute-start.8) | collective-permute-done | bytes 36896 | tf_op jit(solution)/shard_map/ppermute | solution.py:735
  23.6 0.0 collective-permute-done.9.refs_2_.refs_7_.refs_4_.rest_7_
  23.6 0.0 collective-permute-done.7.refs_0_.refs_5_.refs_3_.rest_5_
  23.7 0.1 collective-permute-start.11
  23.7 0.7 %collective-permute-start.12 = (f32[72,128]{1,0:T(8,128)S(1)}, f32[72,128]{1,0:T(8,128)S(1)}, u32[]{:S(2)}, u32[]{:S(2)}) collective-permute-start(f32[72,128]{1,0:T(8,128)S(1)} %get-tuple-element.102), channel_id=1, source_target_pairs={{0,4},{4,0},{8,12},{12,8},{1,5},{5,1},{9,13},{13,9},{2,6},{6,2},{1... | collective-permute-start | bytes 110600 | tf_op jit(solution)/shard_map/ppermute | solution.py:735
  24.4 1.2 %shard_map.169 = f32[57,64,128]{2,1,0:T(8,128)} custom-call(f32[64,64,128]{2,1,0:T(8,128)S(1)} %get-tuple-element.93.states_ref), custom_call_target="tpu_custom_call" | custom-call | tf_op jit(solution)/shard_map/pallas_call | solution.py:43
  25.6 0.7 %shard_map.166 = (f32[896,256]{1,0:T(8,128)S(1)}, bf16[256,384]{1,0:T(8,128)(2,1)S(1)}) custom-call(f32[88,128]{1,0:T(8,128)S(1)} %collective-permute-done.7.refs_0_.refs_5_.refs_3_.rest_5_, f32[72,128]{1,0:T(8,128)S(1)} %collective-permute-done.8.refs_1_.refs_6_.rest_6_, f32[88,128]{1,0:T(8,128)S(1)} %collective-permute-done.9.refs_2_.refs_7_.refs_4_.rest_7_, ...), custom_call_target="tpu_custom_call" | custom-call | tf_op jit(solution)/shard_map/pallas_call | solution.py:43
  26.3 0.3 %shard_map.170 = (f32[960,256]{1,0:T(8,128)S(1)}, f32[80,256]{1,0:T(8,128)S(1)}) custom-call(f32[320,128]{1,0:T(8,128)S(1)} %get-tuple-element.71.wide_ref, f32[88,128]{1,0:T(8,128)S(1)} %collective-permute-done.3.refs_1_.refs_0_.rest_1_, f32[88,128]{1,0:T(8,128)S(1)} %collective-permute-done.5.refs_3_.refs_1_.rest_3_, ...), custom_call_target="tpu_custom_call" | custom-call | tf_op jit(solution)/shard_map/pallas_call | solution.py:43
  26.7 0.4 %collective-permute-done.11.rest_11_ = f32[72,128]{1,0:T(8,128)S(1)} collective-permute-done((f32[72,128]{1,0:T(8,128)S(1)}, f32[72,128]{1,0:T(8,128)S(1)}, u32[]{:S(2)}, u32[]{:S(2)}) %collective-permute-start.11) | collective-permute-done | bytes 36896 | tf_op jit(solution)/shard_map/ppermute | solution.py:735
  27.1 0.0 collective-permute-done.12.rest_12_
  27.1 2.5 %shard_map.171 = (f32[512,128]{1,0:T(8,128)}, f32[64,128]{1,0:T(8,128)}) custom-call(f32[896,256]{1,0:T(8,128)S(1)} %get-tuple-element.95.own_ref, f32[960,256]{1,0:T(8,128)S(1)} %get-tuple-element.96.diag_ref, f32[80,256]{1,0:T(8,128)S(1)} %get-tuple-element.97.mask_ref, f32[64,128]{1,0:T(8,128)S(1)} %get-tuple-element.98.solved_ref, ...), custom_call_target="tpu_custom_call" | custom-call | tf_op jit(solution)/shard_map/pallas_call | solution.py:43
  (5 shorter events, 0.0 us)
Async XLA Ops:
  3.4 4.8 %collective-permute-start.1 = (f32[8,128]{1,0:T(8,128)S(1)}, f32[8,128]{1,0:T(8,128)S(1)}, u32[]{:S(2)}, u32[]{:S(2)}) collective-permute-start(f32[8,128]{1,0:T(8,128)S(1)} %get-tuple-element.64.sums_ref.rest_0_), channel_id=1, source_target_pairs={{0,8},{4,12},{8,0},{12,4},{1,9},{5,13},{9,1},{13,5},{2,10},{6,14},... | collective-permute-start | bytes 12296 | tf_op jit(solution)/shard_map/ppermute | solution.py:735
  6.4 1.8 %collective-permute-start = (f32[24,128]{1,0:T(8,128)S(1)}, f32[24,128]{1,0:T(8,128)S(1)}, u32[]{:S(2)}, u32[]{:S(2)}) collective-permute-start(f32[24,128]{1,0:T(8,128)S(1)} %get-tuple-element.66), channel_id=1, source_target_pairs={{0,4},{4,0},{8,12},{12,8},{1,5},{5,1},{9,13},{13,9},{2,6},{6,2},{1... | collective-permute-start | bytes 36872 | tf_op jit(solution)/shard_map/ppermute | solution.py:735
  6.4 3.2 %collective-permute-start.2 = (f32[24,128]{1,0:T(8,128)S(1)}, f32[24,128]{1,0:T(8,128)S(1)}, u32[]{:S(2)}, u32[]{:S(2)}) collective-permute-start(f32[24,128]{1,0:T(8,128)S(1)} %get-tuple-element.67), channel_id=1, source_target_pairs={{0,12},{4,8},{8,4},{12,0},{1,13},{5,9},{9,5},{13,1},{2,14},{6,10},... | collective-permute-start | bytes 36872 | tf_op jit(solution)/shard_map/ppermute | solution.py:735
  10.5 5.8 %collective-permute-start.6 = (f32[168,128]{1,0:T(8,128)S(1)}, f32[168,128]{1,0:T(8,128)S(1)}, u32[]{:S(2)}, u32[]{:S(2)}) collective-permute-start(f32[168,128]{1,0:T(8,128)S(1)} %shard_map.162), channel_id=1, source_target_pairs={{0,16},{16,0},{1,17},{17,1},{2,18},{18,2},{3,19},{19,3},{4,20},{20... | collective-permute-start | bytes 258056 | tf_op jit(solution)/shard_map/ppermute | solution.py:735
  12.1 7.6 %collective-permute-start.4 = (f32[72,128]{1,0:T(8,128)S(1)}, f32[72,128]{1,0:T(8,128)S(1)}, u32[]{:S(2)}, u32[]{:S(2)}) collective-permute-start(f32[72,128]{1,0:T(8,128)S(1)} %get-tuple-element.85.refs_0_.rest_0_), channel_id=1, source_target_pairs={{0,2},{1,3},{2,0},{3,1},{4,6},{5,7},{6,4},{7,5},{8,10},{9,11},{10,... | collective-permute-start | bytes 110600 | tf_op jit(solution)/shard_map/ppermute | solution.py:735
  14.6 6.1 %collective-permute-start.5 = (f32[88,128]{1,0:T(8,128)S(1)}, f32[88,128]{1,0:T(8,128)S(1)}, u32[]{:S(2)}, u32[]{:S(2)}) collective-permute-start(f32[88,128]{1,0:T(8,128)S(1)} %get-tuple-element.70.block_ref), channel_id=1, source_target_pairs={{0,3},{1,2},{2,1},{3,0},{4,7},{5,6},{6,5},{7,4},{8,11},{9,10},{10,... | collective-permute-start | bytes 135176 | tf_op jit(solution)/shard_map/ppermute | solution.py:735
  16.0 4.8 %collective-permute-start.3 = (f32[88,128]{1,0:T(8,128)S(1)}, f32[88,128]{1,0:T(8,128)S(1)}, u32[]{:S(2)}, u32[]{:S(2)}) collective-permute-start(f32[88,128]{1,0:T(8,128)S(1)} %get-tuple-element.70.block_ref), channel_id=1, source_target_pairs={{0,1},{1,0},{2,3},{3,2},{4,5},{5,4},{6,7},{7,6},{8,9},{9,8},{10,11... | collective-permute-start | bytes 135176 | tf_op jit(solution)/shard_map/ppermute | solution.py:735
  16.2 7.4 %collective-permute-start.9 = (f32[88,128]{1,0:T(8,128)S(1)}, f32[88,128]{1,0:T(8,128)S(1)}, u32[]{:S(2)}, u32[]{:S(2)}) collective-permute-start(f32[88,128]{1,0:T(8,128)S(1)} %shard_map.163), channel_id=1, source_target_pairs={{0,3},{1,2},{2,1},{3,0},{4,7},{5,6},{6,5},{7,4},{8,11},{9,10},{10,... | collective-permute-start | bytes 135176 | tf_op jit(solution)/shard_map/ppermute | solution.py:735
  19.2 4.4 %collective-permute-start.7 = (f32[88,128]{1,0:T(8,128)S(1)}, f32[88,128]{1,0:T(8,128)S(1)}, u32[]{:S(2)}, u32[]{:S(2)}) collective-permute-start(f32[88,128]{1,0:T(8,128)S(1)} %shard_map.163), channel_id=1, source_target_pairs={{0,1},{1,0},{2,3},{3,2},{4,5},{5,4},{6,7},{7,6},{8,9},{9,8},{10,11... | collective-permute-start | bytes 135176 | tf_op jit(solution)/shard_map/ppermute | solution.py:735
  19.7 4.0 %collective-permute-start.8 = (f32[72,128]{1,0:T(8,128)S(1)}, f32[72,128]{1,0:T(8,128)S(1)}, u32[]{:S(2)}, u32[]{:S(2)}) collective-permute-start(f32[72,128]{1,0:T(8,128)S(1)} %collective-permute-done.4.refs_2_.rest_2_), channel_id=1, source_target_pairs={{0,16},{16,0},{1,17},{17,1},{2,18},{18,2},{3,19},{19,3},{4,20},{20... | collective-permute-start | bytes 110600 | tf_op jit(solution)/shard_map/ppermute | solution.py:735
  20.8 1.2 %collective-permute-start.10 = (f32[8,128]{1,0:T(8,128)S(1)}, f32[8,128]{1,0:T(8,128)S(1)}, u32[]{:S(2)}, u32[]{:S(2)}) collective-permute-start(f32[8,128]{1,0:T(8,128)S(1)} %get-tuple-element.78.sums_ref), channel_id=1, source_target_pairs={{0,4},{4,0},{8,12},{12,8},{1,5},{5,1},{9,13},{13,9},{2,6},{6,2},{1... | collective-permute-start | bytes 12296 | tf_op jit(solution)/shard_map/ppermute | solution.py:735
  23.7 3.4 %collective-permute-start.11 = (f32[72,128]{1,0:T(8,128)S(1)}, f32[72,128]{1,0:T(8,128)S(1)}, u32[]{:S(2)}, u32[]{:S(2)}) collective-permute-start(f32[72,128]{1,0:T(8,128)S(1)} %get-tuple-element.101), channel_id=1, source_target_pairs={{0,12},{4,8},{8,4},{12,0},{1,13},{5,9},{9,5},{13,1},{2,14},{6,10},... | collective-permute-start | bytes 110600 | tf_op jit(solution)/shard_map/ppermute | solution.py:735
  23.7 3.4 %collective-permute-start.12 = (f32[72,128]{1,0:T(8,128)S(1)}, f32[72,128]{1,0:T(8,128)S(1)}, u32[]{:S(2)}, u32[]{:S(2)}) collective-permute-start(f32[72,128]{1,0:T(8,128)S(1)} %get-tuple-element.102), channel_id=1, source_target_pairs={{0,4},{4,0},{8,12},{12,8},{1,5},{5,1},{9,13},{13,9},{2,6},{6,2},{1... | collective-permute-start | bytes 110600 | tf_op jit(solution)/shard_map/ppermute | solution.py:735

commit v7 on v6

--- a/solution.py
+++ b/solution.py
@@ -329,10 +329,9 @@
     def body(block_ref, wide_ref, *refs):
         first, last = wide_ref[0:layers, :], wide_ref[wide.shape[0] - layers:, :]
         for ref, k in zip(refs, facing(fib)):
-            ref[0:at, :] = block_ref[...]
-            ref[at:, :] = for_partner(lax.axis_index("fib"), k, first, last)
-
-    return kernel_call(body, [(at + layers, depth)] * len(facing(fib)), block, wide)
+            ref[...] = for_partner(lax.axis_index("fib"), k, first, last)
+
+    return kernel_call(body, [(layers, depth)] * len(facing(fib)), block, wide)
 
 
 def last_solve(shards, voltage, current, misc, table):
@@ -479,7 +478,7 @@
         block, (diag_ref, mask_ref) = dict(zip(needed, refs)), refs[len(needed):]
         shard, mine, place = (lax.axis_index(a) for a in ("len", "fib", "emg"))
         below, above = beside(
-            "fib", [block.get((k, 0)) for k in range(fib)], slice(size + ends, size + ends + 2 * long)
+            "fib", [block.get((k, 0)) for k in range(fib)], slice(0, 2 * long)
         )
 
         def end_lanes(k):
@@ -776,20 +775,21 @@
         states, drive, solved, current, param, misc, rise, fall, near, ends
     )
     with_layers = with_outer(fib, with_ends, wide, rows)
-    blocks = {(k, 0): block for k, block in enumerate(swaps("fib", send, with_layers))}
+    blocks = {(k, 0): block for k, block in enumerate(swaps("fib", send, [with_ends] * len(facing(fib))))}
     across = swaps("emg", send, [with_ends] * len(facing(emg)))
     for m in range(1, emg):
         blocks[0, m] = across[m]
         for k in range(1, fib):
             if m in facing(emg) and k in facing(fib):
-                blocks[k, m] = xor_swap(trimmed(with_ends.shape[0], blocks[k, 0]), "emg", m)
+                blocks[k, m] = xor_swap(blocks[k, 0], "emg", m)
             else:
                 blocks[k, m] = xor_swap(across[m], "fib", k)
+    terms = {**blocks, **{(k, 0): xor_swap(v, "fib", k) for k, v in zip(facing(fib), with_layers)}}
     keys = sorted(blocks, key=lambda key: (all(key), key))
     count_early = sum(not all(key) for key in keys)
     got = [blocks[key] for key in keys]
     solved, sums = last_solve(shards, volt, flow, fires, table)
-    diag, mask = operator_terms((shards, fib, emg), size, ends.shape[0], wide, blocks, rows)
+    diag, mask = operator_terms((shards, fib, emg), size, ends.shape[0], wide, terms, rows)
     _, ahead = lax.optimization_barrier((across, sums))
     other = xor_swap(ahead, "len", 1)
     source, hot = sources(flows, got[:count_early], rows, depth)

time: 29.9 us -> 30.2 us (1.010)
  starting transfers between devices: 14 us -> 14.7 us
  waiting for transfers between devices: 3.77 us -> 3.25 us
    ppermute x13 -> x14, starting transfers between devices: 14 us -> 14.7 us  [xor_swap(): lax.ppermute(value, axis, [(i, i ^ k) for i in range(lax.axis_size(axis))])]
    ppermute x13 -> x14, waiting for transfers between devices: 3.77 us -> 3.25 us  [xor_swap(): lax.ppermute(value, axis, [(i, i ^ k) for i in range(lax.axis_size(axis))])]
    pallas_call x15 -> x14, Pallas kernels: 11.1 us -> 11.2 us  [kernel_call(): pl.pallas_call(body, out_shape=shapes, in_specs=[HBM if i in hbm_ins else...]
  transfers between devices with their start and end apart: 13 -> 14, of which waited for: 5 -> 4; matrix products, arithmetic and copies ran while one was open for 0% -> 0% of each run, Pallas kernels for 17% -> 17%
where the time goes in v7:
time: 30.2 us; the launch traced here: 29.9 us
  starting transfers between devices  14.7 us (49%)
  Pallas kernels  11.2 us (37%)
  waiting for transfers between devices  3.25 us (11%)
  between operations  0.75 us (2%)
    ppermute x14, starting transfers between devices, xor_swap(): lax.ppermute(value, axis, [(i, i ^ k) for i in range(lax.axis_size(axis))])  14.7 us
    pallas_call x14, Pallas kernels, kernel_call(): pl.pallas_call(body, out_shape=shapes, in_specs=[HBM if i in hbm_ins else...  11.2 us
    ppermute x14, waiting for transfers between devices, xor_swap(): lax.ppermute(value, axis, [(i, i ^ k) for i in range(lax.axis_size(axis))])  3.25 us
  transfers between devices with their start and end apart: 14, of which 4 were waited for; matrix products, arithmetic and copies ran while one was open for 0% of the time, Pallas kernels for 17%

profile of v7, /device:TPU:0, one launch (start us, length us, event | category | flops | bytes accessed | tf_op | source)
XLA Modules:
  0.0 29.9 jit_solution(3695260491811689807)
XLA Ops:
  0.6 2.8 %shard_map.157 = (f32[64,64,128]{2,1,0:T(8,128)S(1)}, f32[64,128]{1,0:T(8,128)S(1)}, f32[64,128]{1,0:T(8,128)S(1)}, f32[8,128]{1,0:T(8,128)S(1)}, bf16[64,192]{1...) custom-call(f32[57,57]{1,0:T(8,128)} %refs_0_.1, ...), custom_call_target="tpu_custom_call" | custom-call | tf_op jit(solution)/shard_map/pallas_call | solution.py:43
  3.4 3.0 %collective-permute-start.1 = (f32[8,128]{1,0:T(8,128)S(1)}, f32[8,128]{1,0:T(8,128)S(1)}, u32[]{:S(2)}, u32[]{:S(2)}) collective-permute-start(f32[8,128]{1,0:T(8,128)S(1)} %get-tuple-element.64.sums_ref.rest_0_), channel_id=1, source_target_pairs={{0,8},{4,12},{8,0},{12,4},{1,9},{5,13},{9,1},{13,5},{2,10},{6,14},... | collective-permute-start | bytes 12296 | tf_op jit(solution)/shard_map/ppermute | solution.py:734
  6.4 0.0 collective-permute-start
  6.4 0.2 collective-permute-start.2
  6.6 1.5 %shard_map.158 = (f32[64,64,128]{2,1,0:T(8,128)S(1)}, f32[8,128]{1,0:T(8,128)S(1)}, f32[256,128]{1,0:T(8,128)S(1)}, f32[64,128]{1,0:T(8,128)S(1)}, f32[64,128]{1,0:T(8,128)S(1)}) custom-call(f32[64,64,128]{2,1,0:T(8,128)S(1)} %get-tuple-element.54.states_ref, bf16[64,192]{1,0:T(8,128)(2,1)S(1)} %get-tuple-element.55.triple_ref, f32[256,128]{1,0:T(8,128)} %bitcast.10, ...), custom_call_target="tpu_custom_call" | custom-call | flops 700000000 | bytes 65536 | tf_op jit(solution)/shard_map/pallas_call | solution.py:43
  8.2 0.0 collective-permute-done.1.rest_2_
  8.2 0.0 collective-permute-done.rest_1_
  8.2 1.4 %collective-permute-done.2.rest_3_ = f32[24,128]{1,0:T(8,128)S(1)} collective-permute-done((f32[24,128]{1,0:T(8,128)S(1)}, f32[24,128]{1,0:T(8,128)S(1)}, u32[]{:S(2)}, u32[]{:S(2)}) %collective-permute-start.2) | collective-permute-done | bytes 12320 | tf_op jit(solution)/shard_map/ppermute | solution.py:734
  9.6 0.2 shard_map.160
  9.8 0.7 %shard_map.161 = (f32[64,64,128]{2,1,0:T(8,128)S(1)}, f32[64,128]{1,0:T(8,128)S(1)}, f32[64,128]{1,0:T(8,128)S(1)}, f32[72,128]{1,0:T(8,128)S(1)}, f32[88,128]{1,0:T(8,128)S(1)}) custom-call(f32[64,64,128]{2,1,0:T(8,128)S(1)} %get-tuple-element.54.states_ref, f32[64,64,128]{2,1,0:T(8,128)S(1)} %get-tuple-element.56.drive_ref, ...), custom_call_target="tpu_custom_call" | custom-call | tf_op jit(solution)/shard_map/pallas_call | solution.py:43
  10.4 1.6 %collective-permute-start.6 = (f32[88,128]{1,0:T(8,128)S(1)}, f32[88,128]{1,0:T(8,128)S(1)}, u32[]{:S(2)}, u32[]{:S(2)}) collective-permute-start(f32[88,128]{1,0:T(8,128)S(1)} %get-tuple-element.70.block_ref), channel_id=1, source_target_pairs={{0,16},{16,0},{1,17},{17,1},{2,18},{18,2},{3,19},{19,3},{4,20},{20... | collective-permute-start | bytes 135176 | tf_op jit(solution)/shard_map/ppermute | solution.py:734
  12.0 2.6 %collective-permute-start.4 = (f32[72,128]{1,0:T(8,128)S(1)}, f32[72,128]{1,0:T(8,128)S(1)}, u32[]{:S(2)}, u32[]{:S(2)}) collective-permute-start(f32[72,128]{1,0:T(8,128)S(1)} %get-tuple-element.84.refs_0_.rest_0_), channel_id=1, source_target_pairs={{0,2},{1,3},{2,0},{3,1},{4,6},{5,7},{6,4},{7,5},{8,10},{9,11},{10,... | collective-permute-start | bytes 110600 | tf_op jit(solution)/shard_map/ppermute | solution.py:734
  14.6 1.3 %collective-permute-start.5 = (f32[88,128]{1,0:T(8,128)S(1)}, f32[88,128]{1,0:T(8,128)S(1)}, u32[]{:S(2)}, u32[]{:S(2)}) collective-permute-start(f32[88,128]{1,0:T(8,128)S(1)} %get-tuple-element.70.block_ref), channel_id=1, source_target_pairs={{0,3},{1,2},{2,1},{3,0},{4,7},{5,6},{6,5},{7,4},{8,11},{9,10},{10,... | collective-permute-start | bytes 135176 | tf_op jit(solution)/shard_map/ppermute | solution.py:734
  16.0 0.2 collective-permute-start.3
  16.2 0.0 collective-permute-done.6.refs_4_.rest_4_
  16.2 2.9 %collective-permute-start.9 = (f32[88,128]{1,0:T(8,128)S(1)}, f32[88,128]{1,0:T(8,128)S(1)}, u32[]{:S(2)}, u32[]{:S(2)}) collective-permute-start(f32[88,128]{1,0:T(8,128)S(1)} %collective-permute-done.6.refs_4_.rest_4_), channel_id=1, source_target_pairs={{0,3},{1,2},{2,1},{3,0},{4,7},{5,6},{6,5},{7,4},{8,11},{9,10},{10,... | collective-permute-start | bytes 135176 | tf_op jit(solution)/shard_map/ppermute | solution.py:734
  19.1 0.5 %collective-permute-start.7 = (f32[88,128]{1,0:T(8,128)S(1)}, f32[88,128]{1,0:T(8,128)S(1)}, u32[]{:S(2)}, u32[]{:S(2)}) collective-permute-start(f32[88,128]{1,0:T(8,128)S(1)} %collective-permute-done.6.refs_4_.rest_4_), channel_id=1, source_target_pairs={{0,1},{1,0},{2,3},{3,2},{4,5},{5,4},{6,7},{7,6},{8,9},{9,8},{10,11... | collective-permute-start | bytes 135176 | tf_op jit(solution)/shard_map/ppermute | solution.py:734
  19.6 0.0 collective-permute-done.4.refs_2_.rest_2_
  19.6 0.5 %collective-permute-start.8 = (f32[72,128]{1,0:T(8,128)S(1)}, f32[72,128]{1,0:T(8,128)S(1)}, u32[]{:S(2)}, u32[]{:S(2)}) collective-permute-start(f32[72,128]{1,0:T(8,128)S(1)} %collective-permute-done.4.refs_2_.rest_2_), channel_id=1, source_target_pairs={{0,16},{16,0},{1,17},{17,1},{2,18},{18,2},{3,19},{19,3},{4,20},{20... | collective-permute-start | bytes 110600 | tf_op jit(solution)/shard_map/ppermute | solution.py:734
  20.1 0.1 shard_map.163
  20.2 0.6 %collective-permute-done.5.refs_3_.refs_1_.rest_3_ = f32[88,128]{1,0:T(8,128)S(1)} collective-permute-done((f32[88,128]{1,0:T(8,128)S(1)}, f32[88,128]{1,0:T(8,128)S(1)}, u32[]{:S(2)}, u32[]{:S(2)}) %collective-permute-start.5) | collective-permute-done | bytes 45088 | tf_op jit(solution)/shard_map/ppermute | solution.py:734
  20.8 0.0 collective-permute-done.3.refs_1_.refs_0_.rest_1_
  20.8 0.0 collective-permute-start.10
  20.8 1.1 %collective-permute-start.11 = (f32[80,128]{1,0:T(8,128)S(1)}, f32[80,128]{1,0:T(8,128)S(1)}, u32[]{:S(2)}, u32[]{:S(2)}) collective-permute-start(f32[80,128]{1,0:T(8,128)S(1)} %shard_map.168), channel_id=1, source_target_pairs={{0,16},{16,0},{1,17},{17,1},{2,18},{18,2},{3,19},{19,3},{4,20},{20... | collective-permute-start | bytes 122888 | tf_op jit(solution)/shard_map/ppermute | solution.py:734
  21.9 1.0 %shard_map.162 = (f32[896,256]{1,0:T(8,128)S(1)}, bf16[256,640]{1,0:T(8,128)(2,1)S(1)}) custom-call(f32[72,128]{1,0:T(8,128)S(1)} %get-tuple-element.84.refs_0_.rest_0_, f32[88,128]{1,0:T(8,128)S(1)} %collective-permute-done.3.refs_1_.refs_0_.rest_1_, f32[72,128]{1,0:T(8,128)S(1)} %collective-permute-done.4.refs_2_.rest_2_, ...), custom_call_target="tpu_custom_call" | custom-call | tf_op jit(solution)/shard_map/pallas_call | solution.py:43
  22.9 0.0 collective-permute-done.10.other_ref
  22.9 0.6 %collective-permute-done.8.refs_1_.refs_6_.rest_6_ = f32[72,128]{1,0:T(8,128)S(1)} collective-permute-done((f32[72,128]{1,0:T(8,128)S(1)}, f32[72,128]{1,0:T(8,128)S(1)}, u32[]{:S(2)}, u32[]{:S(2)}) %collective-permute-start.8) | collective-permute-done | bytes 36896 | tf_op jit(solution)/shard_map/ppermute | solution.py:734
  23.5 0.0 collective-permute-done.9.refs_2_.refs_7_.refs_4_.rest_7_
  23.5 0.0 collective-permute-done.7.refs_0_.refs_5_.refs_3_.rest_5_
  23.6 0.1 collective-permute-start.12
  23.7 0.7 %collective-permute-start.13 = (f32[72,128]{1,0:T(8,128)S(1)}, f32[72,128]{1,0:T(8,128)S(1)}, u32[]{:S(2)}, u32[]{:S(2)}) collective-permute-start(f32[72,128]{1,0:T(8,128)S(1)} %get-tuple-element.102), channel_id=1, source_target_pairs={{0,4},{4,0},{8,12},{12,8},{1,5},{5,1},{9,13},{13,9},{2,6},{6,2},{1... | collective-permute-start | bytes 110600 | tf_op jit(solution)/shard_map/ppermute | solution.py:734
  24.3 1.2 %shard_map.167 = f32[57,64,128]{2,1,0:T(8,128)} custom-call(f32[64,64,128]{2,1,0:T(8,128)S(1)} %get-tuple-element.92.states_ref), custom_call_target="tpu_custom_call" | custom-call | tf_op jit(solution)/shard_map/pallas_call | solution.py:43
  25.5 0.7 %shard_map.164 = (f32[896,256]{1,0:T(8,128)S(1)}, bf16[256,384]{1,0:T(8,128)(2,1)S(1)}) custom-call(f32[88,128]{1,0:T(8,128)S(1)} %collective-permute-done.7.refs_0_.refs_5_.refs_3_.rest_5_, f32[72,128]{1,0:T(8,128)S(1)} %collective-permute-done.8.refs_1_.refs_6_.rest_6_, f32[88,128]{1,0:T(8,128)S(1)} %collective-permute-done.9.refs_2_.refs_7_.refs_4_.rest_7_, ...), custom_call_target="tpu_custom_call" | custom-call | tf_op jit(solution)/shard_map/pallas_call | solution.py:43
  26.2 0.0 collective-permute-done.11.refs_2_
  26.2 0.3 %shard_map.169 = (f32[960,256]{1,0:T(8,128)S(1)}, f32[80,256]{1,0:T(8,128)S(1)}) custom-call(f32[320,128]{1,0:T(8,128)S(1)} %get-tuple-element.95.wide_ref, f32[88,128]{1,0:T(8,128)S(1)} %collective-permute-done.3.refs_1_.refs_0_.rest_1_, f32[88,128]{1,0:T(8,128)S(1)} %collective-permute-done.5.refs_3_.refs_1_.rest_3_, ...), custom_call_target="tpu_custom_call" | custom-call | tf_op jit(solution)/shard_map/pallas_call | solution.py:43
  26.6 0.6 %collective-permute-done.12.rest_11_ = f32[72,128]{1,0:T(8,128)S(1)} collective-permute-done((f32[72,128]{1,0:T(8,128)S(1)}, f32[72,128]{1,0:T(8,128)S(1)}, u32[]{:S(2)}, u32[]{:S(2)}) %collective-permute-start.12) | collective-permute-done | bytes 36896 | tf_op jit(solution)/shard_map/ppermute | solution.py:734
  27.2 0.0 collective-permute-done.13.rest_12_
  27.2 2.7 %shard_map.170 = (f32[512,128]{1,0:T(8,128)}, f32[64,128]{1,0:T(8,128)}) custom-call(f32[896,256]{1,0:T(8,128)S(1)} %get-tuple-element.94.own_ref, f32[960,256]{1,0:T(8,128)S(1)} %get-tuple-element.96.diag_ref, f32[80,256]{1,0:T(8,128)S(1)} %get-tuple-element.97.mask_ref, f32[64,128]{1,0:T(8,128)S(1)} %get-tuple-element.98.solved_ref, ...), custom_call_target="tpu_custom_call" | custom-call | tf_op jit(solution)/shard_map/pallas_call | solution.py:43
  (4 shorter events, 0.0 us)
Async XLA Ops:
  3.4 4.8 %collective-permute-start.1 = (f32[8,128]{1,0:T(8,128)S(1)}, f32[8,128]{1,0:T(8,128)S(1)}, u32[]{:S(2)}, u32[]{:S(2)}) collective-permute-start(f32[8,128]{1,0:T(8,128)S(1)} %get-tuple-element.64.sums_ref.rest_0_), channel_id=1, source_target_pairs={{0,8},{4,12},{8,0},{12,4},{1,9},{5,13},{9,1},{13,5},{2,10},{6,14},... | collective-permute-start | bytes 12296 | tf_op jit(solution)/shard_map/ppermute | solution.py:734
  6.4 1.8 %collective-permute-start = (f32[24,128]{1,0:T(8,128)S(1)}, f32[24,128]{1,0:T(8,128)S(1)}, u32[]{:S(2)}, u32[]{:S(2)}) collective-permute-start(f32[24,128]{1,0:T(8,128)S(1)} %get-tuple-element.66), channel_id=1, source_target_pairs={{0,4},{4,0},{8,12},{12,8},{1,5},{5,1},{9,13},{13,9},{2,6},{6,2},{1... | collective-permute-start | bytes 36872 | tf_op jit(solution)/shard_map/ppermute | solution.py:734
  6.4 3.2 %collective-permute-start.2 = (f32[24,128]{1,0:T(8,128)S(1)}, f32[24,128]{1,0:T(8,128)S(1)}, u32[]{:S(2)}, u32[]{:S(2)}) collective-permute-start(f32[24,128]{1,0:T(8,128)S(1)} %get-tuple-element.67), channel_id=1, source_target_pairs={{0,12},{4,8},{8,4},{12,0},{1,13},{5,9},{9,5},{13,1},{2,14},{6,10},... | collective-permute-start | bytes 36872 | tf_op jit(solution)/shard_map/ppermute | solution.py:734
  10.4 5.8 %collective-permute-start.6 = (f32[88,128]{1,0:T(8,128)S(1)}, f32[88,128]{1,0:T(8,128)S(1)}, u32[]{:S(2)}, u32[]{:S(2)}) collective-permute-start(f32[88,128]{1,0:T(8,128)S(1)} %get-tuple-element.70.block_ref), channel_id=1, source_target_pairs={{0,16},{16,0},{1,17},{17,1},{2,18},{18,2},{3,19},{19,3},{4,20},{20... | collective-permute-start | bytes 135176 | tf_op jit(solution)/shard_map/ppermute | solution.py:734
  12.0 7.5 %collective-permute-start.4 = (f32[72,128]{1,0:T(8,128)S(1)}, f32[72,128]{1,0:T(8,128)S(1)}, u32[]{:S(2)}, u32[]{:S(2)}) collective-permute-start(f32[72,128]{1,0:T(8,128)S(1)} %get-tuple-element.84.refs_0_.rest_0_), channel_id=1, source_target_pairs={{0,2},{1,3},{2,0},{3,1},{4,6},{5,7},{6,4},{7,5},{8,10},{9,11},{10,... | collective-permute-start | bytes 110600 | tf_op jit(solution)/shard_map/ppermute | solution.py:734
  14.6 6.2 %collective-permute-start.5 = (f32[88,128]{1,0:T(8,128)S(1)}, f32[88,128]{1,0:T(8,128)S(1)}, u32[]{:S(2)}, u32[]{:S(2)}) collective-permute-start(f32[88,128]{1,0:T(8,128)S(1)} %get-tuple-element.70.block_ref), channel_id=1, source_target_pairs={{0,3},{1,2},{2,1},{3,0},{4,7},{5,6},{6,5},{7,4},{8,11},{9,10},{10,... | collective-permute-start | bytes 135176 | tf_op jit(solution)/shard_map/ppermute | solution.py:734
  16.0 4.9 %collective-permute-start.3 = (f32[88,128]{1,0:T(8,128)S(1)}, f32[88,128]{1,0:T(8,128)S(1)}, u32[]{:S(2)}, u32[]{:S(2)}) collective-permute-start(f32[88,128]{1,0:T(8,128)S(1)} %get-tuple-element.70.block_ref), channel_id=1, source_target_pairs={{0,1},{1,0},{2,3},{3,2},{4,5},{5,4},{6,7},{7,6},{8,9},{9,8},{10,11... | collective-permute-start | bytes 135176 | tf_op jit(solution)/shard_map/ppermute | solution.py:734
  16.2 7.3 %collective-permute-start.9 = (f32[88,128]{1,0:T(8,128)S(1)}, f32[88,128]{1,0:T(8,128)S(1)}, u32[]{:S(2)}, u32[]{:S(2)}) collective-permute-start(f32[88,128]{1,0:T(8,128)S(1)} %collective-permute-done.6.refs_4_.rest_4_), channel_id=1, source_target_pairs={{0,3},{1,2},{2,1},{3,0},{4,7},{5,6},{6,5},{7,4},{8,11},{9,10},{10,... | collective-permute-start | bytes 135176 | tf_op jit(solution)/shard_map/ppermute | solution.py:734
  19.1 4.4 %collective-permute-start.7 = (f32[88,128]{1,0:T(8,128)S(1)}, f32[88,128]{1,0:T(8,128)S(1)}, u32[]{:S(2)}, u32[]{:S(2)}) collective-permute-start(f32[88,128]{1,0:T(8,128)S(1)} %collective-permute-done.6.refs_4_.rest_4_), channel_id=1, source_target_pairs={{0,1},{1,0},{2,3},{3,2},{4,5},{5,4},{6,7},{7,6},{8,9},{9,8},{10,11... | collective-permute-start | bytes 135176 | tf_op jit(solution)/shard_map/ppermute | solution.py:734
  19.6 4.0 %collective-permute-start.8 = (f32[72,128]{1,0:T(8,128)S(1)}, f32[72,128]{1,0:T(8,128)S(1)}, u32[]{:S(2)}, u32[]{:S(2)}) collective-permute-start(f32[72,128]{1,0:T(8,128)S(1)} %collective-permute-done.4.refs_2_.rest_2_), channel_id=1, source_target_pairs={{0,16},{16,0},{1,17},{17,1},{2,18},{18,2},{3,19},{19,3},{4,20},{20... | collective-permute-start | bytes 110600 | tf_op jit(solution)/shard_map/ppermute | solution.py:734
  20.8 2.1 %collective-permute-start.10 = (f32[8,128]{1,0:T(8,128)S(1)}, f32[8,128]{1,0:T(8,128)S(1)}, u32[]{:S(2)}, u32[]{:S(2)}) collective-permute-start(f32[8,128]{1,0:T(8,128)S(1)} %get-tuple-element.77.sums_ref), channel_id=1, source_target_pairs={{0,4},{4,0},{8,12},{12,8},{1,5},{5,1},{9,13},{13,9},{2,6},{6,2},{1... | collective-permute-start | bytes 12296 | tf_op jit(solution)/shard_map/ppermute | solution.py:734
  20.8 5.4 %collective-permute-start.11 = (f32[80,128]{1,0:T(8,128)S(1)}, f32[80,128]{1,0:T(8,128)S(1)}, u32[]{:S(2)}, u32[]{:S(2)}) collective-permute-start(f32[80,128]{1,0:T(8,128)S(1)} %shard_map.168), channel_id=1, source_target_pairs={{0,16},{16,0},{1,17},{17,1},{2,18},{18,2},{3,19},{19,3},{4,20},{20... | collective-permute-start | bytes 122888 | tf_op jit(solution)/shard_map/ppermute | solution.py:734
  23.6 3.7 %collective-permute-start.12 = (f32[72,128]{1,0:T(8,128)S(1)}, f32[72,128]{1,0:T(8,128)S(1)}, u32[]{:S(2)}, u32[]{:S(2)}) collective-permute-start(f32[72,128]{1,0:T(8,128)S(1)} %get-tuple-element.101), channel_id=1, source_target_pairs={{0,12},{4,8},{8,4},{12,0},{1,13},{5,9},{9,5},{13,1},{2,14},{6,10},... | collective-permute-start | bytes 110600 | tf_op jit(solution)/shard_map/ppermute | solution.py:734
  23.7 3.6 %collective-permute-start.13 = (f32[72,128]{1,0:T(8,128)S(1)}, f32[72,128]{1,0:T(8,128)S(1)}, u32[]{:S(2)}, u32[]{:S(2)}) collective-permute-start(f32[72,128]{1,0:T(8,128)S(1)} %get-tuple-element.102), channel_id=1, source_target_pairs={{0,4},{4,0},{8,12},{12,8},{1,5},{5,1},{9,13},{13,9},{2,6},{6,2},{1... | collective-permute-start | bytes 110600 | tf_op jit(solution)/shard_map/ppermute | solution.py:734
